TPU v7x, 32 devices: a whole 2x2x4 slice. The times are simulated.
32 devices in a mesh: group: 4 (over z), tile: 8 (over y, x, core).
Axes of the slice: x: 2, y: 2, z: 4, core: 2. Of those that a mesh axis runs over, the one named last changes fastest.
Arguments:
- contrast: bfloat16 [4096, 1024], P('tile', 'group'), may hold values from -6 to 6
- incident: bfloat16 [4, 8, 4096, 1024], P('group', None, 'tile'), may hold values from -2.5 to 2.5
- signs: int32 [4, 8, 8], P('group'), may hold values from -1 to 1, as said below
- adjoint: bfloat16 [4, 8, 4096, 1024], P('group', None, 'tile'), may hold values from -1 to 1
- proj: bfloat16 [1024, 256], replicated, may hold values from -0.1875 to 0.1875
- mats: bfloat16 [6, 256, 256], replicated, may hold values from -0.15625 to 0.15625
- offsets: int32 [6], replicated, may hold values from -3 to 3, as said below
- expand: bfloat16 [256, 1024], replicated, may hold values from -0.375 to 0.375
Outputs:
- scattered: bfloat16 [4, 8, 4096, 1024], P('group', None, 'tile')
- gradient: float32 [4096, 1024], P('tile', 'group')
Inputs may be any that keep to these rules, and one draw needn't show every extreme that they name: `signs`: each entry is -1 or 1. The offsets are distinct; -3 and 3 both occur.
All inputs are finite; a program needn't handle non-finite values.
Results may differ from a plain program's by a relative error of at most 0.015.
Values may be sent and summed in bfloat16 or wider, within the bound.
No kernel may reach another device: no remote copies, remote signals or barrier semaphores. Data moves between devices by JAX's collectives and lax.ppermute only.
A program may use at most 192 MiB of HBM per device.

v0:
```python
import jax
import jax.numpy as jnp
from jax import lax
from jax.sharding import PartitionSpec as P


def with_halo(block, sides, width):
    for axis, dim in sides:
        count = lax.axis_size(axis)
        forward = [(i, i + 1) for i in range(count - 1)]
        backward = [(target, source) for source, target in forward]
        low = lax.ppermute(
            lax.slice_in_dim(block, block.shape[dim] - width, None, axis=dim), axis, forward
        )
        high = lax.ppermute(lax.slice_in_dim(block, 0, width, axis=dim), axis, backward)
        block = jnp.concatenate([low, block, high], axis=dim)
    return block


def translate(padded, mats, offsets):
    count = mats.shape[0]
    rows = padded.shape[0]
    nbox = padded.shape[1] - 6
    width = mats.shape[2]
    moved = [lax.dynamic_slice_in_dim(padded, offsets[t] + 3, nbox, 1) for t in range(count)]
    stacked = jnp.concatenate(moved, axis=2)
    joined = mats.reshape(count * width, width)
    return jnp.dot(
        stacked.reshape(-1, count * width), joined, preferred_element_type=jnp.float32
    ).reshape(rows, nbox, width)


def on_device(contrast, incident, signs, adjoint, proj, mats, offsets, expand):
    full_contrast = lax.all_gather(contrast, "group", axis=1, tiled=True)
    nbox = full_contrast.shape[0]
    points = full_contrast.shape[1]
    width = proj.shape[1]
    encoded = jnp.einsum(
        "es,sbp->ebp",
        signs[0].astype(jnp.bfloat16),
        incident[0],
        preferred_element_type=jnp.float32,
    ).astype(jnp.bfloat16)
    rows = encoded.shape[0]
    adjoint_f = adjoint[0].astype(jnp.float32)
    source = (full_contrast.astype(jnp.float32)[None] * encoded.astype(jnp.float32)).astype(
        jnp.bfloat16
    )
    coeffs = (
        jnp.dot(source.reshape(-1, points), proj, preferred_element_type=jnp.float32)
        .reshape(rows, nbox, width)
        .astype(jnp.bfloat16)
    )
    padded = with_halo(coeffs, (("tile", 1),), 3)
    local = translate(padded, mats, offsets).astype(jnp.bfloat16)
    field = jnp.dot(local.reshape(-1, width), expand, preferred_element_type=jnp.float32).reshape(
        rows, nbox, points
    )
    total = encoded.astype(jnp.float32) + field
    terms = jnp.sum(adjoint_f * total, axis=0)
    gradient = lax.psum_scatter(terms, "group", scatter_dimension=1, tiled=True)
    return (field.astype(jnp.bfloat16)[None], gradient)


def solution(mesh):
    in_specs = (
        P("tile", "group"),
        P("group", None, "tile", None),
        P("group", None, None),
        P("group", None, "tile", None),
        P(),
        P(),
        P(),
        P(),
    )
    out_specs = (P("group", None, "tile", None), P("tile", "group"))
    return jax.shard_map(
        on_device, mesh=mesh, in_specs=in_specs, out_specs=out_specs, check_vma=False
    )
```

profile of v0, /device:TPU:4, one launch (start us, length us, event | category | flops | bytes accessed | tf_op | source)
XLA Modules:
  0.0 186.1 jit_solution(1090497003061735268)
XLA Ops:
  7.2 0.0 copy-start
  7.2 0.0 all-gather.2.cloned.1.call-start
  7.2 0.7 all-gather.2.cloned.1.call-update
  7.9 0.0 reduce-scatter.2.cloned.1.call-start
  8.0 32.0 %all-gather.2.cloned.1.call-done = bf16[512,1024]{1,0:T(8,128)(2,1)} async-done(((bf16[512,256]{1,0:T(8,128)(2,1)}), bf16[512,1024]{1,0:T(8,128)(2,1)}) %all-gather.2.cloned.1.call-update) | async-done | bytes 1048592 | tf_op jit(solution)/shard_map/all_gather | solution.py:34
  40.0 1.5 convert_element_type.34
  41.5 0.0 copy-start.4
  41.5 12.4 %fusion = (bf16[8,512,1024]{2,0,1:T(8,128)(2,1)}, bf16[8,512,1024]{2,0,1:T(8,128)(2,1)}) fusion(f32[512,1024]{1,0:T(8,128)S(1)} %convert_element_type.34, bf16[8,512,1024]{2,1,0:T(8,128)(2,1)} %bitcast.36, s32[1,8,8]{2,1,0:T(8,128)} %param.10), kind=kOutput, calls=%fused_computation.2 | convolution fusion | flops 83886144 | bytes 27263232 | tf_op jit(solution)/shard_map/es,sbp->ebp/dot_general | solution.py:38
  53.9 0.0 copy-done.4
  53.9 0.0 copy-start.3
  53.9 12.9 %fusion.14 = bf16[8,512,256]{2,1,0:T(8,128)(2,1)S(1)} fusion(bf16[8,512,1024]{2,0,1:T(8,128)(2,1)} %get-tuple-element.10, bf16[1024,256]{1,0:T(8,128)(2,1)S(1)} %copy-done.4), kind=kOutput, calls=%fused_computation.21 | convolution fusion | flops 2148532224 | bytes 11010048 | tf_op jit(solution)/shard_map/dot_general | solution.py:50
  66.8 2.0 %collective-permute-start = (bf16[8,3,256]{2,1,0:T(4,128)(2,1)S(1)}, bf16[8,3,256]{2,1,0:T(4,128)(2,1)S(1)}, u32[]{:S(2)}, u32[]{:S(2)}) collective-permute-start(bf16[8,3,256]{2,1,0:T(4,128)(2,1)S(1)} %get-tuple-element.2), channel_id=1, source_target_pairs={{0,1},{1,2},{2,3},{3,4},{4,5},{5,6},{6,7},{8,9},{9,10},{10,11},{11... | collective-permute-start | bytes 36872 | tf_op jit(solution)/shard_map/ppermute | solution.py:12
  68.8 4.7 %collective-permute-start.1 = (bf16[8,3,256]{2,1,0:T(4,128)(2,1)S(1)}, bf16[8,3,256]{2,1,0:T(4,128)(2,1)S(1)}, u32[]{:S(2)}, u32[]{:S(2)}) collective-permute-start(bf16[8,3,256]{2,1,0:T(4,128)(2,1)S(1)} %get-tuple-element.3), channel_id=1, source_target_pairs={{1,0},{2,1},{3,2},{4,3},{5,4},{6,5},{7,6},{9,8},{10,9},{11,10},{12... | collective-permute-start | bytes 36872 | tf_op jit(solution)/shard_map/ppermute | solution.py:15
  73.5 0.0 copy-done.3
  73.5 0.7 fusion.22
  81.6 0.0 collective-permute-done
  81.7 0.0 collective-permute-done.1
  81.7 0.5 pad_maximum_fusion
  82.2 0.5 dynamic-slice_dynamic-update-slice_fusion.5
  82.7 0.5 dynamic-slice_dynamic-update-slice_fusion.4
  83.3 0.0 copy-start.2
  83.3 0.5 dynamic-slice_dynamic-update-slice_fusion.3
  83.8 0.5 dynamic-slice_dynamic-update-slice_fusion.2
  84.4 0.5 dynamic-slice_dynamic-update-slice_fusion.1
  84.9 0.5 dynamic-slice_dynamic-update-slice_fusion
  85.5 0.0 copy-start.1
  85.5 4.5 %copy-done.1 = bf16[8,512,1536]{2,1,0:T(8,128)(2,1)} copy-done((bf16[8,512,1536]{2,1,0:T(8,128)(2,1)}, bf16[8,512,1536]{2,1,0:T(8,128)(2,1)S(1)}, u32[]{:S(2)}) %copy-start.1) | copy-done | bytes 12582936
  90.0 0.0 copy-done
  90.0 0.0 copy-done.2
  90.0 15.3 %fusion.10 = f32[8,512,1024]{2,1,0:T(8,128)} fusion(bf16[8,512,1536]{2,1,0:T(8,128)(2,1)} %copy-done.1, bf16[1536,256,1]{1,0,2:T(8,128)(2,1)S(1)} %bitcast.35, bf16[256,1024]{1,0:T(8,128)(2,1)S(1)} %copy-done.2), kind=kOutput, calls=%fused_computation.12 | convolution fusion | flops 5369757696 | bytes 30670848 | tf_op jit(solution)/shard_map/dot_general | solution.py:56
  105.3 31.9 %fusion.2 = f32[512,1024]{1,0:T(8,128)} fusion(bf16[8,512,1024]{2,0,1:T(8,128)(2,1)} %get-tuple-element.11, f32[8,512,1024]{2,1,0:T(8,128)} %fusion.10, bf16[1,8,512,1024]{3,2,1,0:T(8,128)(2,1)} %param.11), kind=kLoop, calls=%fused_computation.4 | loop fusion | flops 20447232 | bytes 35651584 | tf_op jit(solution)/shard_map/reduce_sum | solution.py:60
  137.2 0.0 reduce-scatter.2.cloned.1.call-update
  137.3 9.2 %convert_bitcast_fusion = bf16[1,8,512,1024]{3,2,1,0:T(8,128)(2,1)} fusion(f32[8,512,1024]{2,1,0:T(8,128)} %fusion.10), kind=kLoop, calls=%fused_computation.9 | loop fusion | flops 4194304 | bytes 25165824 | tf_op jit(solution)/shard_map/broadcast_in_dim | solution.py:62
  146.5 32.8 %reduce-scatter.2.cloned.1.call-done = f32[512,256]{1,0:T(8,128)} async-done(((f32[512,1024]{1,0:T(8,128)}), f32[512,256]{1,0:T(8,128)}) %reduce-scatter.2.cloned.1.call-update) | async-done | bytes 524304 | tf_op jit(solution)/shard_map/reduce_scatter | solution.py:61
  (1 shorter events, 0.0 us)
Async XLA Ops:
  7.2 82.8 %copy-start = (bf16[6,256,256]{2,1,0:T(8,128)(2,1)S(1)}, bf16[6,256,256]{2,1,0:T(8,128)(2,1)}, u32[]{:S(2)}) copy-start(bf16[6,256,256]{2,1,0:T(8,128)(2,1)} %param.13) | copy-start | bytes 2359300
  7.2 32.8 %all-gather.2.cloned.1.call-start = ((), (), s32[]{:S(2)}) async-start(), calls=%async_computation.1 | async-start | bytes 1310720 | tf_op jit(solution)/shard_map/all_gather | solution.py:34
  7.9 171.4 %reduce-scatter.2.cloned.1.call-start = ((), (), s32[]{:S(2)}) async-start(), calls=%async_computation.2 | async-start | bytes 2621440 | tf_op jit(solution)/shard_map/reduce_scatter | solution.py:61
  41.5 12.4 %copy-start.4 = (bf16[1024,256]{1,0:T(8,128)(2,1)S(1)}, bf16[1024,256]{1,0:T(8,128)(2,1)}, u32[]{:S(2)}) copy-start(bf16[1024,256]{1,0:T(8,128)(2,1)} %param.12) | copy-start | bytes 1572868
  53.9 19.6 %copy-start.3 = (s32[6]{0:T(128)S(1)}, s32[6]{0:T(128)}, u32[]{:S(2)}) copy-start(s32[6]{0:T(128)} %param.14) | copy-start | bytes 76
  66.8 14.8 %collective-permute-start = (bf16[8,3,256]{2,1,0:T(4,128)(2,1)S(1)}, bf16[8,3,256]{2,1,0:T(4,128)(2,1)S(1)}, u32[]{:S(2)}, u32[]{:S(2)}) collective-permute-start(bf16[8,3,256]{2,1,0:T(4,128)(2,1)S(1)} %get-tuple-element.2), channel_id=1, source_target_pairs={{0,1},{1,2},{2,3},{3,4},{4,5},{5,6},{6,7},{8,9},{9,10},{10,11},{11... | collective-permute-start | bytes 36872 | tf_op jit(solution)/shard_map/ppermute | solution.py:12
  68.8 12.9 %collective-permute-start.1 = (bf16[8,3,256]{2,1,0:T(4,128)(2,1)S(1)}, bf16[8,3,256]{2,1,0:T(4,128)(2,1)S(1)}, u32[]{:S(2)}, u32[]{:S(2)}) collective-permute-start(bf16[8,3,256]{2,1,0:T(4,128)(2,1)S(1)} %get-tuple-element.3), channel_id=1, source_target_pairs={{1,0},{2,1},{3,2},{4,3},{5,4},{6,5},{7,6},{9,8},{10,9},{11,10},{12... | collective-permute-start | bytes 36872 | tf_op jit(solution)/shard_map/ppermute | solution.py:15
  83.3 6.7 %copy-start.2 = (bf16[256,1024]{1,0:T(8,128)(2,1)S(1)}, bf16[256,1024]{1,0:T(8,128)(2,1)}, u32[]{:S(2)}) copy-start(bf16[256,1024]{1,0:T(8,128)(2,1)} %param.15) | copy-start | bytes 1572868
  85.5 4.5 %copy-start.1 = (bf16[8,512,1536]{2,1,0:T(8,128)(2,1)}, bf16[8,512,1536]{2,1,0:T(8,128)(2,1)S(1)}, u32[]{:S(2)}) copy-start(bf16[8,512,1536]{2,1,0:T(8,128)(2,1)S(1)} %dynamic-slice_dynamic-update-slice_fusion) | copy-start | bytes 37748740
Sparse Core Ops, SparseCore 0:
  9.6 30.3 all-gather.1
  137.4 41.8 reduce-scatter.1
where the time goes:
time: 188 us; the launch traced here: 186 us
  waiting for transfers between devices  65.5 us (35%)
  other arithmetic  43.1 us (23%)
  matrix products  40.6 us (22%)
  between operations  21.6 us (11%)
  local copies, waits for them, and re-layouts  8.48 us (5%)
  starting transfers between devices  6.76 us (4%)
    reduce_scatter x1, waiting for transfers between devices, on_device(): gradient = lax.psum_scatter(terms, 'group', scatter_dimension=1, tiled=True)  32.8 us
    all_gather x1, waiting for transfers between devices, on_device(): full_contrast = lax.all_gather(contrast, 'group', axis=1, tiled=True)  32 us
    reduce_sum x1, other arithmetic, on_device(): terms = jnp.sum(adjoint_f * total, axis=0)  31.9 us
    dot_general x1, matrix products, on_device(): jnp.dot(local.reshape(-1, width), expand, preferred_element_type=jnp.floa...  15.3 us
    dot_general x1, matrix products, on_device(): jnp.dot(source.reshape(-1, points), proj, preferred_element_type=jnp.floa...  12.9 us
    dot_general x1, matrix products, on_device(): jnp.einsum('es,sbp->ebp', signs[0].astype(jnp.bfloat16), incident[0], pre...  12.4 us
    broadcast_in_dim x1, other arithmetic, on_device(): return (field.astype(jnp.bfloat16)[None], gradient)  9.21 us
    unnamed x15, local copies, waits for them, and re-layouts  7.25 us
  transfers between devices with their start and end apart: 4, of which 2 were waited for; matrix products, arithmetic and copies ran while one was open for 5% of the time, Pallas kernels for 0%

commit v1 on v0

v1 whole, which is shorter than its diff:
```python
import functools

import jax
import jax.numpy as jnp
from jax import lax
from jax.experimental import pallas as pl
from jax.experimental.pallas import tpu as pltpu
from jax.sharding import PartitionSpec as P

F32 = jnp.float32
BF16 = jnp.bfloat16
HALO = 3


def low_bit(m):
    return m & -m


def exchange(x, axis, m, count):
    return lax.ppermute(x, axis, [(i, i ^ m) for i in range(count)])


def gather_pieces(x, axis, count):
    pieces = {0: x}
    for m in sorted(range(1, count), key=lambda m: (bin(m).count("1"), -m)):
        b = low_bit(m)
        pieces[m] = exchange(pieces[m ^ b], axis, b, count)
    return [pieces[m] for m in range(count)]


def scatter_pieces(own, parts, axis, count):
    parts = dict(enumerate(parts, start=1))
    received = []
    for m in sorted(range(1, count), key=lambda m: (-bin(m).count("1"), m)):
        b = low_bit(m)
        got = exchange(parts[m], axis, b, count)
        if m == b:
            received.append(got)
        else:
            parts[m ^ b] = (parts[m ^ b].astype(F32) + got.astype(F32)).astype(BF16)
    for got in received:
        own = own + got.astype(F32)
    return own


def same_box(rows, columns, rows_of, columns_of):
    r = lax.broadcasted_iota(jnp.int32, (rows, columns), 0)
    c = lax.broadcasted_iota(jnp.int32, (rows, columns), 1)
    return rows_of(r) == columns_of(c)


def encode_kernel(signs, inc, adj, enc, part, mix):
    count, block, points = inc.shape[1:]
    outs = adj.shape[1]

    @pl.when(pl.program_id(0) == 0)
    def _():
        size = count * block
        r = lax.broadcasted_iota(jnp.int32, (block, size), 0)
        c = lax.broadcasted_iota(jnp.int32, (block, size), 1)
        diagonal = (c % block) == r
        for e in range(outs):
            value = jnp.zeros((block, size), F32)
            for s in range(count):
                value = jnp.where(c // block == s, signs[0, e, s].astype(F32), value)
            mix[e * block:(e + 1) * block, :] = jnp.where(diagonal, value, 0.0).astype(BF16)

    x = inc[0].reshape(count * block, points)
    encoded = jnp.dot(mix[...], x, preferred_element_type=F32).astype(BF16)
    encoded = encoded.reshape(outs, block, points)
    enc[...] = encoded
    part[...] = jnp.sum(adj[0].astype(F32) * encoded.astype(F32), axis=0)


def encode(signs, incident, adjoint, block):
    _, count, nbox, points = incident.shape
    outs = adjoint.shape[1]
    return pl.pallas_call(
        encode_kernel,
        grid=(nbox // block,),
        in_specs=[
            pl.BlockSpec(memory_space=pltpu.SMEM),
            pl.BlockSpec((1, count, block, points), lambda i: (0, 0, i, 0)),
            pl.BlockSpec((1, outs, block, points), lambda i: (0, 0, i, 0)),
        ],
        out_specs=[
            pl.BlockSpec((outs, block, points), lambda i: (0, i, 0)),
            pl.BlockSpec((block, points), lambda i: (i, 0)),
        ],
        out_shape=[
            jax.ShapeDtypeStruct((outs, nbox, points), BF16),
            jax.ShapeDtypeStruct((nbox, points), F32),
        ],
        scratch_shapes=[pltpu.VMEM((outs * block, count * block), BF16)],
        compiler_params=pltpu.CompilerParams(vmem_limit_bytes=32 * 2**20),
        cost_estimate=pl.CostEstimate(
            flops=2 * outs * count * block * nbox * points,
            bytes_accessed=nbox * points * (2 * (2 * outs + count) + 4),
            transcendentals=0,
        ),
        name="encode",
    )(signs, incident, adjoint)


def project_kernel(axis, count, enc, *refs):
    contrasts, (proj, out, order) = refs[:count], refs[count:]
    outs, block, points = enc.shape
    size = outs * block
    share = points // count
    me = lax.axis_index(axis)

    @pl.when(pl.program_id(0) == 0)
    def _():
        r = lax.broadcasted_iota(jnp.int32, (size, size), 0)
        c = lax.broadcasted_iota(jnp.int32, (size, size), 1)
        hit = (r % outs) * block + r // outs == c
        order[...] = jnp.where(hit, 1.0, 0.0).astype(BF16)

    total = None
    for m in range(count):
        start = pl.multiple_of((me ^ m) * share, share)
        source = contrasts[m][...][None] * enc[:, :, pl.ds(start, share)]
        term = jnp.dot(
            source.reshape(size, share), proj[pl.ds(start, share), :], preferred_element_type=F32
        )
        total = term if total is None else total + term
    coeffs = total.astype(BF16)
    out[...] = jnp.dot(order[...], coeffs, preferred_element_type=F32).astype(BF16)


def project(axis, count, enc, pieces, proj, block):
    outs, nbox, points = enc.shape
    width = proj.shape[1]
    share = points // count
    size = outs * block
    return pl.pallas_call(
        functools.partial(project_kernel, axis, count),
        grid=(nbox // block,),
        in_specs=[pl.BlockSpec((outs, block, points), lambda i: (0, i, 0))]
        + [pl.BlockSpec((block, share), lambda i: (i, 0))] * count
        + [pl.BlockSpec((points, width), lambda i: (0, 0))],
        out_specs=pl.BlockSpec((size, width), lambda i: (i, 0)),
        out_shape=jax.ShapeDtypeStruct((outs * nbox, width), BF16),
        scratch_shapes=[pltpu.VMEM((size, size), BF16)],
        compiler_params=pltpu.CompilerParams(vmem_limit_bytes=32 * 2**20),
        cost_estimate=pl.CostEstimate(
            flops=2 * outs * nbox * width * (points + size),
            bytes_accessed=2 * outs * nbox * (points + width),
            transcendentals=0,
        ),
        name="project",
    )(enc, *pieces, proj)


def expand_kernel(axis, count, edge, offsets, coeffs, low, high, mats, expand, adj, part, *refs):
    scattered, own, others = refs[0], refs[1], refs[2:1 + count]
    order, padded, terms = refs[1 + count:]
    _, outs, block, points = adj.shape
    size = outs * block
    share = points // count
    me = lax.axis_index(axis)
    step = pl.program_id(0)
    rows = coeffs.shape[0]

    @pl.when(step == 0)
    def _():
        r = lax.broadcasted_iota(jnp.int32, (size, size), 0)
        c = lax.broadcasted_iota(jnp.int32, (size, size), 1)
        hit = (r % block) * outs + r // block == c
        order[...] = jnp.where(hit, 1.0, 0.0).astype(BF16)
        padded[0:edge, :] = low[...].astype(F32)
        padded[edge:edge + rows, :] = coeffs[...].astype(F32)
        padded[edge + rows:edge + rows + edge, :] = high[...].astype(F32)

    local = None
    for t in range(mats.shape[0]):
        start = pl.multiple_of(step * size + edge + offsets[t] * outs, outs)
        moved = padded[pl.ds(start, size), :].astype(BF16)
        term = jnp.dot(moved, mats[t], preferred_element_type=F32)
        local = term if local is None else local + term
    local = jnp.dot(order[...], local.astype(BF16), preferred_element_type=F32).astype(BF16)
    field = jnp.dot(local, expand[...], preferred_element_type=F32).reshape(outs, block, points)
    scattered[0] = field.astype(BF16)
    terms[...] = part[...] + jnp.sum(adj[0].astype(F32) * field, axis=0)
    for m in range(count):
        start = pl.multiple_of((me ^ m) * share, share)
        piece = terms[:, pl.ds(start, share)]
        if m == 0:
            own[...] = piece
        else:
            others[m - 1][...] = piece.astype(BF16)


def expanded(axis, count, offsets, coeffs, low, high, mats, expand, adjoint, part, block):
    _, outs, nbox, points = adjoint.shape
    width = expand.shape[0]
    share = points // count
    size = outs * block
    edge = low.shape[0]
    return pl.pallas_call(
        functools.partial(expand_kernel, axis, count, edge),
        grid=(nbox // block,),
        in_specs=[
            pl.BlockSpec(memory_space=pltpu.SMEM),
            pl.BlockSpec(coeffs.shape, lambda i: (0, 0)),
            pl.BlockSpec(low.shape, lambda i: (0, 0)),
            pl.BlockSpec(high.shape, lambda i: (0, 0)),
            pl.BlockSpec(mats.shape, lambda i: (0, 0, 0)),
            pl.BlockSpec(expand.shape, lambda i: (0, 0)),
            pl.BlockSpec((1, outs, block, points), lambda i: (0, 0, i, 0)),
            pl.BlockSpec((block, points), lambda i: (i, 0)),
        ],
        out_specs=[
            pl.BlockSpec((1, outs, block, points), lambda i: (0, 0, i, 0)),
        ]
        + [pl.BlockSpec((block, share), lambda i: (i, 0))] * count,
        out_shape=[
            jax.ShapeDtypeStruct((1, outs, nbox, points), BF16),
            jax.ShapeDtypeStruct((nbox, share), F32),
        ]
        + [jax.ShapeDtypeStruct((nbox, share), BF16)] * (count - 1),
        scratch_shapes=[
            pltpu.VMEM((size, size), BF16),
            pltpu.VMEM((coeffs.shape[0] + 2 * edge, width), F32),
            pltpu.VMEM((block, points), F32),
        ],
        compiler_params=pltpu.CompilerParams(vmem_limit_bytes=40 * 2**20),
        cost_estimate=pl.CostEstimate(
            flops=2 * outs * nbox * width * (mats.shape[0] * width + size + points),
            bytes_accessed=nbox * points * (4 * outs + 8),
            transcendentals=0,
        ),
        name="expand",
    )(offsets, coeffs, low, high, mats, expand, adjoint, part)


def on_device(groups, tiles, contrast, incident, signs, adjoint, proj, mats, offsets, expand):
    outs = adjoint.shape[1]
    nbox = contrast.shape[0]
    block = min(256 // outs, nbox)
    edge = 4 * outs
    pieces = gather_pieces(contrast, "group", groups)
    enc, part = encode(signs, incident, adjoint, block)
    coeffs = project("group", groups, enc, pieces, proj, block)
    upward = [(i, i + 1) for i in range(tiles - 1)]
    downward = [(i + 1, i) for i in range(tiles - 1)]
    low = lax.ppermute(coeffs[nbox * outs - edge:], "tile", upward)
    high = lax.ppermute(coeffs[:edge], "tile", downward)
    scattered, own, *parts = expanded(
        "group", groups, offsets, coeffs, low, high, mats, expand, adjoint, part, block
    )
    gradient = scatter_pieces(own, parts, "group", groups)
    return scattered, gradient


def solution(mesh):
    in_specs = (
        P("tile", "group"),
        P("group", None, "tile", None),
        P("group", None, None),
        P("group", None, "tile", None),
        P(),
        P(),
        P(),
        P(),
    )
    out_specs = (P("group", None, "tile", None), P("tile", "group"))
    return jax.shard_map(
        functools.partial(on_device, mesh.shape["group"], mesh.shape["tile"]),
        mesh=mesh,
        in_specs=in_specs,
        out_specs=out_specs,
        check_vma=False,
    )
```

time: 188 us -> 96.6 us (0.51)
  the two profiles are of different devices: /device:TPU:4 before, /device:TPU:0 now
where the time goes in v1:
time: 96.6 us; the launch traced here: 95.7 us
  Pallas kernels  42.9 us (44%)
  waiting for transfers between devices  31.1 us (32%)
  starting transfers between devices  16 us (17%)
  local copies, waits for them, and re-layouts  4.1 us (4%)
    ppermute x6, waiting for transfers between devices, exchange(): return lax.ppermute(x, axis, [(i, i ^ m) for i in range(count)])  30.2 us
    pallas_call x1, Pallas kernels, expanded(): pl.pallas_call(functools.partial(expand_kernel, axis, count, edge), grid=...  20.7 us
    pallas_call x1, Pallas kernels, encode(): pl.pallas_call(encode_kernel, grid=(nbox // block,), in_specs=[pl.BlockSp...  12.7 us
    ppermute x6, starting transfers between devices, exchange(): return lax.ppermute(x, axis, [(i, i ^ m) for i in range(count)])  11.7 us
    pallas_call x1, Pallas kernels, project(): pl.pallas_call(functools.partial(project_kernel, axis, count), grid=(nbox...  9.46 us
    unnamed x14, local copies, waits for them, and re-layouts  4.09 us
    ppermute x1, starting transfers between devices, on_device(): low = lax.ppermute(coeffs[nbox * outs - edge:], 'tile', upward)  3.03 us
  transfers between devices with their start and end apart: 8, of which 5 were waited for; matrix products, arithmetic and copies ran while one was open for 0% of the time, Pallas kernels for 13%

profile of v1, /device:TPU:0, one launch (start us, length us, event | category | flops | bytes accessed | tf_op | source)
XLA Modules:
  0.0 95.7 jit_solution(356709805512285165)
XLA Ops:
  0.6 4.1 %collective-permute-start.1 = (bf16[512,256]{1,0:T(8,128)(2,1)}, bf16[512,256]{1,0:T(8,128)(2,1)S(1)}, u32[]{:S(2)}, u32[]{:S(2)}) collective-permute-start(bf16[512,256]{1,0:T(8,128)(2,1)} %refs_0_.1), channel_id=1, source_target_pairs={{0,16},{8,24},{16,0},{24,8},{1,17},{9,25},{17,1},{25,9},{2,18},{10... | collective-permute-start | bytes 786440 | tf_op jit(solution)/shard_map/ppermute | solution.py:20
  4.7 1.6 %collective-permute-start = (bf16[512,256]{1,0:T(8,128)(2,1)}, bf16[512,256]{1,0:T(8,128)(2,1)S(1)}, u32[]{:S(2)}, u32[]{:S(2)}) collective-permute-start(bf16[512,256]{1,0:T(8,128)(2,1)} %refs_0_.1), channel_id=1, source_target_pairs={{0,8},{8,0},{16,24},{24,16},{1,9},{9,1},{17,25},{25,17},{2,10},{10... | collective-permute-start | bytes 786440 | tf_op jit(solution)/shard_map/ppermute | solution.py:20
  6.3 10.7 %collective-permute-done.1.refs_2_ = bf16[512,256]{1,0:T(8,128)(2,1)S(1)} collective-permute-done((bf16[512,256]{1,0:T(8,128)(2,1)}, bf16[512,256]{1,0:T(8,128)(2,1)S(1)}, u32[]{:S(2)}, u32[]{:S(2)}) %collective-permute-start.1) | collective-permute-done | bytes 262176 | tf_op jit(solution)/shard_map/ppermute | solution.py:20
  17.0 0.7 collective-permute-start.2
  17.7 0.0 copy-start
  17.7 3.4 %copy-done = bf16[1,8,512,1024]{3,2,1,0:T(8,128)(2,1)S(1)} copy-done((bf16[1,8,512,1024]{3,2,1,0:T(8,128)(2,1)S(1)}, bf16[1,8,512,1024]{3,2,1,0:T(8,128)(2,1)}, u32[]{:S(2)}) %copy-start) | copy-done | bytes 8388632
  21.1 0.0 copy-start.3
  21.1 0.7 copy-done.3
  21.8 0.0 copy-start.1
  21.8 0.0 copy-start.2
  21.8 12.7 %encode.1 = (bf16[8,512,1024]{2,1,0:T(8,128)(2,1)S(1)}, f32[512,1024]{1,0:T(8,128)S(1)}) custom-call(s32[1,8,8]{2,1,0:T(8,128)S(1)} %copy-done.3, bf16[1,8,512,1024]{3,2,1,0:T(8,128)(2,1)S(1)} %copy-done, bf16[1,8,512,1024]{3,2,1,0:T(8,128)(2,1)} %adj.3), custom_call_target="tpu_custom_call" | custom-call | flops 2147483648 | bytes 27262976 | tf_op jit(solution)/shard_map/encode/pallas_call | solution.py:78
  34.5 0.0 copy-start.4
  34.5 0.0 copy-start.5
  34.5 0.0 copy-start.6
  34.5 0.0 collective-permute-done.refs_1_
  34.5 0.0 collective-permute-done.2.refs_3_
  34.5 0.0 copy-done.1
  34.5 0.0 copy-done.2
  34.5 9.5 %project.1.coeffs = bf16[4096,256]{1,0:T(8,128)(2,1)S(1)} custom-call(bf16[8,512,1024]{2,1,0:T(8,128)(2,1)S(1)} %get-tuple-element.9.enc, bf16[512,256]{1,0:T(8,128)(2,1)S(1)} %copy-done.2, bf16[512,256]{1,0:T(8,128)(2,1)S(1)} %collective-permute-done.refs_1_, bf16[512,256]{1,0:T(8,128)(2,1)S(1)} %collective-permute-done.1.refs_2_, ...), custom_call_target="tpu_custom_call" | custom-call | flops 2684354560 | bytes 10485760 | tf_op jit(solution)/shard_map/project/pallas_call | solution.py:136
  44.0 1.3 %collective-permute-start.4 = (bf16[32,256]{1,0:T(8,128)(2,1)S(1)}, bf16[32,256]{1,0:T(8,128)(2,1)S(1)}, u32[]{:S(2)}, u32[]{:S(2)}) collective-permute-start(bf16[32,256]{1,0:T(8,128)(2,1)S(1)} %get-tuple-element.16), channel_id=1, source_target_pairs={{1,0},{2,1},{3,2},{4,3},{5,4},{6,5},{7,6},{9,8},{10,9},{11,10},{12... | collective-permute-start | bytes 49160 | tf_op jit(solution)/shard_map/ppermute | solution.py:248
  45.3 3.0 %collective-permute-start.3 = (bf16[32,256]{1,0:T(8,128)(2,1)S(1)}, bf16[32,256]{1,0:T(8,128)(2,1)S(1)}, u32[]{:S(2)}, u32[]{:S(2)}) collective-permute-start(bf16[32,256]{1,0:T(8,128)(2,1)S(1)} %get-tuple-element.17), channel_id=1, source_target_pairs={{0,1},{1,2},{2,3},{3,4},{4,5},{5,6},{6,7},{8,9},{9,10},{10,11},{11... | collective-permute-start | bytes 49160 | tf_op jit(solution)/shard_map/ppermute | solution.py:247
  48.4 0.0 collective-permute-done.4.high
  48.4 0.8 collective-permute-done.3.low
  49.2 0.0 copy-done.4
  49.2 0.0 copy-done.5
  49.2 0.0 copy-done.6
  49.2 20.7 %expand.2 = (bf16[1,8,512,1024]{3,2,1,0:T(8,128)(2,1)}, f32[512,256]{1,0:T(8,128)S(1)}, bf16[512,256]{1,0:T(8,128)(2,1)S(1)}, bf16[512,256]{1,0:T(8,128)(2,1)S(1)}, bf16[512,256]{1,0:T(8,128)(2,1)S(1)}) custom-call(s32[6]{0:T(128)S(1)} %copy-done.6, bf16[4096,256]{1,0:T(8,128)(2,1)S(1)} %project.1.coeffs, bf16[32,256]{1,0:T(8,128)(2,1)S(1)} %collective-permute-done.3.low, ...), custom_call_target="tpu_custom_call" | custom-call | flops 5905580032 | bytes 20971520 | tf_op jit(solution)/shard_map/expand/pallas_call | solution.py:200
  69.9 1.4 %collective-permute-start.6 = (bf16[512,256]{1,0:T(8,128)(2,1)S(1)}, bf16[512,256]{1,0:T(8,128)(2,1)S(1)}, u32[]{:S(2)}, u32[]{:S(2)}) collective-permute-start(bf16[512,256]{1,0:T(8,128)(2,1)S(1)} %get-tuple-element.15), channel_id=1, source_target_pairs={{0,8},{8,0},{16,24},{24,16},{1,9},{9,1},{17,25},{25,17},{2,10},{10... | collective-permute-start | bytes 786440 | tf_op jit(solution)/shard_map/ppermute | solution.py:20
  71.4 0.6 collective-permute-start.5
  72.0 7.0 %collective-permute-done.6 = bf16[512,256]{1,0:T(8,128)(2,1)S(1)} collective-permute-done((bf16[512,256]{1,0:T(8,128)(2,1)S(1)}, bf16[512,256]{1,0:T(8,128)(2,1)S(1)}, u32[]{:S(2)}, u32[]{:S(2)}) %collective-permute-start.6) | collective-permute-done | bytes 262176 | tf_op jit(solution)/shard_map/ppermute | solution.py:20
  78.9 0.1 add_convert_fusion
  79.0 3.3 %collective-permute-start.7 = (bf16[512,256]{1,0:T(8,128)(2,1)S(1)}, bf16[512,256]{1,0:T(8,128)(2,1)S(1)}, u32[]{:S(2)}, u32[]{:S(2)}) collective-permute-start(bf16[512,256]{1,0:T(8,128)(2,1)S(1)} %add_convert_fusion), channel_id=1, source_target_pairs={{0,16},{8,24},{16,0},{24,8},{1,17},{9,25},{17,1},{25,9},{2,18},{10... | collective-permute-start | bytes 786440 | tf_op jit(solution)/shard_map/ppermute | solution.py:20
  82.3 6.1 %collective-permute-done.5 = bf16[512,256]{1,0:T(8,128)(2,1)S(1)} collective-permute-done((bf16[512,256]{1,0:T(8,128)(2,1)S(1)}, bf16[512,256]{1,0:T(8,128)(2,1)S(1)}, u32[]{:S(2)}, u32[]{:S(2)}) %collective-permute-start.5) | collective-permute-done | bytes 262176 | tf_op jit(solution)/shard_map/ppermute | solution.py:20
  88.4 6.5 %collective-permute-done.7 = bf16[512,256]{1,0:T(8,128)(2,1)S(1)} collective-permute-done((bf16[512,256]{1,0:T(8,128)(2,1)S(1)}, bf16[512,256]{1,0:T(8,128)(2,1)S(1)}, u32[]{:S(2)}, u32[]{:S(2)}) %collective-permute-start.7) | collective-permute-done | bytes 262176 | tf_op jit(solution)/shard_map/ppermute | solution.py:20
  94.9 0.9 convert_add_fusion
  (1 shorter events, 0.0 us)
Async XLA Ops:
  0.6 16.3 %collective-permute-start.1 = (bf16[512,256]{1,0:T(8,128)(2,1)}, bf16[512,256]{1,0:T(8,128)(2,1)S(1)}, u32[]{:S(2)}, u32[]{:S(2)}) collective-permute-start(bf16[512,256]{1,0:T(8,128)(2,1)} %refs_0_.1), channel_id=1, source_target_pairs={{0,16},{8,24},{16,0},{24,8},{1,17},{9,25},{17,1},{25,9},{2,18},{10... | collective-permute-start | bytes 786440 | tf_op jit(solution)/shard_map/ppermute | solution.py:20
  4.7 29.8 %collective-permute-start = (bf16[512,256]{1,0:T(8,128)(2,1)}, bf16[512,256]{1,0:T(8,128)(2,1)S(1)}, u32[]{:S(2)}, u32[]{:S(2)}) collective-permute-start(bf16[512,256]{1,0:T(8,128)(2,1)} %refs_0_.1), channel_id=1, source_target_pairs={{0,8},{8,0},{16,24},{24,16},{1,9},{9,1},{17,25},{25,17},{2,10},{10... | collective-permute-start | bytes 786440 | tf_op jit(solution)/shard_map/ppermute | solution.py:20
  17.0 17.5 %collective-permute-start.2 = (bf16[512,256]{1,0:T(8,128)(2,1)S(1)}, bf16[512,256]{1,0:T(8,128)(2,1)S(1)}, u32[]{:S(2)}, u32[]{:S(2)}) collective-permute-start(bf16[512,256]{1,0:T(8,128)(2,1)S(1)} %collective-permute-done.1.refs_2_), channel_id=1, source_target_pairs={{0,8},{8,0},{16,24},{24,16},{1,9},{9,1},{17,25},{25,17},{2,10},{10... | collective-permute-start | bytes 786440 | tf_op jit(solution)/shard_map/ppermute | solution.py:20
  17.7 3.4 %copy-start = (bf16[1,8,512,1024]{3,2,1,0:T(8,128)(2,1)S(1)}, bf16[1,8,512,1024]{3,2,1,0:T(8,128)(2,1)}, u32[]{:S(2)}) copy-start(bf16[1,8,512,1024]{3,2,1,0:T(8,128)(2,1)} %inc.1) | copy-start | bytes 25165828
  21.1 0.7 copy-start.3
  21.8 12.8 %copy-start.1 = (bf16[1024,256]{1,0:T(8,128)(2,1)S(1)}, bf16[1024,256]{1,0:T(8,128)(2,1)}, u32[]{:S(2)}) copy-start(bf16[1024,256]{1,0:T(8,128)(2,1)} %refs_4_.1) | copy-start | bytes 1572868
  21.8 12.8 %copy-start.2 = (bf16[512,256]{1,0:T(8,128)(2,1)S(1)}, bf16[512,256]{1,0:T(8,128)(2,1)}, u32[]{:S(2)}) copy-start(bf16[512,256]{1,0:T(8,128)(2,1)} %refs_0_.1) | copy-start | bytes 786436
  34.5 14.7 %copy-start.4 = (bf16[6,256,256]{2,1,0:T(8,128)(2,1)S(1)}, bf16[6,256,256]{2,1,0:T(8,128)(2,1)}, u32[]{:S(2)}) copy-start(bf16[6,256,256]{2,1,0:T(8,128)(2,1)} %mats.1) | copy-start | bytes 2359300
  34.5 14.7 %copy-start.5 = (bf16[256,1024]{1,0:T(8,128)(2,1)S(1)}, bf16[256,1024]{1,0:T(8,128)(2,1)}, u32[]{:S(2)}) copy-start(bf16[256,1024]{1,0:T(8,128)(2,1)} %expand.3) | copy-start | bytes 1572868
  34.5 14.7 %copy-start.6 = (s32[6]{0:T(128)S(1)}, s32[6]{0:T(128)}, u32[]{:S(2)}) copy-start(s32[6]{0:T(128)} %offsets.1) | copy-start | bytes 76
  44.0 4.3 %collective-permute-start.4 = (bf16[32,256]{1,0:T(8,128)(2,1)S(1)}, bf16[32,256]{1,0:T(8,128)(2,1)S(1)}, u32[]{:S(2)}, u32[]{:S(2)}) collective-permute-start(bf16[32,256]{1,0:T(8,128)(2,1)S(1)} %get-tuple-element.16), channel_id=1, source_target_pairs={{1,0},{2,1},{3,2},{4,3},{5,4},{6,5},{7,6},{9,8},{10,9},{11,10},{12... | collective-permute-start | bytes 49160 | tf_op jit(solution)/shard_map/ppermute | solution.py:248
  45.3 3.9 %collective-permute-start.3 = (bf16[32,256]{1,0:T(8,128)(2,1)S(1)}, bf16[32,256]{1,0:T(8,128)(2,1)S(1)}, u32[]{:S(2)}, u32[]{:S(2)}) collective-permute-start(bf16[32,256]{1,0:T(8,128)(2,1)S(1)} %get-tuple-element.17), channel_id=1, source_target_pairs={{0,1},{1,2},{2,3},{3,4},{4,5},{5,6},{6,7},{8,9},{9,10},{10,11},{11... | collective-permute-start | bytes 49160 | tf_op jit(solution)/shard_map/ppermute | solution.py:247
  69.9 9.0 %collective-permute-start.6 = (bf16[512,256]{1,0:T(8,128)(2,1)S(1)}, bf16[512,256]{1,0:T(8,128)(2,1)S(1)}, u32[]{:S(2)}, u32[]{:S(2)}) collective-permute-start(bf16[512,256]{1,0:T(8,128)(2,1)S(1)} %get-tuple-element.15), channel_id=1, source_target_pairs={{0,8},{8,0},{16,24},{24,16},{1,9},{9,1},{17,25},{25,17},{2,10},{10... | collective-permute-start | bytes 786440 | tf_op jit(solution)/shard_map/ppermute | solution.py:20
  71.4 17.0 %collective-permute-start.5 = (bf16[512,256]{1,0:T(8,128)(2,1)S(1)}, bf16[512,256]{1,0:T(8,128)(2,1)S(1)}, u32[]{:S(2)}, u32[]{:S(2)}) collective-permute-start(bf16[512,256]{1,0:T(8,128)(2,1)S(1)} %get-tuple-element.13), channel_id=1, source_target_pairs={{0,8},{8,0},{16,24},{24,16},{1,9},{9,1},{17,25},{25,17},{2,10},{10... | collective-permute-start | bytes 786440 | tf_op jit(solution)/shard_map/ppermute | solution.py:20
  79.0 15.9 %collective-permute-start.7 = (bf16[512,256]{1,0:T(8,128)(2,1)S(1)}, bf16[512,256]{1,0:T(8,128)(2,1)S(1)}, u32[]{:S(2)}, u32[]{:S(2)}) collective-permute-start(bf16[512,256]{1,0:T(8,128)(2,1)S(1)} %add_convert_fusion), channel_id=1, source_target_pairs={{0,16},{8,24},{16,0},{24,8},{1,17},{9,25},{17,1},{25,9},{2,18},{10... | collective-permute-start | bytes 786440 | tf_op jit(solution)/shard_map/ppermute | solution.py:20

commit v2 on v0

v2 whole, which is shorter than its diff:
```python
import functools

import jax
import jax.numpy as jnp
from jax import lax
from jax.experimental import pallas as pl
from jax.experimental.pallas import tpu as pltpu
from jax.sharding import PartitionSpec as P

F32 = jnp.float32
BF16 = jnp.bfloat16
ROWS = 16
VMEM = pl.BlockSpec(memory_space=pltpu.VMEM)
SMEM = pl.BlockSpec(memory_space=pltpu.SMEM)
ANY = pl.BlockSpec(memory_space=pl.ANY)


def near(x):
    return pltpu.with_memory_space_constraint(x, pltpu.VMEM)


def in_blocks(segments, size, body):
    done = 0
    for first, extent in segments:
        whole = extent // size
        if whole == 1:
            body(first, done, size)
        elif whole > 1:
            def step(i, carry, first=first, done=done):
                body(
                    pl.multiple_of(first + i * size, ROWS),
                    pl.multiple_of(done + i * size, ROWS),
                    size,
                )
                return carry

            lax.fori_loop(0, whole, step, 0)
        if extent % size:
            body(first + whole * size, done + whole * size, extent % size)
        done += extent


def encode_kernel(block, group, signs, inc, adj, enc, adjv, part, incv, mix, sems):
    count, nbox, points = incv.shape
    outs = enc.shape[0]
    size = count * group
    steps = nbox // block

    def copies(i):
        rows = pl.ds(i * block, block)
        return (
            pltpu.make_async_copy(inc.at[0, :, rows, :], incv.at[:, rows, :], sems.at[0, i]),
            pltpu.make_async_copy(adj.at[0, :, rows, :], adjv.at[:, rows, :], sems.at[1, i]),
        )

    for i in range(steps):
        for copy in copies(i):
            copy.start()

    r = lax.broadcasted_iota(jnp.int32, (group, size), 0)
    c = lax.broadcasted_iota(jnp.int32, (group, size), 1)
    diagonal = (c % group) == r
    for e in range(outs):
        value = jnp.zeros((group, size), F32)
        for s in range(count):
            value = jnp.where(c // group == s, signs[0, e, s].astype(F32), value)
        mix[e * group:(e + 1) * group, :] = jnp.where(diagonal, value, 0.0).astype(BF16)

    def step(i, carry):
        for copy in copies(i):
            copy.wait()
        for j in range(block // group):
            rows = pl.ds(pl.multiple_of(i * block + j * group, ROWS), group)
            x = incv[:, rows, :].reshape(size, points)
            encoded = jnp.dot(mix[...], x, preferred_element_type=F32).astype(BF16)
            encoded = encoded.reshape(outs, group, points)
            enc[:, rows, :] = encoded
            part[rows, :] = jnp.sum(adjv[:, rows, :].astype(F32) * encoded.astype(F32), axis=0)
        return carry

    lax.fori_loop(0, steps, step, 0)


def encode(signs, incident, adjoint, block=64):
    _, count, nbox, points = incident.shape
    outs = adjoint.shape[1]
    group = 256 // count
    return pl.pallas_call(
        functools.partial(encode_kernel, block, group),
        in_specs=[SMEM, ANY, ANY],
        out_specs=[VMEM] * 3,
        out_shape=[
            pltpu.VMEM((outs, nbox, points), BF16),
            pltpu.VMEM((outs, nbox, points), BF16),
            pltpu.VMEM((nbox, points), F32),
        ],
        scratch_shapes=[
            pltpu.VMEM((count, nbox, points), BF16),
            pltpu.VMEM((outs * group, count * group), BF16),
            pltpu.SemaphoreType.DMA((2, nbox // block)),
        ],
        compiler_params=pltpu.CompilerParams(vmem_limit_bytes=32 * 2**20),
        cost_estimate=pl.CostEstimate(
            flops=2 * outs * count * group * nbox * points,
            bytes_accessed=nbox * points * (2 * (2 * outs + count) + 4),
            transcendentals=0,
        ),
        name="encode",
    )(signs, incident, adjoint)


def project_kernel(axis, count, segments, block, enc, *refs):
    contrasts, (proj, out) = refs[:count], refs[count:]
    outs, _, points = enc.shape
    width = proj.shape[1]
    share = points // count
    me = lax.axis_index(axis)
    starts = [pl.multiple_of((me ^ m) * share, share) for m in range(count)]

    def body(first, row, size):
        rows = pl.ds(row, size)
        source = jnp.concatenate(
            [
                contrasts[m][rows, :][None] * enc[:, pl.ds(first, size), pl.ds(starts[m], share)]
                for m in range(count)
            ],
            axis=2,
        ).reshape(outs * size, points)
        weights = jnp.concatenate([proj[pl.ds(starts[m], share), :] for m in range(count)], axis=0)
        coeffs = jnp.dot(source, weights, preferred_element_type=F32)
        out[:, rows, :] = coeffs.astype(BF16).reshape(outs, size, width)

    in_blocks(segments, block, body)


def project(axis, count, segments, enc, pieces, proj, block=128):
    outs, _, points = enc.shape
    width = proj.shape[1]
    nbox = sum(extent for _, extent in segments)
    return pl.pallas_call(
        functools.partial(project_kernel, axis, count, segments, block),
        in_specs=[VMEM] * (count + 2),
        out_specs=VMEM,
        out_shape=pltpu.VMEM((outs, nbox, width), BF16),
        compiler_params=pltpu.CompilerParams(vmem_limit_bytes=16 * 2**20),
        cost_estimate=pl.CostEstimate(
            flops=2 * outs * nbox * width * points,
            bytes_accessed=2 * outs * nbox * width,
            transcendentals=0,
        ),
        name="project",
    )(near(enc), *map(near, pieces), near(proj))


def expand_kernel(axis, count, segments, block, fills, chunk, offsets, *refs):
    sources = refs[:1 + max(f[0] for f in fills)]
    mats, expand, adj, part, _, scattered, own, *others = refs[len(sources):len(sources) + 6 + count]
    padded, ready, terms, sems = refs[len(sources) + 6 + count:]
    outs, _, points = adj.shape
    operators, depth, width = mats.shape
    share = points // count
    me = lax.axis_index(axis)
    halves = padded.shape[0]
    lanes = padded.shape[3]
    edge = ROWS

    for source, begin, extent, place in fills:
        for h in range(halves):
            for e in range(outs):
                padded[h, e, place + edge:place + edge + extent, :] = sources[source][
                    e, begin:begin + extent, h * lanes:(h + 1) * lanes
                ].astype(F32)

    def copy(first, row, size, slot):
        return pltpu.make_async_copy(
            ready.at[:, pl.ds(row, size), :], scattered.at[0, :, pl.ds(first, size), :], sems.at[slot]
        )

    def body(first, row, size):
        moved = [
            padded[h, :, pl.ds(first + edge + offsets[t], size), :]
            .astype(BF16)
            .reshape(outs * size, lanes)
            for t in range(operators)
            for h in range(halves)
        ]
        local = jnp.dot(
            jnp.concatenate(moved, axis=1),
            mats[...].reshape(operators * depth, width),
            preferred_element_type=F32,
        ).astype(BF16)
        rows = pl.ds(row, size)
        for c in range(0, points, chunk):
            columns = slice(c, c + chunk)
            field = jnp.dot(local, expand[:, columns], preferred_element_type=F32)
            field = field.reshape(outs, size, chunk)
            ready[:, rows, columns] = field.astype(BF16)
            terms[0:size, columns] = part[pl.ds(first, size), columns] + jnp.sum(
                adj[:, pl.ds(first, size), columns].astype(F32) * field, axis=0
            )
        for m in range(count):
            start = pl.multiple_of((me ^ m) * share, share)
            piece = terms[0:size, pl.ds(start, share)]
            if m == 0:
                own[rows, :] = piece
            else:
                others[m - 1][rows, :] = piece.astype(BF16)
        copy(first, row, size, lax.div(row, ROWS)).start()

    in_blocks(segments, block, body)
    in_blocks(segments, block, lambda first, row, size: copy(first, row, size, lax.div(row, ROWS)).wait())


def expanded(axis, count, segments, fills, offsets, sources, mats, expand, adj, part, scattered, block=128, chunk=1024):
    outs, nbox, points = adj.shape
    width = expand.shape[0]
    share = points // count
    lanes = min(128, width)
    rows = sum(extent for _, extent in segments)
    alias = {} if scattered is None else {1 + len(sources) + 4: 0}
    if scattered is None:
        scattered = jnp.zeros((8, 128), F32)
    return pl.pallas_call(
        functools.partial(expand_kernel, axis, count, segments, block, fills, chunk),
        in_specs=[SMEM] + [VMEM] * (len(sources) + 4) + [ANY],
        out_specs=[ANY] + [VMEM] * count,
        out_shape=[
            jax.ShapeDtypeStruct((1, outs, nbox, points), BF16),
            pltpu.VMEM((rows, share), F32),
        ]
        + [pltpu.VMEM((rows, share), BF16)] * (count - 1),
        input_output_aliases=alias,
        scratch_shapes=[
            pltpu.VMEM((width // lanes, outs, nbox + 2 * ROWS, lanes), F32),
            pltpu.VMEM((outs, rows, points), BF16),
            pltpu.VMEM((block, points), F32),
            pltpu.SemaphoreType.DMA((rows // ROWS,)),
        ],
        compiler_params=pltpu.CompilerParams(vmem_limit_bytes=30 * 2**20),
        cost_estimate=pl.CostEstimate(
            flops=2 * outs * rows * width * (mats.shape[0] * width + points),
            bytes_accessed=rows * points * 2 * outs,
            transcendentals=0,
        ),
        name="expand",
    )(offsets, *map(near, sources), near(mats), near(expand), near(adj), near(part), scattered)


def exchange(x, axis, m, count):
    return lax.ppermute(x, axis, [(i, i ^ m) for i in range(count)])


def gather_pieces(pieces, axis, count):
    for m in sorted(range(1, count), key=lambda m: (bin(m).count("1"), -m)):
        if m not in pieces:
            pieces[m] = exchange(pieces[m & (m - 1)], axis, m & -m, count)
    return [pieces[m] for m in range(count)]


def scatter_pieces(own, parts, axis, count):
    parts = dict(enumerate(parts, start=1))
    received = []
    for m in sorted(range(1, count), key=lambda m: (-bin(m).count("1"), -m)):
        rest = m & (m - 1)
        got = exchange(parts[m], axis, m & -m, count)
        if rest:
            parts[rest] = (parts[rest].astype(F32) + got.astype(F32)).astype(BF16)
        else:
            received.append(got)
    for got in received:
        own = own + got.astype(F32)
    return own


def on_device(groups, tiles, contrast, incident, signs, adjoint, proj, mats, offsets, expand):
    nbox = contrast.shape[0]
    half = nbox // 2
    projected = [[(0, half), (nbox - ROWS, ROWS)], [(half, half - ROWS)]]
    finished = [[(ROWS, half - 2 * ROWS)], [(0, ROWS), (half - ROWS, half + ROWS)]]
    upward = [(i, i + 1) for i in range(tiles - 1)]
    downward = [(i + 1, i) for i in range(tiles - 1)]

    first = []
    for segments in projected:
        mine = jnp.concatenate([contrast[a:a + n] for a, n in segments], axis=0)
        pieces = {0: mine}
        for m in range(1, groups):
            if m & (m - 1) == 0:
                pieces[m] = exchange(mine, "group", m, groups)
        first.append(pieces)
    enc, adj, part = encode(signs, incident, adjoint)
    enc, first = lax.optimization_barrier((enc, first))

    gathered = gather_pieces(first[0], "group", groups)
    coeffs_a = project("group", groups, projected[0], enc, gathered, proj)
    low = lax.ppermute(coeffs_a[:, half:], "tile", upward)
    high = lax.ppermute(coeffs_a[:, :ROWS], "tile", downward)
    scattered, own_a, *parts_a = expanded(
        "group", groups, finished[0], [(0, 0, half, 0)], offsets, [coeffs_a],
        mats, expand, adj, part, None,
    )
    gathered = gather_pieces(first[1], "group", groups)
    coeffs_b = project("group", groups, projected[1], enc, gathered, proj)
    fills = [(0, 0, 2 * ROWS, 0), (0, half - 2 * ROWS, 2 * ROWS, half - 2 * ROWS)]
    fills += [(0, half, ROWS, nbox - ROWS), (1, 0, half - ROWS, half)]
    fills += [(2, 0, ROWS, -ROWS), (3, 0, ROWS, nbox)]
    grad_a = scatter_pieces(own_a, parts_a, "group", groups)
    scattered, own_b, *parts_b = expanded(
        "group", groups, finished[1], fills, offsets, [coeffs_a, coeffs_b, low, high],
        mats, expand, adj, part, scattered, block=144,
    )
    grad_b = scatter_pieces(own_b, parts_b, "group", groups)
    gradient = jnp.concatenate([grad_b[:ROWS], grad_a, grad_b[ROWS:]], axis=0)
    return scattered, gradient


def solution(mesh):
    in_specs = (
        P("tile", "group"),
        P("group", None, "tile", None),
        P("group", None, None),
        P("group", None, "tile", None),
        P(),
        P(),
        P(),
        P(),
    )
    out_specs = (P("group", None, "tile", None), P("tile", "group"))
    return jax.shard_map(
        functools.partial(on_device, mesh.shape["group"], mesh.shape["tile"]),
        mesh=mesh,
        in_specs=in_specs,
        out_specs=out_specs,
        check_vma=False,
    )
```

time: 188 us -> 67.7 us (0.36)
  waiting for transfers between devices: 65.5 us -> 16.2 us
  other arithmetic: 43.1 us -> 0.99 us
  matrix products: 40.6 us -> 0 us
  Pallas kernels: 0 us -> 24.8 us
  between operations: 21.6 us -> 0.81 us
  starting transfers between devices: 6.76 us -> 21.2 us
  local copies, waits for them, and re-layouts: 8.48 us -> 3.27 us
    dot_general x3 -> x0, matrix products: 40.6 us -> none  [the longest x1 15.3 us: on_device(): jnp.dot(local.reshape(-1, width), expand, preferred_element_type=jnp.floa...]
    reduce_scatter x1 -> x0, waiting for transfers between devices: 32.8 us -> none  [on_device(): gradient = lax.psum_scatter(terms, 'group', scatter_dimension=1, tiled=True)]
    all_gather x1 -> x0, waiting for transfers between devices: 32 us -> none  [on_device(): full_contrast = lax.all_gather(contrast, 'group', axis=1, tiled=True)]
    reduce_sum x1 -> x0, other arithmetic: 31.9 us -> none  [on_device(): terms = jnp.sum(adjoint_f * total, axis=0)]
    pallas_call x0 -> x5, Pallas kernels: none -> 24.8 us  [the longest x2 14.9 us: expanded(): pl.pallas_call(functools.partial(expand_kernel, axis, count, segments, bl...]
    ppermute x2 -> x14, waiting for transfers between devices: 0.01 us -> 16.2 us  [the longest x12 16.2 us: exchange(): return lax.ppermute(x, axis, [(i, i ^ m) for i in range(count)])]
    ppermute x2 -> x14, starting transfers between devices: 6.68 us -> 21.2 us  [the longest x12 14.6 us: exchange(): return lax.ppermute(x, axis, [(i, i ^ m) for i in range(count)])]
    broadcast_in_dim x1 -> x0, other arithmetic: 9.21 us -> none  [on_device(): return (field.astype(jnp.bfloat16)[None], gradient)]
  transfers between devices with their start and end apart: 4 -> 14, of which waited for: 2 -> 6; matrix products, arithmetic and copies ran while one was open for 5% -> 2% of each run, Pallas kernels for 0% -> 34%
where the time goes in v2:
time: 67.7 us; the launch traced here: 67.3 us
  Pallas kernels  24.8 us (37%)
  starting transfers between devices  21.2 us (31%)
  waiting for transfers between devices  16.2 us (24%)
  local copies, waits for them, and re-layouts  3.27 us (5%)
  other arithmetic  0.99 us (1%)
  between operations  0.81 us (1%)
    ppermute x12, waiting for transfers between devices, exchange(): return lax.ppermute(x, axis, [(i, i ^ m) for i in range(count)])  16.2 us
    pallas_call x2, Pallas kernels, expanded(): pl.pallas_call(functools.partial(expand_kernel, axis, count, segments, bl...  14.9 us
    ppermute x12, starting transfers between devices, exchange(): return lax.ppermute(x, axis, [(i, i ^ m) for i in range(count)])  14.6 us
    pallas_call x1, Pallas kernels, encode(): pl.pallas_call(functools.partial(encode_kernel, block, group), in_specs=[...  7.06 us
    ppermute x1, starting transfers between devices, on_device(): high = lax.ppermute(coeffs_a[:, :ROWS], 'tile', downward)  4.72 us
    pallas_call x2, Pallas kernels, project(): pl.pallas_call(functools.partial(project_kernel, axis, count, segments, b...  2.87 us
    slice x3, local copies, waits for them, and re-layouts, on_device(): mine = jnp.concatenate([contrast[a:a + n] for a, n in segments], axis=0)  2.53 us
    ppermute x1, starting transfers between devices, on_device(): low = lax.ppermute(coeffs_a[:, half:], 'tile', upward)  1.92 us
  transfers between devices with their start and end apart: 14, of which 6 were waited for; matrix products, arithmetic and copies ran while one was open for 2% of the time, Pallas kernels for 34%

profile of v2, /device:TPU:4, one launch (start us, length us, event | category | flops | bytes accessed | tf_op | source)
XLA Modules:
  0.0 67.3 jit_solution(3595069888158582921)
XLA Ops:
  0.6 0.9 %slice.21 = bf16[256,256]{1,0:T(8,128)(2,1)S(1)} slice(bf16[512,256]{1,0:T(8,128)(2,1)} %param.8), slice={[0:256], [0:256]} | slice | bytes 262144 | tf_op jit(solution)/shard_map/slice | solution.py:285
  1.5 0.7 %slice.22 = bf16[16,256]{1,0:T(8,128)(2,1)S(1)} slice(bf16[512,256]{1,0:T(8,128)(2,1)} %param.8), slice={[496:512], [0:256]} | slice | bytes 16384 | tf_op jit(solution)/shard_map/slice | solution.py:285
  2.3 1.6 %collective-permute-start = (bf16[272,256]{1,0:T(8,128)(2,1)S(1)}, bf16[272,256]{1,0:T(8,128)(2,1)S(1)}, u32[]{:S(2)}, u32[]{:S(2)}) collective-permute-start(bf16[272,256]{1,0:T(8,128)(2,1)S(1)} %pad_maximum_fusion.1.refs_0_), channel_id=1, source_target_pairs={{0,8},{8,0},{16,24},{24,16},{1,9},{9,1},{17,25},{25,17},{2,10},{10... | collective-permute-start | bytes 417800 | tf_op jit(solution)/shard_map/ppermute | solution.py:250
  3.9 2.6 %collective-permute-start.1 = (bf16[272,256]{1,0:T(8,128)(2,1)S(1)}, bf16[272,256]{1,0:T(8,128)(2,1)S(1)}, u32[]{:S(2)}, u32[]{:S(2)}) collective-permute-start(bf16[272,256]{1,0:T(8,128)(2,1)S(1)} %pad_maximum_fusion.1.refs_0_), channel_id=1, source_target_pairs={{0,16},{8,24},{16,0},{24,8},{1,17},{9,25},{17,1},{25,9},{2,18},{10... | collective-permute-start | bytes 417800 | tf_op jit(solution)/shard_map/ppermute | solution.py:250
  6.5 0.9 %slice.23.refs_0_ = bf16[240,256]{1,0:T(8,128)(2,1)S(1)} slice(bf16[512,256]{1,0:T(8,128)(2,1)} %param.8), slice={[256:496], [0:256]} | slice | bytes 245760 | tf_op jit(solution)/shard_map/slice | solution.py:285
  7.4 0.0 copy-start.1
  7.4 0.5 collective-permute-start.2
  7.9 0.3 collective-permute-start.3
  8.3 0.0 copy-start.3
  8.3 0.7 %copy-done.3 = s32[1,8,8]{2,1,0:T(8,128)S(1)} copy-done((s32[1,8,8]{2,1,0:T(8,128)S(1)}, s32[1,8,8]{2,1,0:T(8,128)}, u32[]{:S(2)}) %copy-start.3) | copy-done | bytes 280
  9.0 7.1 %encode.1 = (bf16[8,512,1024]{2,1,0:T(8,128)(2,1)S(1)}, bf16[8,512,1024]{2,1,0:T(8,128)(2,1)S(1)}, f32[512,1024]{1,0:T(8,128)S(1)}) custom-call(s32[1,8,8]{2,1,0:T(8,128)S(1)} %copy-done.3, bf16[1,8,512,1024]{3,2,1,0:T(8,128)(2,1)} %inc.1, bf16[1,8,512,1024]{3,2,1,0:T(8,128)(2,1)} %adj.1), custom_call_target="tpu_custom_call" | custom-call | flops 2147483648 | bytes 27262976 | tf_op jit(solution)/shard_map/encode/pallas_call | solution.py:88
  16.0 0.0 collective-permute-done.2.refs_1_
  16.0 2.2 %collective-permute-done.3.refs_2_ = bf16[240,256]{1,0:T(8,128)(2,1)S(1)} collective-permute-done((bf16[240,256]{1,0:T(8,128)(2,1)S(1)}, bf16[240,256]{1,0:T(8,128)(2,1)S(1)}, u32[]{:S(2)}, u32[]{:S(2)}) %collective-permute-start.3) | collective-permute-done | bytes 122912 | tf_op jit(solution)/shard_map/ppermute | solution.py:250
  18.2 0.0 collective-permute-done.refs_1_
  18.2 0.0 collective-permute-done.1.refs_2_
  18.2 0.0 copy-start
  18.2 0.0 copy-start.2
  18.3 0.0 copy-start.4
  18.3 0.4 collective-permute-start.5
  18.7 1.7 %collective-permute-start.4 = (bf16[272,256]{1,0:T(8,128)(2,1)S(1)}, bf16[272,256]{1,0:T(8,128)(2,1)S(1)}, u32[]{:S(2)}, u32[]{:S(2)}) collective-permute-start(bf16[272,256]{1,0:T(8,128)(2,1)S(1)} %collective-permute-done.1.refs_2_), channel_id=1, source_target_pairs={{0,8},{8,0},{16,24},{24,16},{1,9},{9,1},{17,25},{25,17},{2,10},{10... | collective-permute-start | bytes 417800 | tf_op jit(solution)/shard_map/ppermute | solution.py:250
  20.4 2.9 %collective-permute-done.5.refs_3_ = bf16[240,256]{1,0:T(8,128)(2,1)S(1)} collective-permute-done((bf16[240,256]{1,0:T(8,128)(2,1)S(1)}, bf16[240,256]{1,0:T(8,128)(2,1)S(1)}, u32[]{:S(2)}, u32[]{:S(2)}) %collective-permute-start.5) | collective-permute-done | bytes 122912 | tf_op jit(solution)/shard_map/ppermute | solution.py:250
  23.2 0.0 copy-done.1
  23.2 1.2 %project.3.refs_1_ = bf16[8,240,256]{2,1,0:T(8,128)(2,1)S(1)} custom-call(bf16[8,512,1024]{2,1,0:T(8,128)(2,1)S(1)} %get-tuple-element.23.enc, bf16[240,256]{1,0:T(8,128)(2,1)S(1)} %slice.23.refs_0_, bf16[240,256]{1,0:T(8,128)(2,1)S(1)} %collective-permute-done.2.refs_1_, bf16[240,256]{1,0:T(8,128)(2,1)S(1)} %collective-permute-done.3.refs_2_, ...), custom_call_target="tpu_custom_call" | custom-call | flops 1006632960 | bytes 983040 | tf_op jit(solution)/shard_map/project/pallas_call | solution.py:140
  24.4 0.3 collective-permute-done.4.refs_3_
  24.7 1.7 %project.2.refs_0_ = bf16[8,272,256]{2,1,0:T(8,128)(2,1)S(1)} custom-call(bf16[8,512,1024]{2,1,0:T(8,128)(2,1)S(1)} %get-tuple-element.23.enc, bf16[272,256]{1,0:T(8,128)(2,1)S(1)} %pad_maximum_fusion.1.refs_0_, bf16[272,256]{1,0:T(8,128)(2,1)S(1)} %collective-permute-done.refs_1_, bf16[272,256]{1,0:T(8,128)(2,1)S(1)} %collective-permute-done.1.refs_2_, ...), custom_call_target="tpu_custom_call" | custom-call | flops 1140850688 | bytes 1114112 | tf_op jit(solution)/shard_map/project/pallas_call | solution.py:140
  26.4 1.9 %collective-permute-start.6 = (bf16[8,16,256]{2,1,0:T(8,128)(2,1)S(1)}, bf16[8,16,256]{2,1,0:T(8,128)(2,1)S(1)}, u32[]{:S(2)}, u32[]{:S(2)}) collective-permute-start(bf16[8,16,256]{2,1,0:T(8,128)(2,1)S(1)} %get-tuple-element.43), channel_id=1, source_target_pairs={{0,1},{1,2},{2,3},{3,4},{4,5},{5,6},{6,7},{8,9},{9,10},{10,11},{11... | collective-permute-start | bytes 196616 | tf_op jit(solution)/shard_map/ppermute | solution.py:296
  28.3 4.7 %collective-permute-start.7 = (bf16[8,16,256]{2,1,0:T(8,128)(2,1)S(1)}, bf16[8,16,256]{2,1,0:T(8,128)(2,1)S(1)}, u32[]{:S(2)}, u32[]{:S(2)}) collective-permute-start(bf16[8,16,256]{2,1,0:T(8,128)(2,1)S(1)} %get-tuple-element.42), channel_id=1, source_target_pairs={{1,0},{2,1},{3,2},{4,3},{5,4},{6,5},{7,6},{9,8},{10,9},{11,10},{12... | collective-permute-start | bytes 196616 | tf_op jit(solution)/shard_map/ppermute | solution.py:297
  33.1 0.0 copy-done
  33.1 0.0 copy-done.2
  33.1 0.0 copy-done.4
  33.1 6.6 %expand.2 = (bf16[1,8,512,1024]{3,2,1,0:T(8,128)(2,1)}, f32[224,256]{1,0:T(8,128)S(1)}, bf16[224,256]{1,0:T(8,128)(2,1)S(1)}, bf16[224,256]{1,0:T(8,128)(2,1)S(1)}, bf16[224,256]{1,0:T(8,128)(2,1)S(1)}) custom-call(s32[6]{0:T(128)S(1)} %copy-done.4, bf16[8,272,256]{2,1,0:T(8,128)(2,1)S(1)} %project.2.refs_0_, bf16[6,256,256]{2,1,0:T(8,128)(2,1)S(1)} %copy-done, ...), custom_call_target="tpu_custom_call" | custom-call | flops 2348810240 | bytes 3670016 | tf_op jit(solution)/shard_map/expand/pallas_call | solution.py:223
  39.7 1.2 %collective-permute-start.11 = (bf16[224,256]{1,0:T(8,128)(2,1)S(1)}, bf16[224,256]{1,0:T(8,128)(2,1)S(1)}, u32[]{:S(2)}, u32[]{:S(2)}) collective-permute-start(bf16[224,256]{1,0:T(8,128)(2,1)S(1)} %get-tuple-element.40), channel_id=1, source_target_pairs={{0,8},{8,0},{16,24},{24,16},{1,9},{9,1},{17,25},{25,17},{2,10},{10... | collective-permute-start | bytes 344072 | tf_op jit(solution)/shard_map/ppermute | solution.py:250
  40.9 0.9 %collective-permute-start.13 = (bf16[224,256]{1,0:T(8,128)(2,1)S(1)}, bf16[224,256]{1,0:T(8,128)(2,1)S(1)}, u32[]{:S(2)}, u32[]{:S(2)}) collective-permute-start(bf16[224,256]{1,0:T(8,128)(2,1)S(1)} %get-tuple-element.41), channel_id=1, source_target_pairs={{0,8},{8,0},{16,24},{24,16},{1,9},{9,1},{17,25},{25,17},{2,10},{10... | collective-permute-start | bytes 344072 | tf_op jit(solution)/shard_map/ppermute | solution.py:250
  41.8 0.0 collective-permute-done.6.refs_2_
  41.8 0.0 collective-permute-done.7.refs_3_
  41.8 8.3 %expand.3 = (bf16[1,8,512,1024]{3,2,1,0:T(8,128)(2,1)}, f32[288,256]{1,0:T(8,128)S(1)}, bf16[288,256]{1,0:T(8,128)(2,1)S(1)}, bf16[288,256]{1,0:T(8,128)(2,1)S(1)}, bf16[288,256]{1,0:T(8,128)(2,1)S(1)}) custom-call(s32[6]{0:T(128)S(1)} %copy-done.4, bf16[8,272,256]{2,1,0:T(8,128)(2,1)S(1)} %project.2.refs_0_, ...), custom_call_target="tpu_custom_call", output_to_operand_aliasing={{0}: (9, {})} | custom-call | flops 3019898880 | bytes 4718592 | tf_op jit(solution)/shard_map/expand/pallas_call | solution.py:223
  50.1 1.2 %collective-permute-start.8 = (bf16[288,256]{1,0:T(8,128)(2,1)S(1)}, bf16[288,256]{1,0:T(8,128)(2,1)S(1)}, u32[]{:S(2)}, u32[]{:S(2)}) collective-permute-start(bf16[288,256]{1,0:T(8,128)(2,1)S(1)} %get-tuple-element.36), channel_id=1, source_target_pairs={{0,8},{8,0},{16,24},{24,16},{1,9},{9,1},{17,25},{25,17},{2,10},{10... | collective-permute-start | bytes 442376 | tf_op jit(solution)/shard_map/ppermute | solution.py:250
  51.4 0.9 %collective-permute-start.10 = (bf16[288,256]{1,0:T(8,128)(2,1)S(1)}, bf16[288,256]{1,0:T(8,128)(2,1)S(1)}, u32[]{:S(2)}, u32[]{:S(2)}) collective-permute-start(bf16[288,256]{1,0:T(8,128)(2,1)S(1)} %get-tuple-element.37), channel_id=1, source_target_pairs={{0,8},{8,0},{16,24},{24,16},{1,9},{9,1},{17,25},{25,17},{2,10},{10... | collective-permute-start | bytes 442376 | tf_op jit(solution)/shard_map/ppermute | solution.py:250
  52.2 0.0 collective-permute-done.11
  52.3 2.3 %collective-permute-start.12 = (bf16[224,256]{1,0:T(8,128)(2,1)S(1)}, bf16[224,256]{1,0:T(8,128)(2,1)S(1)}, u32[]{:S(2)}, u32[]{:S(2)}) collective-permute-start(bf16[224,256]{1,0:T(8,128)(2,1)S(1)} %add_convert_fusion.1), channel_id=1, source_target_pairs={{0,16},{8,24},{16,0},{24,8},{1,17},{9,25},{17,1},{25,9},{2,18},{10... | collective-permute-start | bytes 344072 | tf_op jit(solution)/shard_map/ppermute | solution.py:250
  54.6 3.9 %collective-permute-done.8 = bf16[288,256]{1,0:T(8,128)(2,1)S(1)} collective-permute-done((bf16[288,256]{1,0:T(8,128)(2,1)S(1)}, bf16[288,256]{1,0:T(8,128)(2,1)S(1)}, u32[]{:S(2)}, u32[]{:S(2)}) %collective-permute-start.8) | collective-permute-done | bytes 147488 | tf_op jit(solution)/shard_map/ppermute | solution.py:250
  58.5 0.9 %collective-permute-start.9 = (bf16[288,256]{1,0:T(8,128)(2,1)S(1)}, bf16[288,256]{1,0:T(8,128)(2,1)S(1)}, u32[]{:S(2)}, u32[]{:S(2)}) collective-permute-start(bf16[288,256]{1,0:T(8,128)(2,1)S(1)} %add_convert_fusion), channel_id=1, source_target_pairs={{0,16},{8,24},{16,0},{24,8},{1,17},{9,25},{17,1},{25,9},{2,18},{10... | collective-permute-start | bytes 442376 | tf_op jit(solution)/shard_map/ppermute | solution.py:250
  59.5 0.0 collective-permute-done.13
  59.5 2.0 %collective-permute-done.12 = bf16[224,256]{1,0:T(8,128)(2,1)S(1)} collective-permute-done((bf16[224,256]{1,0:T(8,128)(2,1)S(1)}, bf16[224,256]{1,0:T(8,128)(2,1)S(1)}, u32[]{:S(2)}, u32[]{:S(2)}) %collective-permute-start.12) | collective-permute-done | bytes 114720 | tf_op jit(solution)/shard_map/ppermute | solution.py:250
  61.5 0.0 collective-permute-done.10
  61.6 4.8 %collective-permute-done.9 = bf16[288,256]{1,0:T(8,128)(2,1)S(1)} collective-permute-done((bf16[288,256]{1,0:T(8,128)(2,1)S(1)}, bf16[288,256]{1,0:T(8,128)(2,1)S(1)}, u32[]{:S(2)}, u32[]{:S(2)}) %collective-permute-start.9) | collective-permute-done | bytes 147488 | tf_op jit(solution)/shard_map/ppermute | solution.py:250
  66.5 0.8 %pad_maximum_fusion = f32[512,256]{1,0:T(8,128)} fusion(f32[272,256]{1,0:T(8,128)S(1)} %slice.31, f32[224,256]{1,0:T(8,128)S(1)} %convert_add_fusion.1, f32[16,256]{1,0:T(8,128)S(1)} %slice.30), kind=kLoop, calls=%fused_computation | loop fusion | flops 262144 | bytes 1048576 | tf_op jit(solution)/shard_map/concatenate | solution.py:313
  (9 shorter events, 0.2 us)
Async XLA Ops:
  2.3 16.0 %collective-permute-start = (bf16[272,256]{1,0:T(8,128)(2,1)S(1)}, bf16[272,256]{1,0:T(8,128)(2,1)S(1)}, u32[]{:S(2)}, u32[]{:S(2)}) collective-permute-start(bf16[272,256]{1,0:T(8,128)(2,1)S(1)} %pad_maximum_fusion.1.refs_0_), channel_id=1, source_target_pairs={{0,8},{8,0},{16,24},{24,16},{1,9},{9,1},{17,25},{25,17},{2,10},{10... | collective-permute-start | bytes 417800 | tf_op jit(solution)/shard_map/ppermute | solution.py:250
  3.9 14.3 %collective-permute-start.1 = (bf16[272,256]{1,0:T(8,128)(2,1)S(1)}, bf16[272,256]{1,0:T(8,128)(2,1)S(1)}, u32[]{:S(2)}, u32[]{:S(2)}) collective-permute-start(bf16[272,256]{1,0:T(8,128)(2,1)S(1)} %pad_maximum_fusion.1.refs_0_), channel_id=1, source_target_pairs={{0,16},{8,24},{16,0},{24,8},{1,17},{9,25},{17,1},{25,9},{2,18},{10... | collective-permute-start | bytes 417800 | tf_op jit(solution)/shard_map/ppermute | solution.py:250
  7.4 15.8 %copy-start.1 = (bf16[1024,256]{1,0:T(8,128)(2,1)S(1)}, bf16[1024,256]{1,0:T(8,128)(2,1)}, u32[]{:S(2)}) copy-start(bf16[1024,256]{1,0:T(8,128)(2,1)} %refs_4_.4) | copy-start | bytes 1572868
  7.4 8.6 %collective-permute-start.2 = (bf16[240,256]{1,0:T(8,128)(2,1)S(1)}, bf16[240,256]{1,0:T(8,128)(2,1)S(1)}, u32[]{:S(2)}, u32[]{:S(2)}) collective-permute-start(bf16[240,256]{1,0:T(8,128)(2,1)S(1)} %slice.23.refs_0_), channel_id=1, source_target_pairs={{0,8},{8,0},{16,24},{24,16},{1,9},{9,1},{17,25},{25,17},{2,10},{10... | collective-permute-start | bytes 368648 | tf_op jit(solution)/shard_map/ppermute | solution.py:250
  7.9 10.3 %collective-permute-start.3 = (bf16[240,256]{1,0:T(8,128)(2,1)S(1)}, bf16[240,256]{1,0:T(8,128)(2,1)S(1)}, u32[]{:S(2)}, u32[]{:S(2)}) collective-permute-start(bf16[240,256]{1,0:T(8,128)(2,1)S(1)} %slice.23.refs_0_), channel_id=1, source_target_pairs={{0,16},{8,24},{16,0},{24,8},{1,17},{9,25},{17,1},{25,9},{2,18},{10... | collective-permute-start | bytes 368648 | tf_op jit(solution)/shard_map/ppermute | solution.py:250
  8.3 0.7 %copy-start.3 = (s32[1,8,8]{2,1,0:T(8,128)S(1)}, s32[1,8,8]{2,1,0:T(8,128)}, u32[]{:S(2)}) copy-start(s32[1,8,8]{2,1,0:T(8,128)} %signs.1) | copy-start | bytes 772
  18.2 14.8 %copy-start = (bf16[6,256,256]{2,1,0:T(8,128)(2,1)S(1)}, bf16[6,256,256]{2,1,0:T(8,128)(2,1)}, u32[]{:S(2)}) copy-start(bf16[6,256,256]{2,1,0:T(8,128)(2,1)} %refs_4_.5) | copy-start | bytes 2359300
  18.2 14.8 %copy-start.2 = (bf16[256,1024]{1,0:T(8,128)(2,1)S(1)}, bf16[256,1024]{1,0:T(8,128)(2,1)}, u32[]{:S(2)}) copy-start(bf16[256,1024]{1,0:T(8,128)(2,1)} %refs_5_.1) | copy-start | bytes 1572868
  18.3 14.8 %copy-start.4 = (s32[6]{0:T(128)S(1)}, s32[6]{0:T(128)}, u32[]{:S(2)}) copy-start(s32[6]{0:T(128)} %offsets.3) | copy-start | bytes 76
  18.3 4.9 %collective-permute-start.5 = (bf16[240,256]{1,0:T(8,128)(2,1)S(1)}, bf16[240,256]{1,0:T(8,128)(2,1)S(1)}, u32[]{:S(2)}, u32[]{:S(2)}) collective-permute-start(bf16[240,256]{1,0:T(8,128)(2,1)S(1)} %collective-permute-done.3.refs_2_), channel_id=1, source_target_pairs={{0,8},{8,0},{16,24},{24,16},{1,9},{9,1},{17,25},{25,17},{2,10},{10... | collective-permute-start | bytes 368648 | tf_op jit(solution)/shard_map/ppermute | solution.py:250
  18.7 6.0 %collective-permute-start.4 = (bf16[272,256]{1,0:T(8,128)(2,1)S(1)}, bf16[272,256]{1,0:T(8,128)(2,1)S(1)}, u32[]{:S(2)}, u32[]{:S(2)}) collective-permute-start(bf16[272,256]{1,0:T(8,128)(2,1)S(1)} %collective-permute-done.1.refs_2_), channel_id=1, source_target_pairs={{0,8},{8,0},{16,24},{24,16},{1,9},{9,1},{17,25},{25,17},{2,10},{10... | collective-permute-start | bytes 417800 | tf_op jit(solution)/shard_map/ppermute | solution.py:250
  26.4 15.4 %collective-permute-start.6 = (bf16[8,16,256]{2,1,0:T(8,128)(2,1)S(1)}, bf16[8,16,256]{2,1,0:T(8,128)(2,1)S(1)}, u32[]{:S(2)}, u32[]{:S(2)}) collective-permute-start(bf16[8,16,256]{2,1,0:T(8,128)(2,1)S(1)} %get-tuple-element.43), channel_id=1, source_target_pairs={{0,1},{1,2},{2,3},{3,4},{4,5},{5,6},{6,7},{8,9},{9,10},{10,11},{11... | collective-permute-start | bytes 196616 | tf_op jit(solution)/shard_map/ppermute | solution.py:296
  28.3 13.5 %collective-permute-start.7 = (bf16[8,16,256]{2,1,0:T(8,128)(2,1)S(1)}, bf16[8,16,256]{2,1,0:T(8,128)(2,1)S(1)}, u32[]{:S(2)}, u32[]{:S(2)}) collective-permute-start(bf16[8,16,256]{2,1,0:T(8,128)(2,1)S(1)} %get-tuple-element.42), channel_id=1, source_target_pairs={{1,0},{2,1},{3,2},{4,3},{5,4},{6,5},{7,6},{9,8},{10,9},{11,10},{12... | collective-permute-start | bytes 196616 | tf_op jit(solution)/shard_map/ppermute | solution.py:297
  39.7 12.5 %collective-permute-start.11 = (bf16[224,256]{1,0:T(8,128)(2,1)S(1)}, bf16[224,256]{1,0:T(8,128)(2,1)S(1)}, u32[]{:S(2)}, u32[]{:S(2)}) collective-permute-start(bf16[224,256]{1,0:T(8,128)(2,1)S(1)} %get-tuple-element.40), channel_id=1, source_target_pairs={{0,8},{8,0},{16,24},{24,16},{1,9},{9,1},{17,25},{25,17},{2,10},{10... | collective-permute-start | bytes 344072 | tf_op jit(solution)/shard_map/ppermute | solution.py:250
  40.9 18.5 %collective-permute-start.13 = (bf16[224,256]{1,0:T(8,128)(2,1)S(1)}, bf16[224,256]{1,0:T(8,128)(2,1)S(1)}, u32[]{:S(2)}, u32[]{:S(2)}) collective-permute-start(bf16[224,256]{1,0:T(8,128)(2,1)S(1)} %get-tuple-element.41), channel_id=1, source_target_pairs={{0,8},{8,0},{16,24},{24,16},{1,9},{9,1},{17,25},{25,17},{2,10},{10... | collective-permute-start | bytes 344072 | tf_op jit(solution)/shard_map/ppermute | solution.py:250
  50.1 8.4 %collective-permute-start.8 = (bf16[288,256]{1,0:T(8,128)(2,1)S(1)}, bf16[288,256]{1,0:T(8,128)(2,1)S(1)}, u32[]{:S(2)}, u32[]{:S(2)}) collective-permute-start(bf16[288,256]{1,0:T(8,128)(2,1)S(1)} %get-tuple-element.36), channel_id=1, source_target_pairs={{0,8},{8,0},{16,24},{24,16},{1,9},{9,1},{17,25},{25,17},{2,10},{10... | collective-permute-start | bytes 442376 | tf_op jit(solution)/shard_map/ppermute | solution.py:250
  51.4 10.2 %collective-permute-start.10 = (bf16[288,256]{1,0:T(8,128)(2,1)S(1)}, bf16[288,256]{1,0:T(8,128)(2,1)S(1)}, u32[]{:S(2)}, u32[]{:S(2)}) collective-permute-start(bf16[288,256]{1,0:T(8,128)(2,1)S(1)} %get-tuple-element.37), channel_id=1, source_target_pairs={{0,8},{8,0},{16,24},{24,16},{1,9},{9,1},{17,25},{25,17},{2,10},{10... | collective-permute-start | bytes 442376 | tf_op jit(solution)/shard_map/ppermute | solution.py:250
  52.3 9.2 %collective-permute-start.12 = (bf16[224,256]{1,0:T(8,128)(2,1)S(1)}, bf16[224,256]{1,0:T(8,128)(2,1)S(1)}, u32[]{:S(2)}, u32[]{:S(2)}) collective-permute-start(bf16[224,256]{1,0:T(8,128)(2,1)S(1)} %add_convert_fusion.1), channel_id=1, source_target_pairs={{0,16},{8,24},{16,0},{24,8},{1,17},{9,25},{17,1},{25,9},{2,18},{10... | collective-permute-start | bytes 344072 | tf_op jit(solution)/shard_map/ppermute | solution.py:250
  58.5 7.8 %collective-permute-start.9 = (bf16[288,256]{1,0:T(8,128)(2,1)S(1)}, bf16[288,256]{1,0:T(8,128)(2,1)S(1)}, u32[]{:S(2)}, u32[]{:S(2)}) collective-permute-start(bf16[288,256]{1,0:T(8,128)(2,1)S(1)} %add_convert_fusion), channel_id=1, source_target_pairs={{0,16},{8,24},{16,0},{24,8},{1,17},{9,25},{17,1},{25,9},{2,18},{10... | collective-permute-start | bytes 442376 | tf_op jit(solution)/shard_map/ppermute | solution.py:250

commit v3 on v0

v3 whole, which is shorter than its diff:
```python
import functools

import jax
import jax.numpy as jnp
from jax import lax
from jax.experimental import pallas as pl
from jax.experimental.pallas import tpu as pltpu
from jax.sharding import PartitionSpec as P

F32 = jnp.float32
BF16 = jnp.bfloat16
ROWS = 16
VMEM = pl.BlockSpec(memory_space=pltpu.VMEM)
SMEM = pl.BlockSpec(memory_space=pltpu.SMEM)
ANY = pl.BlockSpec(memory_space=pl.ANY)
HBM = pl.BlockSpec(memory_space=pltpu.HBM)


def near(x):
    return pltpu.with_memory_space_constraint(x, pltpu.VMEM)


def far(x):
    return pltpu.with_memory_space_constraint(x, pltpu.HBM)


def split_kernel(runs, whole, *refs):
    outs, sems = refs[:-1], refs[-1]
    copies = [
        pltpu.make_async_copy(
            whole.at[first:first + extent, :], outs[to].at[row:row + extent, :], sems.at[i]
        )
        for i, (to, row, first, extent) in enumerate(runs)
    ]
    for copy in copies:
        copy.start()
    for copy in copies:
        copy.wait()


def split(x, parts):
    runs, shapes = [], []
    for to, part in enumerate(parts):
        row = 0
        for first, extent in part:
            runs.append((to, row, first, extent))
            row += extent
        shapes.append(pltpu.VMEM((row, x.shape[1]), x.dtype))
    return pl.pallas_call(
        functools.partial(split_kernel, runs),
        in_specs=[HBM],
        out_specs=[VMEM] * len(parts),
        out_shape=shapes,
        scratch_shapes=[pltpu.SemaphoreType.DMA((len(runs),))],
        name="split",
    )(far(x))


def encode_kernel(block, group, signs, inc, enc, incv, mix, sems):
    count, nbox, points = incv.shape
    outs = enc.shape[0]
    size = count * group
    steps = nbox // block

    def copy(i):
        rows = pl.ds(pl.multiple_of(i * block, ROWS), block)
        return pltpu.make_async_copy(inc.at[0, :, rows, :], incv.at[:, rows, :], sems.at[i])

    for i in range(steps):
        copy(i).start()

    r = lax.broadcasted_iota(jnp.int32, (group, size), 0)
    c = lax.broadcasted_iota(jnp.int32, (group, size), 1)
    diagonal = (c % group) == r
    for e in range(outs):
        value = jnp.zeros((group, size), F32)
        for s in range(count):
            value = jnp.where(c // group == s, signs[0, e, s].astype(F32), value)
        mix[e * group:(e + 1) * group, :] = jnp.where(diagonal, value, 0.0).astype(BF16)

    def step(i, carry):
        copy(i).wait()
        for j in range(block // group):
            rows = pl.ds(pl.multiple_of(i * block + j * group, ROWS), group)
            x = incv[:, rows, :].reshape(size, points)
            encoded = jnp.dot(mix[...], x, preferred_element_type=F32).astype(BF16)
            enc[:, rows, :] = encoded.reshape(outs, group, points)
        return carry

    lax.fori_loop(0, steps, step, 0)


def encode(signs, incident, block=64):
    _, count, nbox, points = incident.shape
    outs = signs.shape[1]
    group = 256 // count
    return pl.pallas_call(
        functools.partial(encode_kernel, block, group),
        in_specs=[SMEM, HBM],
        out_specs=VMEM,
        out_shape=pltpu.VMEM((outs, nbox, points), BF16),
        scratch_shapes=[
            pltpu.VMEM((count, nbox, points), BF16),
            pltpu.VMEM((outs * group, count * group), BF16),
            pltpu.SemaphoreType.DMA((nbox // block,)),
        ],
        compiler_params=pltpu.CompilerParams(vmem_limit_bytes=12 * 2**20),
        cost_estimate=pl.CostEstimate(
            flops=2 * outs * count * group * nbox * points,
            bytes_accessed=nbox * points * 2 * count,
            transcendentals=0,
        ),
        name="encode",
    )(signs, far(incident))


def weigh_kernel(block, adj, enc, _, adjv, part, sems):
    nbox = enc.shape[1]
    steps = nbox // block

    def copy(i):
        rows = pl.ds(pl.multiple_of(i * block, ROWS), block)
        return pltpu.make_async_copy(adj.at[0, :, rows, :], adjv.at[:, rows, :], sems.at[i])

    for i in range(steps):
        copy(i).start()

    def step(i, carry):
        copy(i).wait()
        rows = pl.ds(pl.multiple_of(i * block, ROWS), block)
        part[rows, :] = jnp.sum(adjv[:, rows, :].astype(F32) * enc[:, rows, :].astype(F32), axis=0)
        return carry

    lax.fori_loop(0, steps, step, 0)


def weigh(adjoint, enc, after, block=64):
    outs, nbox, points = enc.shape
    return pl.pallas_call(
        functools.partial(weigh_kernel, block),
        in_specs=[HBM, VMEM, VMEM],
        out_specs=[VMEM, VMEM],
        out_shape=[pltpu.VMEM((outs, nbox, points), BF16), pltpu.VMEM((nbox, points), F32)],
        scratch_shapes=[pltpu.SemaphoreType.DMA((nbox // block,))],
        compiler_params=pltpu.CompilerParams(vmem_limit_bytes=8 * 2**20),
        cost_estimate=pl.CostEstimate(
            flops=1, bytes_accessed=1, transcendentals=0
        ),
        name="weigh",
    )(far(adjoint), near(enc), near(after))


def add_kernel(jobs, *refs):
    for out, place, terms in jobs:
        value = None
        for ref, slot, first, extent in terms:
            ref = refs[ref]
            x = ref[first:first + extent, :] if slot is None else ref[slot, first:first + extent, :]
            x = x.astype(F32)
            value = x if value is None else value + x
        refs[out][place:place + value.shape[0], :] = value.astype(refs[out].dtype)


def add(jobs, operands, shapes):
    return pl.pallas_call(
        functools.partial(add_kernel, jobs),
        in_specs=[VMEM] * len(operands),
        out_specs=[VMEM] * len(shapes),
        out_shape=shapes,
        name="add",
    )(*map(near, operands))


def stage_kernel(axis, count, mine, blocks, edges_at, phases, layout, *refs):
    named, at = {}, 0
    for name, number in layout:
        named[name] = refs[at] if number is None else refs[at:at + number]
        at += 1 if number is None else number
    offsets, mats, expand = named["offsets"], named["mats"], named["expand"]
    adj, part = named["adj"], named["part"]
    padded, scattered = named["padded"], named["scattered"]
    ready, held, terms, sems = refs[at:]
    outs, nbox, points = adj.shape
    operators, depth, width = mats.shape
    share = points // count
    halves, _, _, lanes = padded.shape
    me = lax.axis_index(axis)
    starts = [pl.multiple_of((me ^ m) * share, share) for m in range(count)]

    def fill(place, extent, values):
        for h in range(halves):
            padded[h, :, place + ROWS:place + ROWS + extent, :] = values[
                :, :, h * lanes:(h + 1) * lanes
            ].astype(F32)

    if mine:
        enc, proj, contrasts = named["enc"], named["proj"], named["pieces"]
        weights = jnp.concatenate([proj[pl.ds(s, share), :] for s in starts], axis=0)
        for runs in mine:
            source = [
                jnp.concatenate(
                    [
                        contrast[row:row + size, :][None]
                        * enc[:, first:first + size, pl.ds(start, share)]
                        for contrast, start in zip(contrasts, starts)
                    ],
                    axis=2,
                )
                for first, row, size in runs
            ]
            total = sum(size for _, _, size in runs)
            source = jnp.concatenate(source, axis=1).reshape(outs * total, points)
            coeffs = jnp.dot(source, weights, preferred_element_type=F32).astype(BF16)
            coeffs = coeffs.reshape(outs, total, width)
            done = 0
            for first, _, size in runs:
                fill(first, size, coeffs[:, done:done + size, :])
                done += size
    for edge, place in zip(named.get("edges", ()), edges_at):
        for h in range(halves):
            edge[:, :, h * lanes:(h + 1) * lanes] = padded[
                h, :, place + ROWS:place + 2 * ROWS, :
            ].astype(BF16)
    if "low" in named:
        fill(-ROWS, ROWS, named["low"][...])
        fill(nbox, ROWS, named["high"][...])

    def translated(first, size):
        moved = [
            padded[h, :, pl.ds(first + ROWS + offsets[t], size), :]
            .astype(BF16)
            .reshape(outs * size, lanes)
            for t in range(operators)
            for h in range(halves)
        ]
        return jnp.dot(
            jnp.concatenate(moved, axis=1),
            mats[...].reshape(operators * depth, width),
            preferred_element_type=F32,
        ).astype(BF16)

    def copy(i):
        first, size, row = blocks[i]
        return pltpu.make_async_copy(
            ready.at[:, row:row + size, :], scattered.at[0, :, first:first + size, :], sems.at[i]
        )

    def finish(i, local):
        first, size, row = blocks[i]
        field = jnp.dot(local, expand[...], preferred_element_type=F32)
        field = field.reshape(outs, size, points)
        ready[:, row:row + size, :] = field.astype(BF16)
        terms[0:size, :] = part[first:first + size, :] + jnp.sum(
            adj[:, first:first + size, :].astype(F32) * field, axis=0
        )
        named["own"][row:row + size, :] = terms[0:size, pl.ds(starts[0], share)]
        for phase, members in enumerate(phases):
            for slot, m in enumerate(members):
                named["sent"][phase][slot, row:row + size, :] = terms[
                    0:size, pl.ds(starts[m], share)
                ].astype(BF16)

    rows_of = [outs * size for _, size, _ in blocks]
    held[0, 0:rows_of[0], :] = translated(*blocks[0][:2])
    for i in range(len(blocks)):
        if i + 1 < len(blocks):
            following = translated(*blocks[i + 1][:2])
        finish(i, held[i % 2, 0:rows_of[i], :])
        if i + 1 < len(blocks):
            held[(i + 1) % 2, 0:rows_of[i + 1], :] = following
        copy(i).start()
    for i in range(len(blocks)):
        copy(i).wait()


def stage(axis, count, mine, blocks, edges_at, phases, inputs, state, weight=1.0):
    outs, nbox, points = inputs["adj"].shape
    depth, width = inputs["mats"].shape[1:]
    share = points // count
    lanes = min(128, width)
    placed, rows = [], 0
    for first, size in blocks:
        placed.append((first, size, rows))
        rows += size
    most = max(size for _, size in blocks)

    layout, operands, specs = [], [], []
    for name, value in inputs.items():
        many = isinstance(value, (list, tuple))
        layout.append((name, len(value) if many else None))
        for x in value if many else [value]:
            operands.append(x if name == "offsets" else near(x))
            specs.append(SMEM if name == "offsets" else VMEM)
    aliases = {}
    if state is not None:
        layout += [("padded_in", None), ("scattered_in", None)]
        aliases = {len(operands): 0, len(operands) + 1: 1}
        operands += [near(state[0]), state[1]]
        specs += [VMEM, ANY]

    layout += [("padded", None), ("scattered", None), ("own", None), ("sent", len(phases))]
    out_shape = [
        pltpu.VMEM((width // lanes, outs, nbox + 2 * ROWS, lanes), F32),
        jax.ShapeDtypeStruct((1, outs, nbox, points), BF16),
        pltpu.VMEM((rows, share), F32),
    ]
    out_shape += [pltpu.VMEM((len(members), rows, share), BF16) for members in phases]
    out_specs = [VMEM, ANY, VMEM] + [VMEM] * len(phases)
    if edges_at:
        layout.append(("edges", len(edges_at)))
        out_shape += [pltpu.VMEM((outs, ROWS, width), BF16)] * len(edges_at)
        out_specs += [VMEM] * len(edges_at)
    made = sum(size for runs in mine for _, _, size in runs)
    result = pl.pallas_call(
        functools.partial(stage_kernel, axis, count, mine, placed, edges_at, phases, layout),
        in_specs=specs,
        out_specs=out_specs,
        out_shape=out_shape,
        input_output_aliases=aliases,
        scratch_shapes=[
            pltpu.VMEM((outs, rows, points), BF16),
            pltpu.VMEM((2, outs * most, width), BF16),
            pltpu.VMEM((most, points), F32),
            pltpu.SemaphoreType.DMA((len(blocks),)),
        ],
        compiler_params=pltpu.CompilerParams(vmem_limit_bytes=16 * 2**20),
        cost_estimate=pl.CostEstimate(
            flops=int(
                weight * 2 * outs * width
                * (made * points + rows * (inputs["mats"].shape[0] * depth + points))
            ),
            bytes_accessed=int(weight * rows * points * 2 * outs),
            transcendentals=0,
        ),
        name="stage",
    )(*operands)
    state, own, sent = result[:2], result[2], result[3:3 + len(phases)]
    return state, own, sent, result[3 + len(phases):]


def cut_up(first, extent, parts):
    tiles = extent // ROWS
    sizes = [ROWS * (tiles // parts + (i < tiles % parts)) for i in range(parts)]
    return [(first + sum(sizes[:i]), size) for i, size in enumerate(sizes) if size]


def exchange(x, axis, m, count):
    return lax.ppermute(x, axis, [(i, i ^ m) for i in range(count)])


def gather_pieces(pieces, axis, count):
    for m in sorted(range(1, count), key=lambda m: (bin(m).count("1"), -m)):
        if m not in pieces:
            pieces[m] = exchange(pieces[m & (m - 1)], axis, m & -m, count)
    return [pieces[m] for m in range(count)]


def hypercube(count):
    bits = [1 << k for k in range(count.bit_length() - 1)]
    return [[m for m in reversed(range(count)) if m & -m == b] for b in bits]


def folded(members, sent, got, kept):
    for s, m in enumerate(members):
        if m & (m - 1):
            kept[m & (m - 1)] = (kept[m & (m - 1)].astype(F32) + got[s].astype(F32)).astype(BF16)
    return kept


def scatter_steps(sent, axis, count):
    phases = hypercube(count)
    kept = {m: sent[p][s] for p, members in enumerate(phases) for s, m in enumerate(members)}
    final = []
    for p, members in enumerate(phases):
        whole = sent[p] if p == 0 else jnp.stack([kept[m] for m in members])
        got = exchange(whole, axis, 1 << p, count)
        kept = folded(members, sent, got, kept)
        final.append((got, len(members) - 1))
    return final


def first_sums(own, got, sent, after, axis, count):
    phases = hypercube(count)
    came = exchange(sent[0], axis, 1, count)
    rows, share = own.shape
    rows_b = sent[0].shape[1]
    operands = [own] + [x for x, _ in got] + [came] + list(sent[1:]) + [after]
    at = 1 + len(got)
    outs = len(operands)
    jobs = [(outs, 0, [(0, None, 0, rows)] + [(1 + i, slot, 0, rows) for i, (_, slot) in enumerate(got)])]
    shapes = [pltpu.VMEM((rows, share), F32)]
    order = []
    for p, members in enumerate(phases[1:]):
        for s, m in enumerate(members):
            terms = [(at + 1 + p, s, 0, rows_b)]
            if m + 1 in phases[0] and m + 1 < count:
                terms.append((at, phases[0].index(m + 1), 0, rows_b))
            jobs.append((outs + 1 + len(order), 0, terms))
            shapes.append(pltpu.VMEM((rows_b, share), BF16))
            order.append(m)
    total, *kept = add(jobs, operands, shapes)
    return total, (came, dict(zip(order, kept)))


def scatter_last(begun, axis, count):
    came, kept = begun
    phases = hypercube(count)
    final = [(came, len(phases[0]) - 1)]
    for p, members in enumerate(phases):
        if p:
            got = exchange(jnp.stack([kept[m] for m in members]), axis, 1 << p, count)
            kept = folded(members, None, got, kept)
            final.append((got, len(members) - 1))
    return final


def scatter_direct(sent, axis, count):
    return [(exchange(x, axis, m, count), 0) for m, x in enumerate(sent, start=1)]


def on_device(groups, tiles, contrast, incident, signs, adjoint, proj, mats, offsets, expand):
    nbox = contrast.shape[0]
    half = nbox // 2
    cut, last = half + ROWS, nbox - ROWS
    third = half + (last - half) // ROWS // 2 * ROWS
    upward = [(i, i + 1) for i in range(tiles - 1)]
    downward = [(i + 1, i) for i in range(tiles - 1)]

    def started(x):
        return {0: x} | {
            m: exchange(x, "group", m, groups) for m in reversed(range(1, groups)) if not m & (m - 1)
        }

    contrast_a, contrast_b = split(contrast, [[(0, cut), (last, ROWS)], [(cut, last - cut)]])
    pieces_a = started(contrast_a)
    enc = encode(signs, incident)
    top, enc, contrast_b = lax.optimization_barrier((pieces_a[groups // 2], enc, contrast_b))
    pieces_a[groups // 2] = top
    adj, part = weigh(adjoint, enc, top)
    pieces_a = gather_pieces(pieces_a, "group", groups)
    pieces_b = [contrast_b] + [exchange(contrast_b, "group", m, groups) for m in range(1, groups)]

    common = dict(offsets=offsets, mats=mats, expand=expand, adj=adj, part=part)
    mine = [[(first, first, size)] for first, size in cut_up(0, cut, 2)]
    mine[-1].append((last, cut, ROWS))
    state, own_a, sent_a, edges = stage(
        "group", groups, mine, cut_up(ROWS, half - ROWS, 3), (0, last),
        hypercube(groups), common | dict(enc=enc, proj=proj, pieces=pieces_a), None, weight=0.0,
    )
    high = lax.ppermute(edges[0], "tile", downward)
    low = lax.ppermute(edges[1], "tile", upward)

    mine = [[(first, first - cut, size)] for first, size in cut_up(cut, last - cut, 2)]
    state, own_b, sent_b, _ = stage(
        "group", groups, mine, cut_up(half, third - half, 2), (),
        hypercube(groups), common | dict(enc=enc, proj=proj, pieces=pieces_b), state, weight=1.0,
    )
    got_a = scatter_steps(sent_a, "group", groups)
    state, own_c, sent_c, _ = stage(
        "group", groups, [], cut_up(third, nbox - third, 2) + [(0, ROWS)], (),
        [[m] for m in range(1, groups)], common | dict(low=low, high=high), state, weight=1.0,
    )
    share = own_a.shape[1]
    rows_a, rows_b, rows_c = half - ROWS, third - half, nbox - third
    done_a, sent_b = first_sums(own_a, got_a, sent_b, sent_c[0], "group", groups)
    got_b = scatter_last(sent_b, "group", groups)
    got_c = scatter_direct(sent_c, "group", groups)

    operands = [done_a, own_b] + [x for x, _ in got_b] + [own_c] + [x for x, _ in got_c]
    at_c = 2 + len(got_b)
    out = len(operands)
    pick_b = [(1, None)] + [(2 + i, slot) for i, (_, slot) in enumerate(got_b)]
    pick_c = [(at_c, None)] + [(at_c + 1 + i, slot) for i, (_, slot) in enumerate(got_c)]
    jobs = [
        (out, 0, [(ref, slot, rows_c, ROWS) for ref, slot in pick_c]),
        (out, ROWS, [(0, None, 0, rows_a)]),
        (out, half, [(ref, slot, 0, rows_b) for ref, slot in pick_b]),
        (out, third, [(ref, slot, 0, rows_c) for ref, slot in pick_c]),
    ]
    (gradient,) = add(jobs, operands, [jax.ShapeDtypeStruct((nbox, share), F32)])
    return state[1], gradient


def solution(mesh):
    in_specs = (
        P("tile", "group"),
        P("group", None, "tile", None),
        P("group", None, None),
        P("group", None, "tile", None),
        P(),
        P(),
        P(),
        P(),
    )
    out_specs = (P("group", None, "tile", None), P("tile", "group"))
    return jax.shard_map(
        functools.partial(on_device, mesh.shape["group"], mesh.shape["tile"]),
        mesh=mesh,
        in_specs=in_specs,
        out_specs=out_specs,
        check_vma=False,
    )
```

time: 188 us -> 60.2 us (0.32)
  waiting for transfers between devices: 65.5 us -> 7.86 us
  other arithmetic: 43.1 us -> 0.03 us
  matrix products: 40.6 us -> 0 us
  Pallas kernels: 0 us -> 25.4 us
  between operations: 21.6 us -> 0.77 us
  starting transfers between devices: 6.76 us -> 25.2 us
  local copies, waits for them, and re-layouts: 8.48 us -> 0.7 us
    dot_general x3 -> x0, matrix products: 40.6 us -> none  [the longest x1 15.3 us: on_device(): jnp.dot(local.reshape(-1, width), expand, preferred_element_type=jnp.floa...]
    reduce_scatter x1 -> x0, waiting for transfers between devices: 32.8 us -> none  [on_device(): gradient = lax.psum_scatter(terms, 'group', scatter_dimension=1, tiled=True)]
    all_gather x1 -> x0, waiting for transfers between devices: 32 us -> none  [on_device(): full_contrast = lax.all_gather(contrast, 'group', axis=1, tiled=True)]
    reduce_sum x1 -> x0, other arithmetic: 31.9 us -> none  [on_device(): terms = jnp.sum(adjoint_f * total, axis=0)]
    pallas_call x0 -> x8, Pallas kernels: none -> 25.4 us  [the longest x3 14.5 us: stage(): pl.pallas_call(functools.partial(stage_kernel, axis, count, mine, placed,...]
    ppermute x2 -> x15, starting transfers between devices: 6.68 us -> 25.2 us  [the longest x13 18.8 us: exchange(): return lax.ppermute(x, axis, [(i, i ^ m) for i in range(count)])]
    broadcast_in_dim x1 -> x0, other arithmetic: 9.21 us -> none  [on_device(): return (field.astype(jnp.bfloat16)[None], gradient)]
    ppermute x2 -> x15, waiting for transfers between devices: 0.01 us -> 7.86 us  [the longest x13 7.86 us: exchange(): return lax.ppermute(x, axis, [(i, i ^ m) for i in range(count)])]
  transfers between devices with their start and end apart: 4 -> 15, of which waited for: 2 -> 5; matrix products, arithmetic and copies ran while one was open for 5% -> 0% of each run, Pallas kernels for 0% -> 39%
where the time goes in v3:
time: 60.2 us; the launch traced here: 60 us
  Pallas kernels  25.4 us (42%)
  starting transfers between devices  25.2 us (42%)
  waiting for transfers between devices  7.86 us (13%)
  between operations  0.77 us (1%)
  local copies, waits for them, and re-layouts  0.7 us (1%)
    ppermute x13, starting transfers between devices, exchange(): return lax.ppermute(x, axis, [(i, i ^ m) for i in range(count)])  18.8 us
    pallas_call x3, Pallas kernels, stage(): pl.pallas_call(functools.partial(stage_kernel, axis, count, mine, placed,...  14.5 us
    ppermute x13, waiting for transfers between devices, exchange(): return lax.ppermute(x, axis, [(i, i ^ m) for i in range(count)])  7.86 us
    pallas_call x1, Pallas kernels, encode(): pl.pallas_call(functools.partial(encode_kernel, block, group), in_specs=[...  5.44 us
    ppermute x1, starting transfers between devices, on_device(): high = lax.ppermute(edges[0], 'tile', downward)  4.54 us
    pallas_call x1, Pallas kernels, weigh(): pl.pallas_call(functools.partial(weigh_kernel, block), in_specs=[HBM, VME...  3.59 us
    ppermute x1, starting transfers between devices, on_device(): low = lax.ppermute(edges[1], 'tile', upward)  1.92 us
  transfers between devices with their start and end apart: 15, of which 5 were waited for; matrix products, arithmetic and copies ran while one was open for 0% of the time, Pallas kernels for 39%

profile of v3, /device:TPU:4, one launch (start us, length us, event | category | flops | bytes accessed | tf_op | source)
XLA Modules:
  0.0 60.0 jit_solution(6175472119694444666)
XLA Ops:
  0.6 1.0 %split.1 = (bf16[288,256]{1,0:T(8,128)(2,1)S(1)}, bf16[224,256]{1,0:T(8,128)(2,1)S(1)}) custom-call(bf16[512,256]{1,0:T(8,128)(2,1)} %whole.1), custom_call_target="tpu_custom_call" | custom-call | tf_op jit(solution)/shard_map/split/pallas_call | solution.py:49
  1.6 1.6 %collective-permute-start.1 = (bf16[288,256]{1,0:T(8,128)(2,1)S(1)}, bf16[288,256]{1,0:T(8,128)(2,1)S(1)}, u32[]{:S(2)}, u32[]{:S(2)}) collective-permute-start(bf16[288,256]{1,0:T(8,128)(2,1)S(1)} %get-tuple-element.28.refs_7_), channel_id=1, source_target_pairs={{0,8},{8,0},{16,24},{24,16},{1,9},{9,1},{17,25},{25,17},{2,10},{10... | collective-permute-start | bytes 442376 | tf_op jit(solution)/shard_map/ppermute | solution.py:348
  3.3 2.6 %collective-permute-start = (bf16[288,256]{1,0:T(8,128)(2,1)S(1)}, bf16[288,256]{1,0:T(8,128)(2,1)S(1)}, u32[]{:S(2)}, u32[]{:S(2)}) collective-permute-start(bf16[288,256]{1,0:T(8,128)(2,1)S(1)} %get-tuple-element.28.refs_7_), channel_id=1, source_target_pairs={{0,16},{8,24},{16,0},{24,8},{1,17},{9,25},{17,1},{25,9},{2,18},{10... | collective-permute-start | bytes 442376 | tf_op jit(solution)/shard_map/ppermute | solution.py:348
  5.9 0.0 copy-start.4
  5.9 0.7 %copy-done.4 = s32[1,8,8]{2,1,0:T(8,128)S(1)} copy-done((s32[1,8,8]{2,1,0:T(8,128)S(1)}, s32[1,8,8]{2,1,0:T(8,128)}, u32[]{:S(2)}) %copy-start.4) | copy-done | bytes 280
  6.6 5.4 %encode.1.enc.refs_5_ = bf16[8,512,1024]{2,1,0:T(8,128)(2,1)S(1)} custom-call(s32[1,8,8]{2,1,0:T(8,128)S(1)} %copy-done.4, bf16[1,8,512,1024]{3,2,1,0:T(8,128)(2,1)} %inc.1), custom_call_target="tpu_custom_call" | custom-call | flops 2147483648 | bytes 8388608 | tf_op jit(solution)/shard_map/encode/pallas_call | solution.py:97
  12.0 0.7 %collective-permute-done._.refs_9_ = bf16[288,256]{1,0:T(8,128)(2,1)S(1)} collective-permute-done((bf16[288,256]{1,0:T(8,128)(2,1)S(1)}, bf16[288,256]{1,0:T(8,128)(2,1)S(1)}, u32[]{:S(2)}, u32[]{:S(2)}) %collective-permute-start) | collective-permute-done | bytes 147488 | tf_op jit(solution)/shard_map/ppermute | solution.py:348
  12.7 0.0 copy-start
  12.7 0.0 copy-start.1
  12.7 0.0 copy-start.2
  12.7 0.0 copy-start.3
  12.7 0.5 collective-permute-start.2
  13.2 2.1 %collective-permute-start.7 = (bf16[224,256]{1,0:T(8,128)(2,1)S(1)}, bf16[224,256]{1,0:T(8,128)(2,1)S(1)}, u32[]{:S(2)}, u32[]{:S(2)}) collective-permute-start(bf16[224,256]{1,0:T(8,128)(2,1)S(1)} %get-tuple-element.36.refs_7_), channel_id=1, source_target_pairs={{0,24},{8,16},{16,8},{24,0},{1,25},{9,17},{17,9},{25,1},{2,26},{10... | collective-permute-start | bytes 344072 | tf_op jit(solution)/shard_map/ppermute | solution.py:348
  15.3 0.9 %collective-permute-start.6 = (bf16[224,256]{1,0:T(8,128)(2,1)S(1)}, bf16[224,256]{1,0:T(8,128)(2,1)S(1)}, u32[]{:S(2)}, u32[]{:S(2)}) collective-permute-start(bf16[224,256]{1,0:T(8,128)(2,1)S(1)} %get-tuple-element.36.refs_7_), channel_id=1, source_target_pairs={{0,16},{8,24},{16,0},{24,8},{1,17},{9,25},{17,1},{25,9},{2,18},{10... | collective-permute-start | bytes 344072 | tf_op jit(solution)/shard_map/ppermute | solution.py:348
  16.3 1.3 %collective-permute-start.5 = (bf16[224,256]{1,0:T(8,128)(2,1)S(1)}, bf16[224,256]{1,0:T(8,128)(2,1)S(1)}, u32[]{:S(2)}, u32[]{:S(2)}) collective-permute-start(bf16[224,256]{1,0:T(8,128)(2,1)S(1)} %get-tuple-element.36.refs_7_), channel_id=1, source_target_pairs={{0,8},{8,0},{16,24},{24,16},{1,9},{9,1},{17,25},{25,17},{2,10},{10... | collective-permute-start | bytes 344072 | tf_op jit(solution)/shard_map/ppermute | solution.py:348
  17.6 3.6 %weigh.1 = (bf16[8,512,1024]{2,1,0:T(8,128)(2,1)S(1)}, f32[512,1024]{1,0:T(8,128)S(1)}) custom-call(bf16[1,8,512,1024]{3,2,1,0:T(8,128)(2,1)} %adj.1, bf16[8,512,1024]{2,1,0:T(8,128)(2,1)S(1)} %encode.1.enc.refs_5_, bf16[288,256]{1,0:T(8,128)(2,1)S(1)} %collective-permute-done._.refs_9_), custom_call_target="tpu_custom_call" | custom-call | flops 1 | bytes 1 | tf_op jit(solution)/shard_map/weigh/pallas_call | solution.py:139
  21.2 0.0 collective-permute-done.1.refs_8_
  21.2 1.5 %collective-permute-done.2.refs_10_ = bf16[288,256]{1,0:T(8,128)(2,1)S(1)} collective-permute-done((bf16[288,256]{1,0:T(8,128)(2,1)S(1)}, bf16[288,256]{1,0:T(8,128)(2,1)S(1)}, u32[]{:S(2)}, u32[]{:S(2)}) %collective-permute-start.2) | collective-permute-done | bytes 147488 | tf_op jit(solution)/shard_map/ppermute | solution.py:348
  22.8 0.0 copy-done
  22.8 0.0 copy-done.1
  22.8 0.0 copy-done.2
  22.8 0.0 copy-done.3
  22.8 6.3 %stage.3 = (f32[2,8,544,128]{3,2,1,0:T(8,128)S(1)}, bf16[1,8,512,1024]{3,2,1,0:T(8,128)(2,1)}, f32[240,256]{1,0:T(8,128)S(1)}, bf16[2,240,256]{2,1,0:T(8,128)(2,...) custom-call(s32[6]{0:T(128)S(1)} %copy-done.3, ...), custom_call_target="tpu_custom_call" | custom-call | tf_op jit(solution)/shard_map/stage/pallas_call | solution.py:314
  29.1 0.1 collective-permute-start.8
  29.2 1.9 %collective-permute-start.3 = (bf16[8,16,256]{2,1,0:T(8,128)(2,1)S(1)}, bf16[8,16,256]{2,1,0:T(8,128)(2,1)S(1)}, u32[]{:S(2)}, u32[]{:S(2)}) collective-permute-start(bf16[8,16,256]{2,1,0:T(8,128)(2,1)S(1)} %get-tuple-element.34), channel_id=1, source_target_pairs={{0,1},{1,2},{2,3},{3,4},{4,5},{5,6},{6,7},{8,9},{9,10},{10,11},{11... | collective-permute-start | bytes 196616 | tf_op jit(solution)/shard_map/ppermute | solution.py:451
  31.1 0.0 collective-permute-done.7.refs_10_
  31.1 4.5 %collective-permute-start.4 = (bf16[8,16,256]{2,1,0:T(8,128)(2,1)S(1)}, bf16[8,16,256]{2,1,0:T(8,128)(2,1)S(1)}, u32[]{:S(2)}, u32[]{:S(2)}) collective-permute-start(bf16[8,16,256]{2,1,0:T(8,128)(2,1)S(1)} %get-tuple-element.35), channel_id=1, source_target_pairs={{1,0},{2,1},{3,2},{4,3},{5,4},{6,5},{7,6},{9,8},{10,9},{11,10},{12... | collective-permute-start | bytes 196616 | tf_op jit(solution)/shard_map/ppermute | solution.py:450
  35.6 0.0 collective-permute-done.6.refs_9_
  35.7 0.0 collective-permute-done.5.refs_8_
  35.7 4.4 %stage.4 = (f32[2,8,544,128]{3,2,1,0:T(8,128)S(1)}, bf16[1,8,512,1024]{3,2,1,0:T(8,128)(2,1)}, f32[112,256]{1,0:T(8,128)S(1)}, bf16[2,112,256]{2,1,0:T(8,128)(2,1)S(1)}, bf16[1,112,256]{2,1,0:T(8,128)(2,1)S(1)}) custom-call(s32[6]{0:T(128)S(1)} %copy-done.3, bf16[6,256,256]{2,1,0:T(8,128)(2,1)S(1)} %copy-done, ...), custom_call_target="tpu_custom_call", output_to_operand_aliasing={{0}: (11, {}), {1}: (12, {})} | custom-call | flops 2113929216 | bytes 1835008 | tf_op jit(solution)/shard_map/stage/pallas_call | solution.py:314
  40.1 2.1 %collective-permute-start.10 = (bf16[2,112,256]{2,1,0:T(8,128)(2,1)S(1)}, bf16[2,112,256]{2,1,0:T(8,128)(2,1)S(1)}, u32[]{:S(2)}, u32[]{:S(2)}) collective-permute-start(bf16[2,112,256]{2,1,0:T(8,128)(2,1)S(1)} %get-tuple-element.45), channel_id=1, source_target_pairs={{0,8},{8,0},{16,24},{24,16},{1,9},{9,1},{17,25},{25,17},{2,10},{10... | collective-permute-start | bytes 344072 | tf_op jit(solution)/shard_map/ppermute | solution.py:348
  42.1 0.0 collective-permute-done.8.refs_1_
  42.2 1.0 %collective-permute-start.9 = (bf16[1,240,256]{2,1,0:T(8,128)(2,1)S(1)}, bf16[1,240,256]{2,1,0:T(8,128)(2,1)S(1)}, u32[]{:S(2)}, u32[]{:S(2)}) collective-permute-start(bf16[1,240,256]{2,1,0:T(8,128)(2,1)S(1)} %add_convert_fusion), channel_id=1, source_target_pairs={{0,16},{8,24},{16,0},{24,8},{1,17},{9,25},{17,1},{25,9},{2,18},{10... | collective-permute-start | bytes 368648 | tf_op jit(solution)/shard_map/ppermute | solution.py:348
  43.2 0.0 collective-permute-done.3.refs_5_
  43.2 0.0 collective-permute-done.4.refs_6_
  43.2 3.8 %stage.5 = (f32[2,8,544,128]{3,2,1,0:T(8,128)S(1)}, bf16[1,8,512,1024]{3,2,1,0:T(8,128)(2,1)}, f32[160,256]{1,0:T(8,128)S(1)}, bf16[1,160,256]{2,1,0:T(8,128)(2,...) custom-call(s32[6]{0:T(128)S(1)} %copy-done.3, ...), custom_call_target="tpu_custom_call", output_to_operand_aliasing={{0}: (7, {}), {1}: (8, {})} | custom-call | flops 1677721600 | bytes 2621440 | tf_op jit(solution)/shard_map/stage/pallas_call | solution.py:314
  47.0 2.1 %collective-permute-start.13 = (bf16[1,160,256]{2,1,0:T(8,128)(2,1)S(1)}, bf16[1,160,256]{2,1,0:T(8,128)(2,1)S(1)}, u32[]{:S(2)}, u32[]{:S(2)}) collective-permute-start(bf16[1,160,256]{2,1,0:T(8,128)(2,1)S(1)} %get-tuple-element.52), channel_id=1, source_target_pairs={{0,16},{8,24},{16,0},{24,8},{1,17},{9,25},{17,1},{25,9},{2,18},{10... | collective-permute-start | bytes 245768 | tf_op jit(solution)/shard_map/ppermute | solution.py:348
  49.0 2.4 %collective-permute-start.14 = (bf16[1,160,256]{2,1,0:T(8,128)(2,1)S(1)}, bf16[1,160,256]{2,1,0:T(8,128)(2,1)S(1)}, u32[]{:S(2)}, u32[]{:S(2)}) collective-permute-start(bf16[1,160,256]{2,1,0:T(8,128)(2,1)S(1)} %get-tuple-element.53), channel_id=1, source_target_pairs={{0,24},{8,16},{16,8},{24,0},{1,25},{9,17},{17,9},{25,1},{2,26},{10... | collective-permute-start | bytes 245768 | tf_op jit(solution)/shard_map/ppermute | solution.py:348
  51.4 0.0 collective-permute-start.12
  51.4 0.0 collective-permute-done.10.refs_3_.refs_2_
  51.4 0.0 collective-permute-done.9.refs_2_
  51.4 0.1 add.8
  51.5 2.1 %collective-permute-start.11 = (bf16[1,112,256]{2,1,0:T(8,128)(2,1)S(1)}, bf16[1,112,256]{2,1,0:T(8,128)(2,1)S(1)}, u32[]{:S(2)}, u32[]{:S(2)}) collective-permute-start(bf16[1,112,256]{2,1,0:T(8,128)(2,1)S(1)} %bitcast.1), channel_id=1, source_target_pairs={{0,16},{8,24},{16,0},{24,8},{1,17},{9,25},{17,1},{25,9},{2,18},{10... | collective-permute-start | bytes 172040 | tf_op jit(solution)/shard_map/ppermute | solution.py:348
  53.6 3.0 %collective-permute-done.13.refs_6_ = bf16[1,160,256]{2,1,0:T(8,128)(2,1)S(1)} collective-permute-done((bf16[1,160,256]{2,1,0:T(8,128)(2,1)S(1)}, bf16[1,160,256]{2,1,0:T(8,128)(2,1)S(1)}, u32[]{:S(2)}, u32[]{:S(2)}) %collective-permute-start.13) | collective-permute-done | bytes 81952 | tf_op jit(solution)/shard_map/ppermute | solution.py:348
  56.6 0.0 collective-permute-done.14.refs_7_
  56.6 0.8 %collective-permute-done.12.refs_5_ = bf16[1,160,256]{2,1,0:T(8,128)(2,1)S(1)} collective-permute-done((bf16[1,160,256]{2,1,0:T(8,128)(2,1)S(1)}, bf16[1,160,256]{2,1,0:T(8,128)(2,1)S(1)}, u32[]{:S(2)}, u32[]{:S(2)}) %collective-permute-start.12) | collective-permute-done | bytes 81952 | tf_op jit(solution)/shard_map/ppermute | solution.py:348
  57.4 1.8 %collective-permute-done.11.refs_3_ = bf16[1,112,256]{2,1,0:T(8,128)(2,1)S(1)} collective-permute-done((bf16[1,112,256]{2,1,0:T(8,128)(2,1)S(1)}, bf16[1,112,256]{2,1,0:T(8,128)(2,1)S(1)}, u32[]{:S(2)}, u32[]{:S(2)}) %collective-permute-start.11) | collective-permute-done | bytes 57376 | tf_op jit(solution)/shard_map/ppermute | solution.py:348
  59.2 0.9 %add.9 = f32[512,256]{1,0:T(8,128)} custom-call(f32[240,256]{1,0:T(8,128)S(1)} %get-tuple-element.48.refs_0_, f32[112,256]{1,0:T(8,128)S(1)} %get-tuple-element.49.refs_1_, bf16[2,112,256]{2,1,0:T(8,128)(2,1)S(1)} %collective-permute-done.10.refs_3_.refs_2_, bf16[1,112,256]{2,1,0:T(8,128)(2,1)S(1)} %collective-permute-done.11.refs_3_, ...), custom_call_target="tpu_custom_call" | custom-call | tf_op jit(solution)/shard_map/add/pallas_call | solution.py:165
  (1 shorter events, 0.0 us)
Async XLA Ops:
  1.6 19.6 %collective-permute-start.1 = (bf16[288,256]{1,0:T(8,128)(2,1)S(1)}, bf16[288,256]{1,0:T(8,128)(2,1)S(1)}, u32[]{:S(2)}, u32[]{:S(2)}) collective-permute-start(bf16[288,256]{1,0:T(8,128)(2,1)S(1)} %get-tuple-element.28.refs_7_), channel_id=1, source_target_pairs={{0,8},{8,0},{16,24},{24,16},{1,9},{9,1},{17,25},{25,17},{2,10},{10... | collective-permute-start | bytes 442376 | tf_op jit(solution)/shard_map/ppermute | solution.py:348
  3.3 9.4 %collective-permute-start = (bf16[288,256]{1,0:T(8,128)(2,1)S(1)}, bf16[288,256]{1,0:T(8,128)(2,1)S(1)}, u32[]{:S(2)}, u32[]{:S(2)}) collective-permute-start(bf16[288,256]{1,0:T(8,128)(2,1)S(1)} %get-tuple-element.28.refs_7_), channel_id=1, source_target_pairs={{0,16},{8,24},{16,0},{24,8},{1,17},{9,25},{17,1},{25,9},{2,18},{10... | collective-permute-start | bytes 442376 | tf_op jit(solution)/shard_map/ppermute | solution.py:348
  5.9 0.7 %copy-start.4 = (s32[1,8,8]{2,1,0:T(8,128)S(1)}, s32[1,8,8]{2,1,0:T(8,128)}, u32[]{:S(2)}) copy-start(s32[1,8,8]{2,1,0:T(8,128)} %signs.1) | copy-start | bytes 772
  12.7 10.1 %copy-start = (bf16[6,256,256]{2,1,0:T(8,128)(2,1)S(1)}, bf16[6,256,256]{2,1,0:T(8,128)(2,1)}, u32[]{:S(2)}) copy-start(bf16[6,256,256]{2,1,0:T(8,128)(2,1)} %refs_1_.5) | copy-start | bytes 2359300
  12.7 10.1 %copy-start.1 = (bf16[256,1024]{1,0:T(8,128)(2,1)S(1)}, bf16[256,1024]{1,0:T(8,128)(2,1)}, u32[]{:S(2)}) copy-start(bf16[256,1024]{1,0:T(8,128)(2,1)} %refs_2_.5) | copy-start | bytes 1572868
  12.7 10.1 %copy-start.2 = (bf16[1024,256]{1,0:T(8,128)(2,1)S(1)}, bf16[1024,256]{1,0:T(8,128)(2,1)}, u32[]{:S(2)}) copy-start(bf16[1024,256]{1,0:T(8,128)(2,1)} %refs_6_.3) | copy-start | bytes 1572868
  12.7 10.1 %copy-start.3 = (s32[6]{0:T(128)S(1)}, s32[6]{0:T(128)}, u32[]{:S(2)}) copy-start(s32[6]{0:T(128)} %refs_0_.5) | copy-start | bytes 76
  12.7 10.0 %collective-permute-start.2 = (bf16[288,256]{1,0:T(8,128)(2,1)S(1)}, bf16[288,256]{1,0:T(8,128)(2,1)S(1)}, u32[]{:S(2)}, u32[]{:S(2)}) collective-permute-start(bf16[288,256]{1,0:T(8,128)(2,1)S(1)} %collective-permute-done._.refs_9_), channel_id=1, source_target_pairs={{0,8},{8,0},{16,24},{24,16},{1,9},{9,1},{17,25},{25,17},{2,10},{10... | collective-permute-start | bytes 442376 | tf_op jit(solution)/shard_map/ppermute | solution.py:348
  13.2 17.9 %collective-permute-start.7 = (bf16[224,256]{1,0:T(8,128)(2,1)S(1)}, bf16[224,256]{1,0:T(8,128)(2,1)S(1)}, u32[]{:S(2)}, u32[]{:S(2)}) collective-permute-start(bf16[224,256]{1,0:T(8,128)(2,1)S(1)} %get-tuple-element.36.refs_7_), channel_id=1, source_target_pairs={{0,24},{8,16},{16,8},{24,0},{1,25},{9,17},{17,9},{25,1},{2,26},{10... | collective-permute-start | bytes 344072 | tf_op jit(solution)/shard_map/ppermute | solution.py:348
  15.3 20.3 %collective-permute-start.6 = (bf16[224,256]{1,0:T(8,128)(2,1)S(1)}, bf16[224,256]{1,0:T(8,128)(2,1)S(1)}, u32[]{:S(2)}, u32[]{:S(2)}) collective-permute-start(bf16[224,256]{1,0:T(8,128)(2,1)S(1)} %get-tuple-element.36.refs_7_), channel_id=1, source_target_pairs={{0,16},{8,24},{16,0},{24,8},{1,17},{9,25},{17,1},{25,9},{2,18},{10... | collective-permute-start | bytes 344072 | tf_op jit(solution)/shard_map/ppermute | solution.py:348
  16.3 19.4 %collective-permute-start.5 = (bf16[224,256]{1,0:T(8,128)(2,1)S(1)}, bf16[224,256]{1,0:T(8,128)(2,1)S(1)}, u32[]{:S(2)}, u32[]{:S(2)}) collective-permute-start(bf16[224,256]{1,0:T(8,128)(2,1)S(1)} %get-tuple-element.36.refs_7_), channel_id=1, source_target_pairs={{0,8},{8,0},{16,24},{24,16},{1,9},{9,1},{17,25},{25,17},{2,10},{10... | collective-permute-start | bytes 344072 | tf_op jit(solution)/shard_map/ppermute | solution.py:348
  29.1 13.0 %collective-permute-start.8 = (bf16[2,240,256]{2,1,0:T(8,128)(2,1)S(1)}, bf16[2,240,256]{2,1,0:T(8,128)(2,1)S(1)}, u32[]{:S(2)}, u32[]{:S(2)}) collective-permute-start(bf16[2,240,256]{2,1,0:T(8,128)(2,1)S(1)} %get-tuple-element.43), channel_id=1, source_target_pairs={{0,8},{8,0},{16,24},{24,16},{1,9},{9,1},{17,25},{25,17},{2,10},{10... | collective-permute-start | bytes 737288 | tf_op jit(solution)/shard_map/ppermute | solution.py:348
  29.2 14.0 %collective-permute-start.3 = (bf16[8,16,256]{2,1,0:T(8,128)(2,1)S(1)}, bf16[8,16,256]{2,1,0:T(8,128)(2,1)S(1)}, u32[]{:S(2)}, u32[]{:S(2)}) collective-permute-start(bf16[8,16,256]{2,1,0:T(8,128)(2,1)S(1)} %get-tuple-element.34), channel_id=1, source_target_pairs={{0,1},{1,2},{2,3},{3,4},{4,5},{5,6},{6,7},{8,9},{9,10},{10,11},{11... | collective-permute-start | bytes 196616 | tf_op jit(solution)/shard_map/ppermute | solution.py:451
  31.1 12.1 %collective-permute-start.4 = (bf16[8,16,256]{2,1,0:T(8,128)(2,1)S(1)}, bf16[8,16,256]{2,1,0:T(8,128)(2,1)S(1)}, u32[]{:S(2)}, u32[]{:S(2)}) collective-permute-start(bf16[8,16,256]{2,1,0:T(8,128)(2,1)S(1)} %get-tuple-element.35), channel_id=1, source_target_pairs={{1,0},{2,1},{3,2},{4,3},{5,4},{6,5},{7,6},{9,8},{10,9},{11,10},{12... | collective-permute-start | bytes 196616 | tf_op jit(solution)/shard_map/ppermute | solution.py:450
  40.1 11.3 %collective-permute-start.10 = (bf16[2,112,256]{2,1,0:T(8,128)(2,1)S(1)}, bf16[2,112,256]{2,1,0:T(8,128)(2,1)S(1)}, u32[]{:S(2)}, u32[]{:S(2)}) collective-permute-start(bf16[2,112,256]{2,1,0:T(8,128)(2,1)S(1)} %get-tuple-element.45), channel_id=1, source_target_pairs={{0,8},{8,0},{16,24},{24,16},{1,9},{9,1},{17,25},{25,17},{2,10},{10... | collective-permute-start | bytes 344072 | tf_op jit(solution)/shard_map/ppermute | solution.py:348
  42.2 9.2 %collective-permute-start.9 = (bf16[1,240,256]{2,1,0:T(8,128)(2,1)S(1)}, bf16[1,240,256]{2,1,0:T(8,128)(2,1)S(1)}, u32[]{:S(2)}, u32[]{:S(2)}) collective-permute-start(bf16[1,240,256]{2,1,0:T(8,128)(2,1)S(1)} %add_convert_fusion), channel_id=1, source_target_pairs={{0,16},{8,24},{16,0},{24,8},{1,17},{9,25},{17,1},{25,9},{2,18},{10... | collective-permute-start | bytes 368648 | tf_op jit(solution)/shard_map/ppermute | solution.py:348
  47.0 9.6 %collective-permute-start.13 = (bf16[1,160,256]{2,1,0:T(8,128)(2,1)S(1)}, bf16[1,160,256]{2,1,0:T(8,128)(2,1)S(1)}, u32[]{:S(2)}, u32[]{:S(2)}) collective-permute-start(bf16[1,160,256]{2,1,0:T(8,128)(2,1)S(1)} %get-tuple-element.52), channel_id=1, source_target_pairs={{0,16},{8,24},{16,0},{24,8},{1,17},{9,25},{17,1},{25,9},{2,18},{10... | collective-permute-start | bytes 245768 | tf_op jit(solution)/shard_map/ppermute | solution.py:348
  49.0 7.6 %collective-permute-start.14 = (bf16[1,160,256]{2,1,0:T(8,128)(2,1)S(1)}, bf16[1,160,256]{2,1,0:T(8,128)(2,1)S(1)}, u32[]{:S(2)}, u32[]{:S(2)}) collective-permute-start(bf16[1,160,256]{2,1,0:T(8,128)(2,1)S(1)} %get-tuple-element.53), channel_id=1, source_target_pairs={{0,24},{8,16},{16,8},{24,0},{1,25},{9,17},{17,9},{25,1},{2,26},{10... | collective-permute-start | bytes 245768 | tf_op jit(solution)/shard_map/ppermute | solution.py:348
  51.4 6.0 %collective-permute-start.12 = (bf16[1,160,256]{2,1,0:T(8,128)(2,1)S(1)}, bf16[1,160,256]{2,1,0:T(8,128)(2,1)S(1)}, u32[]{:S(2)}, u32[]{:S(2)}) collective-permute-start(bf16[1,160,256]{2,1,0:T(8,128)(2,1)S(1)} %get-tuple-element.47.refs_5_), channel_id=1, source_target_pairs={{0,8},{8,0},{16,24},{24,16},{1,9},{9,1},{17,25},{25,17},{2,10},{10... | collective-permute-start | bytes 245768 | tf_op jit(solution)/shard_map/ppermute | solution.py:348
  51.5 7.7 %collective-permute-start.11 = (bf16[1,112,256]{2,1,0:T(8,128)(2,1)S(1)}, bf16[1,112,256]{2,1,0:T(8,128)(2,1)S(1)}, u32[]{:S(2)}, u32[]{:S(2)}) collective-permute-start(bf16[1,112,256]{2,1,0:T(8,128)(2,1)S(1)} %bitcast.1), channel_id=1, source_target_pairs={{0,16},{8,24},{16,0},{24,8},{1,17},{9,25},{17,1},{25,9},{2,18},{10... | collective-permute-start | bytes 172040 | tf_op jit(solution)/shard_map/ppermute | solution.py:348

commit v4 on v3

--- a/solution.py
+++ b/solution.py
@@ -52,22 +52,31 @@
         out_specs=[VMEM] * len(parts),
         out_shape=shapes,
         scratch_shapes=[pltpu.SemaphoreType.DMA((len(runs),))],
+        compiler_params=pltpu.CompilerParams(vmem_limit_bytes=4 * 2**20),
         name="split",
     )(far(x))
 
 
-def encode_kernel(block, group, signs, inc, enc, incv, mix, sems):
+def encode_kernel(block, group, weighed, signs_in, inc, adj, enc, adjv, part, signs, incv, mix, sems):
     count, nbox, points = incv.shape
     outs = enc.shape[0]
     size = count * group
     steps = nbox // block
 
-    def copy(i):
+    def copies(i):
         rows = pl.ds(pl.multiple_of(i * block, ROWS), block)
-        return pltpu.make_async_copy(inc.at[0, :, rows, :], incv.at[:, rows, :], sems.at[i])
-
+        inc_copy = pltpu.make_async_copy(inc.at[0, :, rows, :], incv.at[:, rows, :], sems.at[0, i])
+        adj_copy = pltpu.make_async_copy(adj.at[0, :, rows, :], adjv.at[:, rows, :], sems.at[1, i])
+        return inc_copy, adj_copy
+
+    signs_copy = pltpu.make_async_copy(signs_in, signs, sems.at[0, steps])
+    signs_copy.start()
     for i in range(steps):
-        copy(i).start()
+        inc_copy, adj_copy = copies(i)
+        inc_copy.start()
+        if i < weighed:
+            adj_copy.start()
+    signs_copy.wait()
 
     r = lax.broadcasted_iota(jnp.int32, (group, size), 0)
     c = lax.broadcasted_iota(jnp.int32, (group, size), 1)
@@ -78,31 +87,43 @@
             value = jnp.where(c // group == s, signs[0, e, s].astype(F32), value)
         mix[e * group:(e + 1) * group, :] = jnp.where(diagonal, value, 0.0).astype(BF16)
 
-    def step(i, carry):
-        copy(i).wait()
+    def step(i, carry, weigh):
+        inc_copy, adj_copy = copies(i)
+        inc_copy.wait()
+        if weigh:
+            adj_copy.wait()
         for j in range(block // group):
             rows = pl.ds(pl.multiple_of(i * block + j * group, ROWS), group)
             x = incv[:, rows, :].reshape(size, points)
             encoded = jnp.dot(mix[...], x, preferred_element_type=F32).astype(BF16)
-            enc[:, rows, :] = encoded.reshape(outs, group, points)
+            encoded = encoded.reshape(outs, group, points)
+            enc[:, rows, :] = encoded
+            if weigh:
+                part[rows, :] = jnp.sum(adjv[:, rows, :].astype(F32) * encoded.astype(F32), axis=0)
         return carry
 
-    lax.fori_loop(0, steps, step, 0)
-
-
-def encode(signs, incident, block=64):
+    lax.fori_loop(0, weighed, functools.partial(step, weigh=True), 0)
+    lax.fori_loop(weighed, steps, functools.partial(step, weigh=False), 0)
+
+
+def encode(signs, incident, adjoint, weighed, block=64):
     _, count, nbox, points = incident.shape
-    outs = signs.shape[1]
+    outs = adjoint.shape[1]
     group = 256 // count
     return pl.pallas_call(
-        functools.partial(encode_kernel, block, group),
-        in_specs=[SMEM, HBM],
-        out_specs=VMEM,
-        out_shape=pltpu.VMEM((outs, nbox, points), BF16),
+        functools.partial(encode_kernel, block, group, weighed // block),
+        in_specs=[HBM, HBM, HBM],
+        out_specs=[VMEM] * 3,
+        out_shape=[
+            pltpu.VMEM((outs, nbox, points), BF16),
+            pltpu.VMEM((outs, nbox, points), BF16),
+            pltpu.VMEM((nbox, points), F32),
+        ],
         scratch_shapes=[
+            pltpu.SMEM(signs.shape, signs.dtype),
             pltpu.VMEM((count, nbox, points), BF16),
             pltpu.VMEM((outs * group, count * group), BF16),
-            pltpu.SemaphoreType.DMA((nbox // block,)),
+            pltpu.SemaphoreType.DMA((2, nbox // block + 1)),
         ],
         compiler_params=pltpu.CompilerParams(vmem_limit_bytes=12 * 2**20),
         cost_estimate=pl.CostEstimate(
@@ -111,10 +132,10 @@
             transcendentals=0,
         ),
         name="encode",
-    )(signs, far(incident))
-
-
-def weigh_kernel(block, adj, enc, _, adjv, part, sems):
+    )(far(signs), far(incident), far(adjoint))
+
+
+def weigh_kernel(block, first, adj, enc, _, adj_in, part_in, adjv, part, sems):
     nbox = enc.shape[1]
     steps = nbox // block
 
@@ -122,7 +143,7 @@
         rows = pl.ds(pl.multiple_of(i * block, ROWS), block)
         return pltpu.make_async_copy(adj.at[0, :, rows, :], adjv.at[:, rows, :], sems.at[i])
 
-    for i in range(steps):
+    for i in range(first, steps):
         copy(i).start()
 
     def step(i, carry):
@@ -131,23 +152,22 @@
         part[rows, :] = jnp.sum(adjv[:, rows, :].astype(F32) * enc[:, rows, :].astype(F32), axis=0)
         return carry
 
-    lax.fori_loop(0, steps, step, 0)
-
-
-def weigh(adjoint, enc, after, block=64):
+    lax.fori_loop(first, steps, step, 0)
+
+
+def weigh(adjoint, enc, adj, part, weighed, after, block=32):
     outs, nbox, points = enc.shape
     return pl.pallas_call(
-        functools.partial(weigh_kernel, block),
-        in_specs=[HBM, VMEM, VMEM],
+        functools.partial(weigh_kernel, block, weighed // block),
+        in_specs=[HBM] + [VMEM] * 4,
         out_specs=[VMEM, VMEM],
         out_shape=[pltpu.VMEM((outs, nbox, points), BF16), pltpu.VMEM((nbox, points), F32)],
+        input_output_aliases={3: 0, 4: 1},
         scratch_shapes=[pltpu.SemaphoreType.DMA((nbox // block,))],
         compiler_params=pltpu.CompilerParams(vmem_limit_bytes=8 * 2**20),
-        cost_estimate=pl.CostEstimate(
-            flops=1, bytes_accessed=1, transcendentals=0
-        ),
+        cost_estimate=pl.CostEstimate(flops=1, bytes_accessed=1, transcendentals=0),
         name="weigh",
-    )(far(adjoint), near(enc), near(after))
+    )(far(adjoint), near(enc), near(after), near(adj), near(part))
 
 
 def add_kernel(jobs, *refs):
@@ -167,8 +187,21 @@
         in_specs=[VMEM] * len(operands),
         out_specs=[VMEM] * len(shapes),
         out_shape=shapes,
+        compiler_params=pltpu.CompilerParams(vmem_limit_bytes=4 * 2**20),
         name="add",
     )(*map(near, operands))
+
+
+def leaving(ready, scattered, segments, sems):
+    copies, row = [], 0
+    for i, (first, size) in enumerate(segments):
+        copies.append(
+            pltpu.make_async_copy(
+                ready.at[:, row:row + size, :], scattered.at[0, :, first:first + size, :], sems.at[i]
+            )
+        )
+        row += size
+    return copies
 
 
 def stage_kernel(axis, count, mine, blocks, edges_at, phases, layout, *refs):
@@ -178,8 +211,8 @@
         at += 1 if number is None else number
     offsets, mats, expand = named["offsets"], named["mats"], named["expand"]
     adj, part = named["adj"], named["part"]
-    padded, scattered = named["padded"], named["scattered"]
-    ready, held, terms, sems = refs[at:]
+    padded, ready = named["padded"], named["ready"]
+    held, terms = refs[at:]
     outs, nbox, points = adj.shape
     operators, depth, width = mats.shape
     share = points // count
@@ -239,12 +272,6 @@
             preferred_element_type=F32,
         ).astype(BF16)
 
-    def copy(i):
-        first, size, row = blocks[i]
-        return pltpu.make_async_copy(
-            ready.at[:, row:row + size, :], scattered.at[0, :, first:first + size, :], sems.at[i]
-        )
-
     def finish(i, local):
         first, size, row = blocks[i]
         field = jnp.dot(local, expand[...], preferred_element_type=F32)
@@ -268,9 +295,6 @@
         finish(i, held[i % 2, 0:rows_of[i], :])
         if i + 1 < len(blocks):
             held[(i + 1) % 2, 0:rows_of[i + 1], :] = following
-        copy(i).start()
-    for i in range(len(blocks)):
-        copy(i).wait()
 
 
 def stage(axis, count, mine, blocks, edges_at, phases, inputs, state, weight=1.0):
@@ -293,19 +317,19 @@
             specs.append(SMEM if name == "offsets" else VMEM)
     aliases = {}
     if state is not None:
-        layout += [("padded_in", None), ("scattered_in", None)]
-        aliases = {len(operands): 0, len(operands) + 1: 1}
-        operands += [near(state[0]), state[1]]
-        specs += [VMEM, ANY]
-
-    layout += [("padded", None), ("scattered", None), ("own", None), ("sent", len(phases))]
+        layout.append(("padded_in", None))
+        aliases = {len(operands): 0}
+        operands.append(near(state))
+        specs.append(VMEM)
+
+    layout += [("padded", None), ("ready", None), ("own", None), ("sent", len(phases))]
     out_shape = [
         pltpu.VMEM((width // lanes, outs, nbox + 2 * ROWS, lanes), F32),
-        jax.ShapeDtypeStruct((1, outs, nbox, points), BF16),
+        pltpu.VMEM((outs, rows, points), BF16),
         pltpu.VMEM((rows, share), F32),
     ]
     out_shape += [pltpu.VMEM((len(members), rows, share), BF16) for members in phases]
-    out_specs = [VMEM, ANY, VMEM] + [VMEM] * len(phases)
+    out_specs = [VMEM] * 3 + [VMEM] * len(phases)
     if edges_at:
         layout.append(("edges", len(edges_at)))
         out_shape += [pltpu.VMEM((outs, ROWS, width), BF16)] * len(edges_at)
@@ -318,10 +342,8 @@
         out_shape=out_shape,
         input_output_aliases=aliases,
         scratch_shapes=[
-            pltpu.VMEM((outs, rows, points), BF16),
             pltpu.VMEM((2, outs * most, width), BF16),
             pltpu.VMEM((most, points), F32),
-            pltpu.SemaphoreType.DMA((len(blocks),)),
         ],
         compiler_params=pltpu.CompilerParams(vmem_limit_bytes=16 * 2**20),
         cost_estimate=pl.CostEstimate(
@@ -334,8 +356,44 @@
         ),
         name="stage",
     )(*operands)
-    state, own, sent = result[:2], result[2], result[3:3 + len(phases)]
-    return state, own, sent, result[3 + len(phases):]
+    padded, ready, own = result[:3]
+    return padded, (ready, joined(blocks)), own, result[3:3 + len(phases)], result[3 + len(phases):]
+
+
+def joined(blocks):
+    segments = []
+    for first, size in blocks:
+        if segments and sum(segments[-1]) == first:
+            segments[-1] = (segments[-1][0], segments[-1][1] + size)
+        else:
+            segments.append((first, size))
+    return segments
+
+
+def flush_kernel(segments, *refs):
+    scattered, sems = refs[-2:]
+    copies = []
+    for ready, held in zip(refs, segments):
+        copies += leaving(ready, scattered, held, sems.at[pl.ds(len(copies), len(held))])
+    for copy in copies:
+        copy.start()
+    for copy in copies:
+        copy.wait()
+
+
+def flush(fields, nbox, after):
+    outs, _, points = fields[0][0].shape
+    segments = [held for _, held in fields]
+    return pl.pallas_call(
+        functools.partial(flush_kernel, segments),
+        in_specs=[VMEM] * (len(fields) + 1),
+        out_specs=HBM,
+        out_shape=jax.ShapeDtypeStruct((1, outs, nbox, points), BF16),
+        scratch_shapes=[pltpu.SemaphoreType.DMA((sum(map(len, segments)),))],
+        compiler_params=pltpu.CompilerParams(vmem_limit_bytes=4 * 2**20),
+        cost_estimate=pl.CostEstimate(flops=1, bytes_accessed=1, transcendentals=0),
+        name="flush",
+    )(*[near(ready) for ready, _ in fields], near(after))
 
 
 def cut_up(first, extent, parts):
@@ -420,30 +478,28 @@
 
 def on_device(groups, tiles, contrast, incident, signs, adjoint, proj, mats, offsets, expand):
     nbox = contrast.shape[0]
-    half = nbox // 2
+    half = nbox // 32 * 15
     cut, last = half + ROWS, nbox - ROWS
-    third = half + (last - half) // ROWS // 2 * ROWS
+    third = nbox // 32 * 23
     upward = [(i, i + 1) for i in range(tiles - 1)]
     downward = [(i + 1, i) for i in range(tiles - 1)]
 
-    def started(x):
-        return {0: x} | {
-            m: exchange(x, "group", m, groups) for m in reversed(range(1, groups)) if not m & (m - 1)
-        }
-
     contrast_a, contrast_b = split(contrast, [[(0, cut), (last, ROWS)], [(cut, last - cut)]])
-    pieces_a = started(contrast_a)
-    enc = encode(signs, incident)
-    top, enc, contrast_b = lax.optimization_barrier((pieces_a[groups // 2], enc, contrast_b))
-    pieces_a[groups // 2] = top
-    adj, part = weigh(adjoint, enc, top)
-    pieces_a = gather_pieces(pieces_a, "group", groups)
+    far_side = groups // 2
+    first = exchange(contrast_a, "group", 1, groups)
+    top = exchange(contrast_a, "group", far_side, groups)
+    weighed = nbox // 2
+    enc, adj, part = encode(signs, incident, adjoint, weighed)
+    top, first, enc = lax.optimization_barrier((top, first, enc))
+    pieces_a = gather_pieces({0: contrast_a, 1: first, far_side: top}, "group", groups)
+    adj, part = weigh(adjoint, enc, adj, part, weighed, top)
+    part, contrast_b = lax.optimization_barrier((part, contrast_b))
     pieces_b = [contrast_b] + [exchange(contrast_b, "group", m, groups) for m in range(1, groups)]
 
     common = dict(offsets=offsets, mats=mats, expand=expand, adj=adj, part=part)
     mine = [[(first, first, size)] for first, size in cut_up(0, cut, 2)]
     mine[-1].append((last, cut, ROWS))
-    state, own_a, sent_a, edges = stage(
+    state, field_a, own_a, sent_a, edges = stage(
         "group", groups, mine, cut_up(ROWS, half - ROWS, 3), (0, last),
         hypercube(groups), common | dict(enc=enc, proj=proj, pieces=pieces_a), None, weight=0.0,
     )
@@ -451,12 +507,12 @@
     low = lax.ppermute(edges[1], "tile", upward)
 
     mine = [[(first, first - cut, size)] for first, size in cut_up(cut, last - cut, 2)]
-    state, own_b, sent_b, _ = stage(
+    state, field_b, own_b, sent_b, _ = stage(
         "group", groups, mine, cut_up(half, third - half, 2), (),
         hypercube(groups), common | dict(enc=enc, proj=proj, pieces=pieces_b), state, weight=1.0,
     )
     got_a = scatter_steps(sent_a, "group", groups)
-    state, own_c, sent_c, _ = stage(
+    _, field_c, own_c, sent_c, _ = stage(
         "group", groups, [], cut_up(third, nbox - third, 2) + [(0, ROWS)], (),
         [[m] for m in range(1, groups)], common | dict(low=low, high=high), state, weight=1.0,
     )
@@ -478,7 +534,8 @@
         (out, third, [(ref, slot, 0, rows_c) for ref, slot in pick_c]),
     ]
     (gradient,) = add(jobs, operands, [jax.ShapeDtypeStruct((nbox, share), F32)])
-    return state[1], gradient
+    scattered = flush([field_a, field_b, field_c], nbox, got_c[0][0])
+    return scattered, gradient
 
 
 def solution(mesh):

time: 60.2 us -> 54.9 us (0.912)
  waiting for transfers between devices: 7.86 us -> 4.88 us
  starting transfers between devices: 25.2 us -> 24.3 us
  Pallas kernels: 25.4 us -> 24.7 us
  local copies, waits for them, and re-layouts: 0.7 us -> 0.01 us
    pallas_call x3, Pallas kernels: 14.5 us -> 11 us  [stage(): pl.pallas_call(functools.partial(stage_kernel, axis, count, mine, placed,...]
    ppermute x13, waiting for transfers between devices: 7.86 us -> 4.87 us  [exchange(): return lax.ppermute(x, axis, [(i, i ^ m) for i in range(count)])]
    pallas_call x2 -> x3, Pallas kernels: 9.02 us -> 11.7 us  [the longest x1 5.87 us: encode(): pl.pallas_call(functools.partial(encode_kernel, block, group, weighed //...]
    ppermute x13, starting transfers between devices: 18.8 us -> 17.9 us  [exchange(): return lax.ppermute(x, axis, [(i, i ^ m) for i in range(count)])]
    unnamed x10 -> x8, local copies, waits for them, and re-layouts: 0.7 us -> 0.01 us
  transfers between devices with their start and end apart: 15 -> 15, of which waited for: 5 -> 4; matrix products, arithmetic and copies ran while one was open for 0% -> 0% of each run, Pallas kernels for 39% -> 42%
where the time goes in v4:
time: 54.9 us; the launch traced here: 54.7 us
  Pallas kernels  24.7 us (45%)
  starting transfers between devices  24.3 us (44%)
  waiting for transfers between devices  4.88 us (9%)
  between operations  0.78 us (1%)
    ppermute x13, starting transfers between devices, exchange(): return lax.ppermute(x, axis, [(i, i ^ m) for i in range(count)])  17.9 us
    pallas_call x3, Pallas kernels, stage(): pl.pallas_call(functools.partial(stage_kernel, axis, count, mine, placed,...  11 us
    pallas_call x1, Pallas kernels, encode(): pl.pallas_call(functools.partial(encode_kernel, block, group, weighed //...  5.87 us
    ppermute x13, waiting for transfers between devices, exchange(): return lax.ppermute(x, axis, [(i, i ^ m) for i in range(count)])  4.87 us
    ppermute x1, starting transfers between devices, on_device(): high = lax.ppermute(edges[0], 'tile', downward)  4.54 us
    pallas_call x1, Pallas kernels, flush(): pl.pallas_call(functools.partial(flush_kernel, segments), in_specs=[VMEM]...  3.34 us
    pallas_call x1, Pallas kernels, weigh(): pl.pallas_call(functools.partial(weigh_kernel, block, weighed // block),...  2.48 us
    ppermute x1, starting transfers between devices, on_device(): low = lax.ppermute(edges[1], 'tile', upward)  1.91 us
  transfers between devices with their start and end apart: 15, of which 4 were waited for; matrix products, arithmetic and copies ran while one was open for 0% of the time, Pallas kernels for 42%

profile of v4, /device:TPU:4, one launch (start us, length us, event | category | flops | bytes accessed | tf_op | source)
XLA Modules:
  0.0 54.7 jit_solution(9089899647568258274)
XLA Ops:
  0.6 1.0 %split.1 = (bf16[272,256]{1,0:T(8,128)(2,1)S(1)}, bf16[240,256]{1,0:T(8,128)(2,1)S(1)}) custom-call(bf16[512,256]{1,0:T(8,128)(2,1)} %whole.1), custom_call_target="tpu_custom_call" | custom-call | tf_op jit(solution)/shard_map/split/pallas_call | solution.py:49
  1.6 1.6 %collective-permute-start.1 = (bf16[272,256]{1,0:T(8,128)(2,1)S(1)}, bf16[272,256]{1,0:T(8,128)(2,1)S(1)}, u32[]{:S(2)}, u32[]{:S(2)}) collective-permute-start(bf16[272,256]{1,0:T(8,128)(2,1)S(1)} %get-tuple-element.33.refs_7_), channel_id=1, source_target_pairs={{0,8},{8,0},{16,24},{24,16},{1,9},{9,1},{17,25},{25,17},{2,10},{10... | collective-permute-start | bytes 417800 | tf_op jit(solution)/shard_map/ppermute | solution.py:406
  3.3 2.6 %collective-permute-start = (bf16[272,256]{1,0:T(8,128)(2,1)S(1)}, bf16[272,256]{1,0:T(8,128)(2,1)S(1)}, u32[]{:S(2)}, u32[]{:S(2)}) collective-permute-start(bf16[272,256]{1,0:T(8,128)(2,1)S(1)} %get-tuple-element.33.refs_7_), channel_id=1, source_target_pairs={{0,16},{8,24},{16,0},{24,8},{1,17},{9,25},{17,1},{25,9},{2,18},{10... | collective-permute-start | bytes 417800 | tf_op jit(solution)/shard_map/ppermute | solution.py:406
  5.9 5.9 %encode.1 = (bf16[8,512,1024]{2,1,0:T(8,128)(2,1)S(1)}, bf16[8,512,1024]{2,1,0:T(8,128)(2,1)S(1)}, f32[512,1024]{1,0:T(8,128)S(1)}) custom-call(s32[1,8,8]{2,1,0:T(8,128)} %signs_in.1, bf16[1,8,512,1024]{3,2,1,0:T(8,128)(2,1)} %inc.1, bf16[1,8,512,1024]{3,2,1,0:T(8,128)(2,1)} %adj.3), custom_call_target="tpu_custom_call" | custom-call | flops 2147483648 | bytes 8388608 | tf_op jit(solution)/shard_map/encode/pallas_call | solution.py:113
  11.8 0.0 collective-permute-done.1.refs_8_
  11.8 0.6 %collective-permute-done._.refs_9_ = bf16[272,256]{1,0:T(8,128)(2,1)S(1)} collective-permute-done((bf16[272,256]{1,0:T(8,128)(2,1)S(1)}, bf16[272,256]{1,0:T(8,128)(2,1)S(1)}, u32[]{:S(2)}, u32[]{:S(2)}) %collective-permute-start) | collective-permute-done | bytes 139296 | tf_op jit(solution)/shard_map/ppermute | solution.py:406
  12.4 0.4 collective-permute-start.2
  12.8 0.0 copy-start
  12.8 0.0 copy-start.1
  12.8 0.0 copy-start.2
  12.8 0.0 copy-start.3
  12.8 2.5 %weigh.1 = (bf16[8,512,1024]{2,1,0:T(8,128)(2,1)S(1)}, f32[512,1024]{1,0:T(8,128)S(1)}) custom-call(bf16[1,8,512,1024]{3,2,1,0:T(8,128)(2,1)} %adj.3, bf16[8,512,1024]{2,1,0:T(8,128)(2,1)S(1)} %get-tuple-element.35.enc.refs_5_, bf16[272,256]{1,0:T(8,128)(2,1)S(1)} %collective-permute-done._.refs_9_, ...), custom_call_target="tpu_custom_call", output_to_operand_aliasing={{0}: (3, {}), {1}: (4, {})} | custom-call | flops 1 | bytes 1 | tf_op jit(solution)/shard_map/weigh/pallas_call | solution.py:160
  15.3 2.1 %collective-permute-start.5 = (bf16[240,256]{1,0:T(8,128)(2,1)S(1)}, bf16[240,256]{1,0:T(8,128)(2,1)S(1)}, u32[]{:S(2)}, u32[]{:S(2)}) collective-permute-start(bf16[240,256]{1,0:T(8,128)(2,1)S(1)} %get-tuple-element.45.refs_7_), channel_id=1, source_target_pairs={{0,24},{8,16},{16,8},{24,0},{1,25},{9,17},{17,9},{25,1},{2,26},{10... | collective-permute-start | bytes 368648 | tf_op jit(solution)/shard_map/ppermute | solution.py:406
  17.4 1.0 %collective-permute-start.4 = (bf16[240,256]{1,0:T(8,128)(2,1)S(1)}, bf16[240,256]{1,0:T(8,128)(2,1)S(1)}, u32[]{:S(2)}, u32[]{:S(2)}) collective-permute-start(bf16[240,256]{1,0:T(8,128)(2,1)S(1)} %get-tuple-element.45.refs_7_), channel_id=1, source_target_pairs={{0,16},{8,24},{16,0},{24,8},{1,17},{9,25},{17,1},{25,9},{2,18},{10... | collective-permute-start | bytes 368648 | tf_op jit(solution)/shard_map/ppermute | solution.py:406
  18.4 1.3 %collective-permute-start.3 = (bf16[240,256]{1,0:T(8,128)(2,1)S(1)}, bf16[240,256]{1,0:T(8,128)(2,1)S(1)}, u32[]{:S(2)}, u32[]{:S(2)}) collective-permute-start(bf16[240,256]{1,0:T(8,128)(2,1)S(1)} %get-tuple-element.45.refs_7_), channel_id=1, source_target_pairs={{0,8},{8,0},{16,24},{24,16},{1,9},{9,1},{17,25},{25,17},{2,10},{10... | collective-permute-start | bytes 368648 | tf_op jit(solution)/shard_map/ppermute | solution.py:406
  19.8 0.0 collective-permute-done.2.refs_10_
  19.8 0.0 copy-done
  19.8 0.0 copy-done.1
  19.8 0.0 copy-done.2
  19.8 0.0 copy-done.3
  19.8 4.9 %stage.3 = (f32[2,8,544,128]{3,2,1,0:T(8,128)S(1)}, bf16[8,224,1024]{2,1,0:T(8,128)(2,1)S(1)}, f32[224,256]{1,0:T(8,128)S(1)}, bf16[2,224,256]{2,1,0:T(8,128)(2,...) custom-call(s32[6]{0:T(128)S(1)} %copy-done.3, ...), custom_call_target="tpu_custom_call" | custom-call | tf_op jit(solution)/shard_map/stage/pallas_call | solution.py:338
  24.6 0.7 %collective-permute-start.9 = (bf16[2,224,256]{2,1,0:T(8,128)(2,1)S(1)}, bf16[2,224,256]{2,1,0:T(8,128)(2,1)S(1)}, u32[]{:S(2)}, u32[]{:S(2)}) collective-permute-start(bf16[2,224,256]{2,1,0:T(8,128)(2,1)S(1)} %get-tuple-element.54), channel_id=1, source_target_pairs={{0,8},{8,0},{16,24},{24,16},{1,9},{9,1},{17,25},{25,17},{2,10},{10... | collective-permute-start | bytes 688136 | tf_op jit(solution)/shard_map/ppermute | solution.py:406
  25.4 1.9 %collective-permute-start.6 = (bf16[8,16,256]{2,1,0:T(8,128)(2,1)S(1)}, bf16[8,16,256]{2,1,0:T(8,128)(2,1)S(1)}, u32[]{:S(2)}, u32[]{:S(2)}) collective-permute-start(bf16[8,16,256]{2,1,0:T(8,128)(2,1)S(1)} %get-tuple-element.48), channel_id=1, source_target_pairs={{0,1},{1,2},{2,3},{3,4},{4,5},{5,6},{6,7},{8,9},{9,10},{10,11},{11... | collective-permute-start | bytes 196616 | tf_op jit(solution)/shard_map/ppermute | solution.py:507
  27.3 0.0 collective-permute-done.5.refs_10_
  27.3 4.5 %collective-permute-start.7 = (bf16[8,16,256]{2,1,0:T(8,128)(2,1)S(1)}, bf16[8,16,256]{2,1,0:T(8,128)(2,1)S(1)}, u32[]{:S(2)}, u32[]{:S(2)}) collective-permute-start(bf16[8,16,256]{2,1,0:T(8,128)(2,1)S(1)} %get-tuple-element.49), channel_id=1, source_target_pairs={{1,0},{2,1},{3,2},{4,3},{5,4},{6,5},{7,6},{9,8},{10,9},{11,10},{12... | collective-permute-start | bytes 196616 | tf_op jit(solution)/shard_map/ppermute | solution.py:506
  31.9 0.0 collective-permute-done.4.refs_9_
  31.9 0.0 collective-permute-done.3.refs_8_
  31.9 3.4 %stage.4 = (f32[2,8,544,128]{3,2,1,0:T(8,128)S(1)}, bf16[8,128,1024]{2,1,0:T(8,128)(2,1)S(1)}, f32[128,256]{1,0:T(8,128)S(1)}, bf16[2,128,256]{2,1,0:T(8,128)(2,1)S(1)}, bf16[1,128,256]{2,1,0:T(8,128)(2,1)S(1)}) custom-call(s32[6]{0:T(128)S(1)} %copy-done.3, bf16[6,256,256]{2,1,0:T(8,128)(2,1)S(1)} %copy-done, ...), custom_call_target="tpu_custom_call", output_to_operand_aliasing={{0}: (11, {})} | custom-call | flops 2348810240 | bytes 2097152 | tf_op jit(solution)/shard_map/stage/pallas_call | solution.py:338
  35.3 1.4 %collective-permute-start.11 = (bf16[2,128,256]{2,1,0:T(8,128)(2,1)S(1)}, bf16[2,128,256]{2,1,0:T(8,128)(2,1)S(1)}, u32[]{:S(2)}, u32[]{:S(2)}) collective-permute-start(bf16[2,128,256]{2,1,0:T(8,128)(2,1)S(1)} %get-tuple-element.56), channel_id=1, source_target_pairs={{0,8},{8,0},{16,24},{24,16},{1,9},{9,1},{17,25},{25,17},{2,10},{10... | collective-permute-start | bytes 393224 | tf_op jit(solution)/shard_map/ppermute | solution.py:406
  36.7 0.0 collective-permute-done.9.refs_1_
  36.8 1.8 %collective-permute-start.10 = (bf16[1,224,256]{2,1,0:T(8,128)(2,1)S(1)}, bf16[1,224,256]{2,1,0:T(8,128)(2,1)S(1)}, u32[]{:S(2)}, u32[]{:S(2)}) collective-permute-start(bf16[1,224,256]{2,1,0:T(8,128)(2,1)S(1)} %add_convert_fusion), channel_id=1, source_target_pairs={{0,16},{8,24},{16,0},{24,8},{1,17},{9,25},{17,1},{25,9},{2,18},{10... | collective-permute-start | bytes 344072 | tf_op jit(solution)/shard_map/ppermute | solution.py:406
  38.5 0.0 collective-permute-done.6.refs_5_
  38.5 0.0 collective-permute-done.7.refs_6_
  38.5 2.8 %stage.5 = (f32[2,8,544,128]{3,2,1,0:T(8,128)S(1)}, bf16[8,160,1024]{2,1,0:T(8,128)(2,1)S(1)}, f32[160,256]{1,0:T(8,128)S(1)}, bf16[1,160,256]{2,1,0:T(8,128)(2,...) custom-call(s32[6]{0:T(128)S(1)} %copy-done.3, ...), custom_call_target="tpu_custom_call", output_to_operand_aliasing={{0}: (7, {})} | custom-call | flops 1677721600 | bytes 2621440 | tf_op jit(solution)/shard_map/stage/pallas_call | solution.py:338
  41.3 1.0 %collective-permute-start.8 = (bf16[1,160,256]{2,1,0:T(8,128)(2,1)S(1)}, bf16[1,160,256]{2,1,0:T(8,128)(2,1)S(1)}, u32[]{:S(2)}, u32[]{:S(2)}) collective-permute-start(bf16[1,160,256]{2,1,0:T(8,128)(2,1)S(1)} %get-tuple-element.52.refs_5_), channel_id=1, source_target_pairs={{0,8},{8,0},{16,24},{24,16},{1,9},{9,1},{17,25},{25,17},{2,10},{10... | collective-permute-start | bytes 245768 | tf_op jit(solution)/shard_map/ppermute | solution.py:406
  42.3 1.0 %collective-permute-start.13 = (bf16[1,160,256]{2,1,0:T(8,128)(2,1)S(1)}, bf16[1,160,256]{2,1,0:T(8,128)(2,1)S(1)}, u32[]{:S(2)}, u32[]{:S(2)}) collective-permute-start(bf16[1,160,256]{2,1,0:T(8,128)(2,1)S(1)} %get-tuple-element.62), channel_id=1, source_target_pairs={{0,16},{8,24},{16,0},{24,8},{1,17},{9,25},{17,1},{25,9},{2,18},{10... | collective-permute-start | bytes 245768 | tf_op jit(solution)/shard_map/ppermute | solution.py:406
  43.3 2.5 %collective-permute-start.14 = (bf16[1,160,256]{2,1,0:T(8,128)(2,1)S(1)}, bf16[1,160,256]{2,1,0:T(8,128)(2,1)S(1)}, u32[]{:S(2)}, u32[]{:S(2)}) collective-permute-start(bf16[1,160,256]{2,1,0:T(8,128)(2,1)S(1)} %get-tuple-element.63), channel_id=1, source_target_pairs={{0,24},{8,16},{16,8},{24,0},{1,25},{9,17},{17,9},{25,1},{2,26},{10... | collective-permute-start | bytes 245768 | tf_op jit(solution)/shard_map/ppermute | solution.py:406
  45.8 0.0 collective-permute-done.11.refs_3_.refs_2_
  45.8 0.0 collective-permute-done.10.refs_2_
  45.8 0.1 add.8
  45.9 0.4 collective-permute-start.12
  46.2 0.9 %collective-permute-done.8.refs_3_.refs_5_ = bf16[1,160,256]{2,1,0:T(8,128)(2,1)S(1)} collective-permute-done((bf16[1,160,256]{2,1,0:T(8,128)(2,1)S(1)}, bf16[1,160,256]{2,1,0:T(8,128)(2,1)S(1)}, u32[]{:S(2)}, u32[]{:S(2)}) %collective-permute-start.8) | collective-permute-done | bytes 81952 | tf_op jit(solution)/shard_map/ppermute | solution.py:406
  47.1 3.3 %flush.1 = bf16[1,8,512,1024]{3,2,1,0:T(8,128)(2,1)} custom-call(bf16[8,224,1024]{2,1,0:T(8,128)(2,1)S(1)} %get-tuple-element.44.refs_0_, bf16[8,128,1024]{2,1,0:T(8,128)(2,1)S(1)} %get-tuple-element.47.refs_1_, bf16[8,160,1024]{2,1,0:T(8,128)(2,1)S(1)} %get-tuple-element.51.refs_2_, bf16[1,160,256]{2,1,0:T(8,128)(2,1)S(1)} %collective-permute-done.8.refs_3_.refs_5_), custom_call_target="tpu_custom_call" | custom-call | flops 1 | bytes 1 | tf_op jit(solution)/shard_map/flush/pallas_call | solution.py:387
  50.5 1.5 %collective-permute-done.13.refs_6_ = bf16[1,160,256]{2,1,0:T(8,128)(2,1)S(1)} collective-permute-done((bf16[1,160,256]{2,1,0:T(8,128)(2,1)S(1)}, bf16[1,160,256]{2,1,0:T(8,128)(2,1)S(1)}, u32[]{:S(2)}, u32[]{:S(2)}) %collective-permute-start.13) | collective-permute-done | bytes 81952 | tf_op jit(solution)/shard_map/ppermute | solution.py:406
  51.9 0.0 collective-permute-done.14.refs_7_
  52.0 1.9 %collective-permute-done.12.refs_3_ = bf16[1,128,256]{2,1,0:T(8,128)(2,1)S(1)} collective-permute-done((bf16[1,128,256]{2,1,0:T(8,128)(2,1)S(1)}, bf16[1,128,256]{2,1,0:T(8,128)(2,1)S(1)}, u32[]{:S(2)}, u32[]{:S(2)}) %collective-permute-start.12) | collective-permute-done | bytes 65568 | tf_op jit(solution)/shard_map/ppermute | solution.py:406
  53.8 0.9 %add.9 = f32[512,256]{1,0:T(8,128)} custom-call(f32[224,256]{1,0:T(8,128)S(1)} %get-tuple-element.58.refs_0_, f32[128,256]{1,0:T(8,128)S(1)} %get-tuple-element.59.refs_1_, bf16[2,128,256]{2,1,0:T(8,128)(2,1)S(1)} %collective-permute-done.11.refs_3_.refs_2_, bf16[1,128,256]{2,1,0:T(8,128)(2,1)S(1)} %collective-permute-done.12.refs_3_, ...), custom_call_target="tpu_custom_call" | custom-call | tf_op jit(solution)/shard_map/add/pallas_call | solution.py:185
  (1 shorter events, 0.0 us)
Async XLA Ops:
  1.6 10.1 %collective-permute-start.1 = (bf16[272,256]{1,0:T(8,128)(2,1)S(1)}, bf16[272,256]{1,0:T(8,128)(2,1)S(1)}, u32[]{:S(2)}, u32[]{:S(2)}) collective-permute-start(bf16[272,256]{1,0:T(8,128)(2,1)S(1)} %get-tuple-element.33.refs_7_), channel_id=1, source_target_pairs={{0,8},{8,0},{16,24},{24,16},{1,9},{9,1},{17,25},{25,17},{2,10},{10... | collective-permute-start | bytes 417800 | tf_op jit(solution)/shard_map/ppermute | solution.py:406
  3.3 9.1 %collective-permute-start = (bf16[272,256]{1,0:T(8,128)(2,1)S(1)}, bf16[272,256]{1,0:T(8,128)(2,1)S(1)}, u32[]{:S(2)}, u32[]{:S(2)}) collective-permute-start(bf16[272,256]{1,0:T(8,128)(2,1)S(1)} %get-tuple-element.33.refs_7_), channel_id=1, source_target_pairs={{0,16},{8,24},{16,0},{24,8},{1,17},{9,25},{17,1},{25,9},{2,18},{10... | collective-permute-start | bytes 417800 | tf_op jit(solution)/shard_map/ppermute | solution.py:406
  12.4 7.4 %collective-permute-start.2 = (bf16[272,256]{1,0:T(8,128)(2,1)S(1)}, bf16[272,256]{1,0:T(8,128)(2,1)S(1)}, u32[]{:S(2)}, u32[]{:S(2)}) collective-permute-start(bf16[272,256]{1,0:T(8,128)(2,1)S(1)} %collective-permute-done._.refs_9_), channel_id=1, source_target_pairs={{0,8},{8,0},{16,24},{24,16},{1,9},{9,1},{17,25},{25,17},{2,10},{10... | collective-permute-start | bytes 417800 | tf_op jit(solution)/shard_map/ppermute | solution.py:406
  12.8 7.0 %copy-start = (bf16[6,256,256]{2,1,0:T(8,128)(2,1)S(1)}, bf16[6,256,256]{2,1,0:T(8,128)(2,1)}, u32[]{:S(2)}) copy-start(bf16[6,256,256]{2,1,0:T(8,128)(2,1)} %refs_1_.5) | copy-start | bytes 2359300
  12.8 7.0 %copy-start.1 = (bf16[256,1024]{1,0:T(8,128)(2,1)S(1)}, bf16[256,1024]{1,0:T(8,128)(2,1)}, u32[]{:S(2)}) copy-start(bf16[256,1024]{1,0:T(8,128)(2,1)} %refs_2_.5) | copy-start | bytes 1572868
  12.8 7.0 %copy-start.2 = (bf16[1024,256]{1,0:T(8,128)(2,1)S(1)}, bf16[1024,256]{1,0:T(8,128)(2,1)}, u32[]{:S(2)}) copy-start(bf16[1024,256]{1,0:T(8,128)(2,1)} %refs_6_.3) | copy-start | bytes 1572868
  12.8 7.0 %copy-start.3 = (s32[6]{0:T(128)S(1)}, s32[6]{0:T(128)}, u32[]{:S(2)}) copy-start(s32[6]{0:T(128)} %refs_0_.5) | copy-start | bytes 76
  15.3 12.0 %collective-permute-start.5 = (bf16[240,256]{1,0:T(8,128)(2,1)S(1)}, bf16[240,256]{1,0:T(8,128)(2,1)S(1)}, u32[]{:S(2)}, u32[]{:S(2)}) collective-permute-start(bf16[240,256]{1,0:T(8,128)(2,1)S(1)} %get-tuple-element.45.refs_7_), channel_id=1, source_target_pairs={{0,24},{8,16},{16,8},{24,0},{1,25},{9,17},{17,9},{25,1},{2,26},{10... | collective-permute-start | bytes 368648 | tf_op jit(solution)/shard_map/ppermute | solution.py:406
  17.4 14.5 %collective-permute-start.4 = (bf16[240,256]{1,0:T(8,128)(2,1)S(1)}, bf16[240,256]{1,0:T(8,128)(2,1)S(1)}, u32[]{:S(2)}, u32[]{:S(2)}) collective-permute-start(bf16[240,256]{1,0:T(8,128)(2,1)S(1)} %get-tuple-element.45.refs_7_), channel_id=1, source_target_pairs={{0,16},{8,24},{16,0},{24,8},{1,17},{9,25},{17,1},{25,9},{2,18},{10... | collective-permute-start | bytes 368648 | tf_op jit(solution)/shard_map/ppermute | solution.py:406
  18.4 13.5 %collective-permute-start.3 = (bf16[240,256]{1,0:T(8,128)(2,1)S(1)}, bf16[240,256]{1,0:T(8,128)(2,1)S(1)}, u32[]{:S(2)}, u32[]{:S(2)}) collective-permute-start(bf16[240,256]{1,0:T(8,128)(2,1)S(1)} %get-tuple-element.45.refs_7_), channel_id=1, source_target_pairs={{0,8},{8,0},{16,24},{24,16},{1,9},{9,1},{17,25},{25,17},{2,10},{10... | collective-permute-start | bytes 368648 | tf_op jit(solution)/shard_map/ppermute | solution.py:406
  24.6 12.1 %collective-permute-start.9 = (bf16[2,224,256]{2,1,0:T(8,128)(2,1)S(1)}, bf16[2,224,256]{2,1,0:T(8,128)(2,1)S(1)}, u32[]{:S(2)}, u32[]{:S(2)}) collective-permute-start(bf16[2,224,256]{2,1,0:T(8,128)(2,1)S(1)} %get-tuple-element.54), channel_id=1, source_target_pairs={{0,8},{8,0},{16,24},{24,16},{1,9},{9,1},{17,25},{25,17},{2,10},{10... | collective-permute-start | bytes 688136 | tf_op jit(solution)/shard_map/ppermute | solution.py:406
  25.4 13.2 %collective-permute-start.6 = (bf16[8,16,256]{2,1,0:T(8,128)(2,1)S(1)}, bf16[8,16,256]{2,1,0:T(8,128)(2,1)S(1)}, u32[]{:S(2)}, u32[]{:S(2)}) collective-permute-start(bf16[8,16,256]{2,1,0:T(8,128)(2,1)S(1)} %get-tuple-element.48), channel_id=1, source_target_pairs={{0,1},{1,2},{2,3},{3,4},{4,5},{5,6},{6,7},{8,9},{9,10},{10,11},{11... | collective-permute-start | bytes 196616 | tf_op jit(solution)/shard_map/ppermute | solution.py:507
  27.3 11.2 %collective-permute-start.7 = (bf16[8,16,256]{2,1,0:T(8,128)(2,1)S(1)}, bf16[8,16,256]{2,1,0:T(8,128)(2,1)S(1)}, u32[]{:S(2)}, u32[]{:S(2)}) collective-permute-start(bf16[8,16,256]{2,1,0:T(8,128)(2,1)S(1)} %get-tuple-element.49), channel_id=1, source_target_pairs={{1,0},{2,1},{3,2},{4,3},{5,4},{6,5},{7,6},{9,8},{10,9},{11,10},{12... | collective-permute-start | bytes 196616 | tf_op jit(solution)/shard_map/ppermute | solution.py:506
  35.3 10.5 %collective-permute-start.11 = (bf16[2,128,256]{2,1,0:T(8,128)(2,1)S(1)}, bf16[2,128,256]{2,1,0:T(8,128)(2,1)S(1)}, u32[]{:S(2)}, u32[]{:S(2)}) collective-permute-start(bf16[2,128,256]{2,1,0:T(8,128)(2,1)S(1)} %get-tuple-element.56), channel_id=1, source_target_pairs={{0,8},{8,0},{16,24},{24,16},{1,9},{9,1},{17,25},{25,17},{2,10},{10... | collective-permute-start | bytes 393224 | tf_op jit(solution)/shard_map/ppermute | solution.py:406
  36.8 9.0 %collective-permute-start.10 = (bf16[1,224,256]{2,1,0:T(8,128)(2,1)S(1)}, bf16[1,224,256]{2,1,0:T(8,128)(2,1)S(1)}, u32[]{:S(2)}, u32[]{:S(2)}) collective-permute-start(bf16[1,224,256]{2,1,0:T(8,128)(2,1)S(1)} %add_convert_fusion), channel_id=1, source_target_pairs={{0,16},{8,24},{16,0},{24,8},{1,17},{9,25},{17,1},{25,9},{2,18},{10... | collective-permute-start | bytes 344072 | tf_op jit(solution)/shard_map/ppermute | solution.py:406
  41.3 5.8 %collective-permute-start.8 = (bf16[1,160,256]{2,1,0:T(8,128)(2,1)S(1)}, bf16[1,160,256]{2,1,0:T(8,128)(2,1)S(1)}, u32[]{:S(2)}, u32[]{:S(2)}) collective-permute-start(bf16[1,160,256]{2,1,0:T(8,128)(2,1)S(1)} %get-tuple-element.52.refs_5_), channel_id=1, source_target_pairs={{0,8},{8,0},{16,24},{24,16},{1,9},{9,1},{17,25},{25,17},{2,10},{10... | collective-permute-start | bytes 245768 | tf_op jit(solution)/shard_map/ppermute | solution.py:406
  42.3 9.6 %collective-permute-start.13 = (bf16[1,160,256]{2,1,0:T(8,128)(2,1)S(1)}, bf16[1,160,256]{2,1,0:T(8,128)(2,1)S(1)}, u32[]{:S(2)}, u32[]{:S(2)}) collective-permute-start(bf16[1,160,256]{2,1,0:T(8,128)(2,1)S(1)} %get-tuple-element.62), channel_id=1, source_target_pairs={{0,16},{8,24},{16,0},{24,8},{1,17},{9,25},{17,1},{25,9},{2,18},{10... | collective-permute-start | bytes 245768 | tf_op jit(solution)/shard_map/ppermute | solution.py:406
  43.3 8.7 %collective-permute-start.14 = (bf16[1,160,256]{2,1,0:T(8,128)(2,1)S(1)}, bf16[1,160,256]{2,1,0:T(8,128)(2,1)S(1)}, u32[]{:S(2)}, u32[]{:S(2)}) collective-permute-start(bf16[1,160,256]{2,1,0:T(8,128)(2,1)S(1)} %get-tuple-element.63), channel_id=1, source_target_pairs={{0,24},{8,16},{16,8},{24,0},{1,25},{9,17},{17,9},{25,1},{2,26},{10... | collective-permute-start | bytes 245768 | tf_op jit(solution)/shard_map/ppermute | solution.py:406
  45.9 8.0 %collective-permute-start.12 = (bf16[1,128,256]{2,1,0:T(8,128)(2,1)S(1)}, bf16[1,128,256]{2,1,0:T(8,128)(2,1)S(1)}, u32[]{:S(2)}, u32[]{:S(2)}) collective-permute-start(bf16[1,128,256]{2,1,0:T(8,128)(2,1)S(1)} %bitcast.1), channel_id=1, source_target_pairs={{0,16},{8,24},{16,0},{24,8},{1,17},{9,25},{17,1},{25,9},{2,18},{10... | collective-permute-start | bytes 196616 | tf_op jit(solution)/shard_map/ppermute | solution.py:406

commit v5 on v4

--- a/solution.py
+++ b/solution.py
@@ -437,27 +437,29 @@
     return final
 
 
-def first_sums(own, got, sent, after, axis, count):
+def first_step(sent, after, axis, count, own=None, got=()):
     phases = hypercube(count)
     came = exchange(sent[0], axis, 1, count)
-    rows, share = own.shape
-    rows_b = sent[0].shape[1]
-    operands = [own] + [x for x, _ in got] + [came] + list(sent[1:]) + [after]
-    at = 1 + len(got)
-    outs = len(operands)
-    jobs = [(outs, 0, [(0, None, 0, rows)] + [(1 + i, slot, 0, rows) for i, (_, slot) in enumerate(got)])]
-    shapes = [pltpu.VMEM((rows, share), F32)]
-    order = []
+    rows, share = sent[0].shape[1:]
+    operands = [came] + list(sent[1:]) + list(after)
+    jobs, shapes, order = [], [], []
+    outs = len(operands) + (0 if own is None else 1 + len(got))
     for p, members in enumerate(phases[1:]):
         for s, m in enumerate(members):
-            terms = [(at + 1 + p, s, 0, rows_b)]
-            if m + 1 in phases[0] and m + 1 < count:
-                terms.append((at, phases[0].index(m + 1), 0, rows_b))
-            jobs.append((outs + 1 + len(order), 0, terms))
-            shapes.append(pltpu.VMEM((rows_b, share), BF16))
+            terms = [(1 + p, s, 0, rows)]
+            if m + 1 in phases[0]:
+                terms.append((0, phases[0].index(m + 1), 0, rows))
+            jobs.append((outs + len(order), 0, terms))
+            shapes.append(pltpu.VMEM((rows, share), BF16))
             order.append(m)
-    total, *kept = add(jobs, operands, shapes)
-    return total, (came, dict(zip(order, kept)))
+    if own is not None:
+        terms = [(len(operands), None, 0, own.shape[0])]
+        terms += [(len(operands) + 1 + i, slot, 0, own.shape[0]) for i, (_, slot) in enumerate(got)]
+        jobs.append((outs + len(order), 0, terms))
+        shapes.append(pltpu.VMEM(own.shape, F32))
+        operands += [own] + [x for x, _ in got]
+    result = add(jobs, operands, shapes)
+    return (came, dict(zip(order, result))), result[len(order):]
 
 
 def scatter_last(begun, axis, count):
@@ -480,7 +482,7 @@
     nbox = contrast.shape[0]
     half = nbox // 32 * 15
     cut, last = half + ROWS, nbox - ROWS
-    third = nbox // 32 * 23
+    third = nbox // 32 * 27
     upward = [(i, i + 1) for i in range(tiles - 1)]
     downward = [(i + 1, i) for i in range(tiles - 1)]
 
@@ -514,13 +516,14 @@
     got_a = scatter_steps(sent_a, "group", groups)
     _, field_c, own_c, sent_c, _ = stage(
         "group", groups, [], cut_up(third, nbox - third, 2) + [(0, ROWS)], (),
-        [[m] for m in range(1, groups)], common | dict(low=low, high=high), state, weight=1.0,
+        hypercube(groups), common | dict(low=low, high=high), state, weight=1.0,
     )
     share = own_a.shape[1]
     rows_a, rows_b, rows_c = half - ROWS, third - half, nbox - third
-    done_a, sent_b = first_sums(own_a, got_a, sent_b, sent_c[0], "group", groups)
-    got_b = scatter_last(sent_b, "group", groups)
-    got_c = scatter_direct(sent_c, "group", groups)
+    begun_b, _ = first_step(sent_b, [sent_c[0]], "group", groups)
+    got_b = scatter_last(begun_b, "group", groups)
+    begun_c, (done_a,) = first_step(sent_c, [begun_b[1][2]] if groups > 2 else [], "group", groups, own_a, got_a)
+    got_c = scatter_last(begun_c, "group", groups)
 
     operands = [done_a, own_b] + [x for x, _ in got_b] + [own_c] + [x for x, _ in got_c]
     at_c = 2 + len(got_b)

time: 54.9 us -> 54.5 us (level); the launches traced: 54.7 us -> 53.6 us
  starting transfers between devices: 24.3 us -> 22.8 us
    ppermute x13 -> x12, starting transfers between devices: 17.9 us -> 16.3 us  [exchange(): return lax.ppermute(x, axis, [(i, i ^ m) for i in range(count)])]
    ppermute x13 -> x12, waiting for transfers between devices: 4.87 us -> 5.28 us  [exchange(): return lax.ppermute(x, axis, [(i, i ^ m) for i in range(count)])]
  transfers between devices with their start and end apart: 15 -> 14, of which waited for: 4 -> 4; matrix products, arithmetic and copies ran while one was open for 0% -> 0% of each run, Pallas kernels for 42% -> 43%
where the time goes in v5:
time: 54.5 us; the launch traced here: 53.6 us
  Pallas kernels  24.8 us (46%)
  starting transfers between devices  22.8 us (42%)
  waiting for transfers between devices  5.28 us (10%)
  between operations  0.78 us (1%)
    ppermute x12, starting transfers between devices, exchange(): return lax.ppermute(x, axis, [(i, i ^ m) for i in range(count)])  16.3 us
    pallas_call x3, Pallas kernels, stage(): pl.pallas_call(functools.partial(stage_kernel, axis, count, mine, placed,...  11.1 us
    pallas_call x1, Pallas kernels, encode(): pl.pallas_call(functools.partial(encode_kernel, block, group, weighed //...  5.87 us
    ppermute x12, waiting for transfers between devices, exchange(): return lax.ppermute(x, axis, [(i, i ^ m) for i in range(count)])  5.28 us
    ppermute x1, starting transfers between devices, on_device(): high = lax.ppermute(edges[0], 'tile', downward)  4.54 us
    pallas_call x1, Pallas kernels, flush(): pl.pallas_call(functools.partial(flush_kernel, segments), in_specs=[VMEM]...  3.37 us
    pallas_call x1, Pallas kernels, weigh(): pl.pallas_call(functools.partial(weigh_kernel, block, weighed // block),...  2.48 us
    ppermute x1, starting transfers between devices, on_device(): low = lax.ppermute(edges[1], 'tile', upward)  1.92 us
  transfers between devices with their start and end apart: 14, of which 4 were waited for; matrix products, arithmetic and copies ran while one was open for 0% of the time, Pallas kernels for 43%

profile of v5, /device:TPU:4, one launch (start us, length us, event | category | flops | bytes accessed | tf_op | source)
XLA Modules:
  0.0 53.6 jit_solution(11522309179255504847)
XLA Ops:
  0.6 1.0 %split.1 = (bf16[272,256]{1,0:T(8,128)(2,1)S(1)}, bf16[240,256]{1,0:T(8,128)(2,1)S(1)}) custom-call(bf16[512,256]{1,0:T(8,128)(2,1)} %whole.1), custom_call_target="tpu_custom_call" | custom-call | tf_op jit(solution)/shard_map/split/pallas_call | solution.py:49
  1.6 1.6 %collective-permute-start.1 = (bf16[272,256]{1,0:T(8,128)(2,1)S(1)}, bf16[272,256]{1,0:T(8,128)(2,1)S(1)}, u32[]{:S(2)}, u32[]{:S(2)}) collective-permute-start(bf16[272,256]{1,0:T(8,128)(2,1)S(1)} %get-tuple-element.32.refs_7_), channel_id=1, source_target_pairs={{0,8},{8,0},{16,24},{24,16},{1,9},{9,1},{17,25},{25,17},{2,10},{10... | collective-permute-start | bytes 417800 | tf_op jit(solution)/shard_map/ppermute | solution.py:406
  3.3 2.6 %collective-permute-start = (bf16[272,256]{1,0:T(8,128)(2,1)S(1)}, bf16[272,256]{1,0:T(8,128)(2,1)S(1)}, u32[]{:S(2)}, u32[]{:S(2)}) collective-permute-start(bf16[272,256]{1,0:T(8,128)(2,1)S(1)} %get-tuple-element.32.refs_7_), channel_id=1, source_target_pairs={{0,16},{8,24},{16,0},{24,8},{1,17},{9,25},{17,1},{25,9},{2,18},{10... | collective-permute-start | bytes 417800 | tf_op jit(solution)/shard_map/ppermute | solution.py:406
  5.9 5.9 %encode.1 = (bf16[8,512,1024]{2,1,0:T(8,128)(2,1)S(1)}, bf16[8,512,1024]{2,1,0:T(8,128)(2,1)S(1)}, f32[512,1024]{1,0:T(8,128)S(1)}) custom-call(s32[1,8,8]{2,1,0:T(8,128)} %signs_in.1, bf16[1,8,512,1024]{3,2,1,0:T(8,128)(2,1)} %inc.1, bf16[1,8,512,1024]{3,2,1,0:T(8,128)(2,1)} %adj.3), custom_call_target="tpu_custom_call" | custom-call | flops 2147483648 | bytes 8388608 | tf_op jit(solution)/shard_map/encode/pallas_call | solution.py:113
  11.8 0.0 collective-permute-done.1.refs_8_
  11.8 0.6 %collective-permute-done._.refs_9_ = bf16[272,256]{1,0:T(8,128)(2,1)S(1)} collective-permute-done((bf16[272,256]{1,0:T(8,128)(2,1)S(1)}, bf16[272,256]{1,0:T(8,128)(2,1)S(1)}, u32[]{:S(2)}, u32[]{:S(2)}) %collective-permute-start) | collective-permute-done | bytes 139296 | tf_op jit(solution)/shard_map/ppermute | solution.py:406
  12.4 0.4 collective-permute-start.2
  12.8 0.0 copy-start
  12.8 0.0 copy-start.1
  12.8 0.0 copy-start.2
  12.8 0.0 copy-start.3
  12.8 2.5 %weigh.1 = (bf16[8,512,1024]{2,1,0:T(8,128)(2,1)S(1)}, f32[512,1024]{1,0:T(8,128)S(1)}) custom-call(bf16[1,8,512,1024]{3,2,1,0:T(8,128)(2,1)} %adj.3, bf16[8,512,1024]{2,1,0:T(8,128)(2,1)S(1)} %get-tuple-element.34.enc.refs_5_, bf16[272,256]{1,0:T(8,128)(2,1)S(1)} %collective-permute-done._.refs_9_, ...), custom_call_target="tpu_custom_call", output_to_operand_aliasing={{0}: (3, {}), {1}: (4, {})} | custom-call | flops 1 | bytes 1 | tf_op jit(solution)/shard_map/weigh/pallas_call | solution.py:160
  15.3 2.1 %collective-permute-start.5 = (bf16[240,256]{1,0:T(8,128)(2,1)S(1)}, bf16[240,256]{1,0:T(8,128)(2,1)S(1)}, u32[]{:S(2)}, u32[]{:S(2)}) collective-permute-start(bf16[240,256]{1,0:T(8,128)(2,1)S(1)} %get-tuple-element.44.refs_7_), channel_id=1, source_target_pairs={{0,24},{8,16},{16,8},{24,0},{1,25},{9,17},{17,9},{25,1},{2,26},{10... | collective-permute-start | bytes 368648 | tf_op jit(solution)/shard_map/ppermute | solution.py:406
  17.4 1.0 %collective-permute-start.4 = (bf16[240,256]{1,0:T(8,128)(2,1)S(1)}, bf16[240,256]{1,0:T(8,128)(2,1)S(1)}, u32[]{:S(2)}, u32[]{:S(2)}) collective-permute-start(bf16[240,256]{1,0:T(8,128)(2,1)S(1)} %get-tuple-element.44.refs_7_), channel_id=1, source_target_pairs={{0,16},{8,24},{16,0},{24,8},{1,17},{9,25},{17,1},{25,9},{2,18},{10... | collective-permute-start | bytes 368648 | tf_op jit(solution)/shard_map/ppermute | solution.py:406
  18.4 1.3 %collective-permute-start.3 = (bf16[240,256]{1,0:T(8,128)(2,1)S(1)}, bf16[240,256]{1,0:T(8,128)(2,1)S(1)}, u32[]{:S(2)}, u32[]{:S(2)}) collective-permute-start(bf16[240,256]{1,0:T(8,128)(2,1)S(1)} %get-tuple-element.44.refs_7_), channel_id=1, source_target_pairs={{0,8},{8,0},{16,24},{24,16},{1,9},{9,1},{17,25},{25,17},{2,10},{10... | collective-permute-start | bytes 368648 | tf_op jit(solution)/shard_map/ppermute | solution.py:406
  19.8 0.0 collective-permute-done.2.refs_10_
  19.8 0.0 copy-done
  19.8 0.0 copy-done.1
  19.8 0.0 copy-done.2
  19.8 0.0 copy-done.3
  19.8 4.8 %stage.3 = (f32[2,8,544,128]{3,2,1,0:T(8,128)S(1)}, bf16[8,224,1024]{2,1,0:T(8,128)(2,1)S(1)}, f32[224,256]{1,0:T(8,128)S(1)}, bf16[2,224,256]{2,1,0:T(8,128)(2,...) custom-call(s32[6]{0:T(128)S(1)} %copy-done.3, ...), custom_call_target="tpu_custom_call" | custom-call | tf_op jit(solution)/shard_map/stage/pallas_call | solution.py:338
  24.6 1.9 %collective-permute-start.6 = (bf16[8,16,256]{2,1,0:T(8,128)(2,1)S(1)}, bf16[8,16,256]{2,1,0:T(8,128)(2,1)S(1)}, u32[]{:S(2)}, u32[]{:S(2)}) collective-permute-start(bf16[8,16,256]{2,1,0:T(8,128)(2,1)S(1)} %get-tuple-element.47), channel_id=1, source_target_pairs={{0,1},{1,2},{2,3},{3,4},{4,5},{5,6},{6,7},{8,9},{9,10},{10,11},{11... | collective-permute-start | bytes 196616 | tf_op jit(solution)/shard_map/ppermute | solution.py:509
  26.6 4.5 %collective-permute-start.7 = (bf16[8,16,256]{2,1,0:T(8,128)(2,1)S(1)}, bf16[8,16,256]{2,1,0:T(8,128)(2,1)S(1)}, u32[]{:S(2)}, u32[]{:S(2)}) collective-permute-start(bf16[8,16,256]{2,1,0:T(8,128)(2,1)S(1)} %get-tuple-element.48), channel_id=1, source_target_pairs={{1,0},{2,1},{3,2},{4,3},{5,4},{6,5},{7,6},{9,8},{10,9},{11,10},{12... | collective-permute-start | bytes 196616 | tf_op jit(solution)/shard_map/ppermute | solution.py:508
  31.1 0.0 collective-permute-done.5.refs_10_
  31.1 0.7 %collective-permute-start.10 = (bf16[2,224,256]{2,1,0:T(8,128)(2,1)S(1)}, bf16[2,224,256]{2,1,0:T(8,128)(2,1)S(1)}, u32[]{:S(2)}, u32[]{:S(2)}) collective-permute-start(bf16[2,224,256]{2,1,0:T(8,128)(2,1)S(1)} %get-tuple-element.56), channel_id=1, source_target_pairs={{0,8},{8,0},{16,24},{24,16},{1,9},{9,1},{17,25},{25,17},{2,10},{10... | collective-permute-start | bytes 688136 | tf_op jit(solution)/shard_map/ppermute | solution.py:406
  31.9 0.0 collective-permute-done.4.refs_9_
  31.9 0.0 collective-permute-done.3.refs_8_
  31.9 4.2 %stage.4 = (f32[2,8,544,128]{3,2,1,0:T(8,128)S(1)}, bf16[8,192,1024]{2,1,0:T(8,128)(2,1)S(1)}, f32[192,256]{1,0:T(8,128)S(1)}, bf16[2,192,256]{2,1,0:T(8,128)(2,1)S(1)}, bf16[1,192,256]{2,1,0:T(8,128)(2,1)S(1)}) custom-call(s32[6]{0:T(128)S(1)} %copy-done.3, bf16[6,256,256]{2,1,0:T(8,128)(2,1)S(1)} %copy-done, ...), custom_call_target="tpu_custom_call", output_to_operand_aliasing={{0}: (11, {})} | custom-call | flops 3019898880 | bytes 3145728 | tf_op jit(solution)/shard_map/stage/pallas_call | solution.py:338
  36.0 1.4 %collective-permute-start.9 = (bf16[2,192,256]{2,1,0:T(8,128)(2,1)S(1)}, bf16[2,192,256]{2,1,0:T(8,128)(2,1)S(1)}, u32[]{:S(2)}, u32[]{:S(2)}) collective-permute-start(bf16[2,192,256]{2,1,0:T(8,128)(2,1)S(1)} %get-tuple-element.53), channel_id=1, source_target_pairs={{0,8},{8,0},{16,24},{24,16},{1,9},{9,1},{17,25},{25,17},{2,10},{10... | collective-permute-start | bytes 589832 | tf_op jit(solution)/shard_map/ppermute | solution.py:406
  37.5 0.4 collective-permute-done.10.refs_4_
  37.9 1.6 %collective-permute-start.11 = (bf16[1,224,256]{2,1,0:T(8,128)(2,1)S(1)}, bf16[1,224,256]{2,1,0:T(8,128)(2,1)S(1)}, u32[]{:S(2)}, u32[]{:S(2)}) collective-permute-start(bf16[1,224,256]{2,1,0:T(8,128)(2,1)S(1)} %add_convert_fusion), channel_id=1, source_target_pairs={{0,16},{8,24},{16,0},{24,8},{1,17},{9,25},{17,1},{25,9},{2,18},{10... | collective-permute-start | bytes 344072 | tf_op jit(solution)/shard_map/ppermute | solution.py:406
  39.5 0.0 collective-permute-done.6.refs_5_
  39.5 0.0 collective-permute-done.7.refs_6_
  39.5 2.1 %stage.5 = (f32[2,8,544,128]{3,2,1,0:T(8,128)S(1)}, bf16[8,96,1024]{2,1,0:T(8,128)(2,1)S(1)}, f32[96,256]{1,0:T(8,128)S(1)}, bf16[2,96,256]{2,1,0:T(8,128)(2,1)S(1)}, bf16[1,96,256]{2,1,0:T(8,128)(2,1)S(1)}) custom-call(s32[6]{0:T(128)S(1)} %copy-done.3, bf16[6,256,256]{2,1,0:T(8,128)(2,1)S(1)} %copy-done, ...), custom_call_target="tpu_custom_call", output_to_operand_aliasing={{0}: (7, {})} | custom-call | flops 1006632960 | bytes 1572864 | tf_op jit(solution)/shard_map/stage/pallas_call | solution.py:338
  41.6 1.0 %collective-permute-start.8 = (bf16[2,96,256]{2,1,0:T(8,128)(2,1)S(1)}, bf16[2,96,256]{2,1,0:T(8,128)(2,1)S(1)}, u32[]{:S(2)}, u32[]{:S(2)}) collective-permute-start(bf16[2,96,256]{2,1,0:T(8,128)(2,1)S(1)} %get-tuple-element.51.refs_2_), channel_id=1, source_target_pairs={{0,8},{8,0},{16,24},{24,16},{1,9},{9,1},{17,25},{25,17},{2,10},{10... | collective-permute-start | bytes 294920 | tf_op jit(solution)/shard_map/ppermute | solution.py:406
  42.5 3.2 %collective-permute-done.9.refs_0_.refs_2_ = bf16[2,192,256]{2,1,0:T(8,128)(2,1)S(1)} collective-permute-done((bf16[2,192,256]{2,1,0:T(8,128)(2,1)S(1)}, bf16[2,192,256]{2,1,0:T(8,128)(2,1)S(1)}, u32[]{:S(2)}, u32[]{:S(2)}) %collective-permute-start.9) | collective-permute-done | bytes 196640 | tf_op jit(solution)/shard_map/ppermute | solution.py:406
  45.8 0.2 collective-permute-start.12
  46.0 1.0 %collective-permute-done.8.refs_3_.refs_0_.refs_5_ = bf16[2,96,256]{2,1,0:T(8,128)(2,1)S(1)} collective-permute-done((bf16[2,96,256]{2,1,0:T(8,128)(2,1)S(1)}, bf16[2,96,256]{2,1,0:T(8,128)(2,1)S(1)}, u32[]{:S(2)}, u32[]{:S(2)}) %collective-permute-start.8) | collective-permute-done | bytes 98336 | tf_op jit(solution)/shard_map/ppermute | solution.py:406
  47.0 0.0 collective-permute-done.11.refs_5_
  47.1 2.3 %collective-permute-start.13 = (bf16[1,96,256]{2,1,0:T(8,128)(2,1)S(1)}, bf16[1,96,256]{2,1,0:T(8,128)(2,1)S(1)}, u32[]{:S(2)}, u32[]{:S(2)}) collective-permute-start(bf16[1,96,256]{2,1,0:T(8,128)(2,1)S(1)} %bitcast.3), channel_id=1, source_target_pairs={{0,16},{8,24},{16,0},{24,8},{1,17},{9,25},{17,1},{25,9},{2,18},{10... | collective-permute-start | bytes 147464 | tf_op jit(solution)/shard_map/ppermute | solution.py:406
  49.4 3.4 %flush.1 = bf16[1,8,512,1024]{3,2,1,0:T(8,128)(2,1)} custom-call(bf16[8,224,1024]{2,1,0:T(8,128)(2,1)S(1)} %get-tuple-element.43.refs_0_, bf16[8,192,1024]{2,1,0:T(8,128)(2,1)S(1)} %get-tuple-element.46.refs_1_, bf16[8,96,1024]{2,1,0:T(8,128)(2,1)S(1)} %get-tuple-element.50.refs_2_, bf16[2,96,256]{2,1,0:T(8,128)(2,1)S(1)} %collective-permute-done.8.refs_3_.refs_0_.refs_5_), custom_call_target="tpu_custom_call" | custom-call | flops 1 | bytes 1 | tf_op jit(solution)/shard_map/flush/pallas_call | solution.py:387
  52.7 0.0 collective-permute-done.12.refs_3_
  52.8 0.0 collective-permute-done.13.refs_6_
  52.8 0.9 %add.11 = f32[512,256]{1,0:T(8,128)} custom-call(f32[224,256]{1,0:T(8,128)S(1)} %get-tuple-element.58.refs_0_, f32[192,256]{1,0:T(8,128)S(1)} %get-tuple-element.59.refs_1_, bf16[2,192,256]{2,1,0:T(8,128)(2,1)S(1)} %collective-permute-done.9.refs_0_.refs_2_, bf16[1,192,256]{2,1,0:T(8,128)(2,1)S(1)} %collective-permute-done.12.refs_3_, ...), custom_call_target="tpu_custom_call" | custom-call | tf_op jit(solution)/shard_map/add/pallas_call | solution.py:185
  (3 shorter events, 0.1 us)
Async XLA Ops:
  1.6 10.1 %collective-permute-start.1 = (bf16[272,256]{1,0:T(8,128)(2,1)S(1)}, bf16[272,256]{1,0:T(8,128)(2,1)S(1)}, u32[]{:S(2)}, u32[]{:S(2)}) collective-permute-start(bf16[272,256]{1,0:T(8,128)(2,1)S(1)} %get-tuple-element.32.refs_7_), channel_id=1, source_target_pairs={{0,8},{8,0},{16,24},{24,16},{1,9},{9,1},{17,25},{25,17},{2,10},{10... | collective-permute-start | bytes 417800 | tf_op jit(solution)/shard_map/ppermute | solution.py:406
  3.3 9.1 %collective-permute-start = (bf16[272,256]{1,0:T(8,128)(2,1)S(1)}, bf16[272,256]{1,0:T(8,128)(2,1)S(1)}, u32[]{:S(2)}, u32[]{:S(2)}) collective-permute-start(bf16[272,256]{1,0:T(8,128)(2,1)S(1)} %get-tuple-element.32.refs_7_), channel_id=1, source_target_pairs={{0,16},{8,24},{16,0},{24,8},{1,17},{9,25},{17,1},{25,9},{2,18},{10... | collective-permute-start | bytes 417800 | tf_op jit(solution)/shard_map/ppermute | solution.py:406
  12.4 7.4 %collective-permute-start.2 = (bf16[272,256]{1,0:T(8,128)(2,1)S(1)}, bf16[272,256]{1,0:T(8,128)(2,1)S(1)}, u32[]{:S(2)}, u32[]{:S(2)}) collective-permute-start(bf16[272,256]{1,0:T(8,128)(2,1)S(1)} %collective-permute-done._.refs_9_), channel_id=1, source_target_pairs={{0,8},{8,0},{16,24},{24,16},{1,9},{9,1},{17,25},{25,17},{2,10},{10... | collective-permute-start | bytes 417800 | tf_op jit(solution)/shard_map/ppermute | solution.py:406
  12.8 7.0 %copy-start = (bf16[6,256,256]{2,1,0:T(8,128)(2,1)S(1)}, bf16[6,256,256]{2,1,0:T(8,128)(2,1)}, u32[]{:S(2)}) copy-start(bf16[6,256,256]{2,1,0:T(8,128)(2,1)} %refs_1_.5) | copy-start | bytes 2359300
  12.8 7.0 %copy-start.1 = (bf16[256,1024]{1,0:T(8,128)(2,1)S(1)}, bf16[256,1024]{1,0:T(8,128)(2,1)}, u32[]{:S(2)}) copy-start(bf16[256,1024]{1,0:T(8,128)(2,1)} %refs_2_.5) | copy-start | bytes 1572868
  12.8 7.0 %copy-start.2 = (bf16[1024,256]{1,0:T(8,128)(2,1)S(1)}, bf16[1024,256]{1,0:T(8,128)(2,1)}, u32[]{:S(2)}) copy-start(bf16[1024,256]{1,0:T(8,128)(2,1)} %refs_6_.3) | copy-start | bytes 1572868
  12.8 7.0 %copy-start.3 = (s32[6]{0:T(128)S(1)}, s32[6]{0:T(128)}, u32[]{:S(2)}) copy-start(s32[6]{0:T(128)} %refs_0_.5) | copy-start | bytes 76
  15.3 15.8 %collective-permute-start.5 = (bf16[240,256]{1,0:T(8,128)(2,1)S(1)}, bf16[240,256]{1,0:T(8,128)(2,1)S(1)}, u32[]{:S(2)}, u32[]{:S(2)}) collective-permute-start(bf16[240,256]{1,0:T(8,128)(2,1)S(1)} %get-tuple-element.44.refs_7_), channel_id=1, source_target_pairs={{0,24},{8,16},{16,8},{24,0},{1,25},{9,17},{17,9},{25,1},{2,26},{10... | collective-permute-start | bytes 368648 | tf_op jit(solution)/shard_map/ppermute | solution.py:406
  17.4 14.5 %collective-permute-start.4 = (bf16[240,256]{1,0:T(8,128)(2,1)S(1)}, bf16[240,256]{1,0:T(8,128)(2,1)S(1)}, u32[]{:S(2)}, u32[]{:S(2)}) collective-permute-start(bf16[240,256]{1,0:T(8,128)(2,1)S(1)} %get-tuple-element.44.refs_7_), channel_id=1, source_target_pairs={{0,16},{8,24},{16,0},{24,8},{1,17},{9,25},{17,1},{25,9},{2,18},{10... | collective-permute-start | bytes 368648 | tf_op jit(solution)/shard_map/ppermute | solution.py:406
  18.4 13.5 %collective-permute-start.3 = (bf16[240,256]{1,0:T(8,128)(2,1)S(1)}, bf16[240,256]{1,0:T(8,128)(2,1)S(1)}, u32[]{:S(2)}, u32[]{:S(2)}) collective-permute-start(bf16[240,256]{1,0:T(8,128)(2,1)S(1)} %get-tuple-element.44.refs_7_), channel_id=1, source_target_pairs={{0,8},{8,0},{16,24},{24,16},{1,9},{9,1},{17,25},{25,17},{2,10},{10... | collective-permute-start | bytes 368648 | tf_op jit(solution)/shard_map/ppermute | solution.py:406
  24.6 14.8 %collective-permute-start.6 = (bf16[8,16,256]{2,1,0:T(8,128)(2,1)S(1)}, bf16[8,16,256]{2,1,0:T(8,128)(2,1)S(1)}, u32[]{:S(2)}, u32[]{:S(2)}) collective-permute-start(bf16[8,16,256]{2,1,0:T(8,128)(2,1)S(1)} %get-tuple-element.47), channel_id=1, source_target_pairs={{0,1},{1,2},{2,3},{3,4},{4,5},{5,6},{6,7},{8,9},{9,10},{10,11},{11... | collective-permute-start | bytes 196616 | tf_op jit(solution)/shard_map/ppermute | solution.py:509
  26.6 12.9 %collective-permute-start.7 = (bf16[8,16,256]{2,1,0:T(8,128)(2,1)S(1)}, bf16[8,16,256]{2,1,0:T(8,128)(2,1)S(1)}, u32[]{:S(2)}, u32[]{:S(2)}) collective-permute-start(bf16[8,16,256]{2,1,0:T(8,128)(2,1)S(1)} %get-tuple-element.48), channel_id=1, source_target_pairs={{1,0},{2,1},{3,2},{4,3},{5,4},{6,5},{7,6},{9,8},{10,9},{11,10},{12... | collective-permute-start | bytes 196616 | tf_op jit(solution)/shard_map/ppermute | solution.py:508
  31.1 6.8 %collective-permute-start.10 = (bf16[2,224,256]{2,1,0:T(8,128)(2,1)S(1)}, bf16[2,224,256]{2,1,0:T(8,128)(2,1)S(1)}, u32[]{:S(2)}, u32[]{:S(2)}) collective-permute-start(bf16[2,224,256]{2,1,0:T(8,128)(2,1)S(1)} %get-tuple-element.56), channel_id=1, source_target_pairs={{0,8},{8,0},{16,24},{24,16},{1,9},{9,1},{17,25},{25,17},{2,10},{10... | collective-permute-start | bytes 688136 | tf_op jit(solution)/shard_map/ppermute | solution.py:406
  36.0 9.7 %collective-permute-start.9 = (bf16[2,192,256]{2,1,0:T(8,128)(2,1)S(1)}, bf16[2,192,256]{2,1,0:T(8,128)(2,1)S(1)}, u32[]{:S(2)}, u32[]{:S(2)}) collective-permute-start(bf16[2,192,256]{2,1,0:T(8,128)(2,1)S(1)} %get-tuple-element.53), channel_id=1, source_target_pairs={{0,8},{8,0},{16,24},{24,16},{1,9},{9,1},{17,25},{25,17},{2,10},{10... | collective-permute-start | bytes 589832 | tf_op jit(solution)/shard_map/ppermute | solution.py:406
  37.9 9.1 %collective-permute-start.11 = (bf16[1,224,256]{2,1,0:T(8,128)(2,1)S(1)}, bf16[1,224,256]{2,1,0:T(8,128)(2,1)S(1)}, u32[]{:S(2)}, u32[]{:S(2)}) collective-permute-start(bf16[1,224,256]{2,1,0:T(8,128)(2,1)S(1)} %add_convert_fusion), channel_id=1, source_target_pairs={{0,16},{8,24},{16,0},{24,8},{1,17},{9,25},{17,1},{25,9},{2,18},{10... | collective-permute-start | bytes 344072 | tf_op jit(solution)/shard_map/ppermute | solution.py:406
  41.6 5.4 %collective-permute-start.8 = (bf16[2,96,256]{2,1,0:T(8,128)(2,1)S(1)}, bf16[2,96,256]{2,1,0:T(8,128)(2,1)S(1)}, u32[]{:S(2)}, u32[]{:S(2)}) collective-permute-start(bf16[2,96,256]{2,1,0:T(8,128)(2,1)S(1)} %get-tuple-element.51.refs_2_), channel_id=1, source_target_pairs={{0,8},{8,0},{16,24},{24,16},{1,9},{9,1},{17,25},{25,17},{2,10},{10... | collective-permute-start | bytes 294920 | tf_op jit(solution)/shard_map/ppermute | solution.py:406
  45.8 7.0 %collective-permute-start.12 = (bf16[1,192,256]{2,1,0:T(8,128)(2,1)S(1)}, bf16[1,192,256]{2,1,0:T(8,128)(2,1)S(1)}, u32[]{:S(2)}, u32[]{:S(2)}) collective-permute-start(bf16[1,192,256]{2,1,0:T(8,128)(2,1)S(1)} %bitcast.2), channel_id=1, source_target_pairs={{0,16},{8,24},{16,0},{24,8},{1,17},{9,25},{17,1},{25,9},{2,18},{10... | collective-permute-start | bytes 294920 | tf_op jit(solution)/shard_map/ppermute | solution.py:406
  47.1 5.7 %collective-permute-start.13 = (bf16[1,96,256]{2,1,0:T(8,128)(2,1)S(1)}, bf16[1,96,256]{2,1,0:T(8,128)(2,1)S(1)}, u32[]{:S(2)}, u32[]{:S(2)}) collective-permute-start(bf16[1,96,256]{2,1,0:T(8,128)(2,1)S(1)} %bitcast.3), channel_id=1, source_target_pairs={{0,16},{8,24},{16,0},{24,8},{1,17},{9,25},{17,1},{25,9},{2,18},{10... | collective-permute-start | bytes 147464 | tf_op jit(solution)/shard_map/ppermute | solution.py:406

commit v6 on v5

--- a/solution.py
+++ b/solution.py
@@ -106,7 +106,7 @@
     lax.fori_loop(weighed, steps, functools.partial(step, weigh=False), 0)
 
 
-def encode(signs, incident, adjoint, weighed, block=64):
+def encode(signs, incident, adjoint, weighed, block=32):
     _, count, nbox, points = incident.shape
     outs = adjoint.shape[1]
     group = 256 // count
@@ -490,7 +490,7 @@
     far_side = groups // 2
     first = exchange(contrast_a, "group", 1, groups)
     top = exchange(contrast_a, "group", far_side, groups)
-    weighed = nbox // 2
+    weighed = nbox // 8 * 5
     enc, adj, part = encode(signs, incident, adjoint, weighed)
     top, first, enc = lax.optimization_barrier((top, first, enc))
     pieces_a = gather_pieces({0: contrast_a, 1: first, far_side: top}, "group", groups)

time: 54.5 us -> 53.5 us (0.982); the launches traced: 53.6 us -> 53.3 us
    pallas_call x1, Pallas kernels: 5.87 us -> 6.74 us  [encode(): pl.pallas_call(functools.partial(encode_kernel, block, group, weighed //...]
  transfers between devices with their start and end apart: 14 -> 14, of which waited for: 4 -> 3; matrix products, arithmetic and copies ran while one was open for 0% -> 0% of each run, Pallas kernels for 43% -> 44%
where the time goes in v6:
time: 53.5 us; the launch traced here: 53.3 us
  Pallas kernels  25.3 us (47%)
  starting transfers between devices  22.4 us (42%)
  waiting for transfers between devices  4.79 us (9%)
  between operations  0.78 us (1%)
    ppermute x12, starting transfers between devices, exchange(): return lax.ppermute(x, axis, [(i, i ^ m) for i in range(count)])  15.9 us
    pallas_call x3, Pallas kernels, stage(): pl.pallas_call(functools.partial(stage_kernel, axis, count, mine, placed,...  11.1 us
    pallas_call x1, Pallas kernels, encode(): pl.pallas_call(functools.partial(encode_kernel, block, group, weighed //...  6.74 us
    ppermute x12, waiting for transfers between devices, exchange(): return lax.ppermute(x, axis, [(i, i ^ m) for i in range(count)])  4.78 us
    ppermute x1, starting transfers between devices, on_device(): high = lax.ppermute(edges[0], 'tile', downward)  4.54 us
    pallas_call x1, Pallas kernels, flush(): pl.pallas_call(functools.partial(flush_kernel, segments), in_specs=[VMEM]...  3.37 us
    pallas_call x1, Pallas kernels, weigh(): pl.pallas_call(functools.partial(weigh_kernel, block, weighed // block),...  2.16 us
    ppermute x1, starting transfers between devices, on_device(): low = lax.ppermute(edges[1], 'tile', upward)  1.92 us
  transfers between devices with their start and end apart: 14, of which 3 were waited for; matrix products, arithmetic and copies ran while one was open for 0% of the time, Pallas kernels for 44%

profile of v6, /device:TPU:4, one launch (start us, length us, event | category | flops | bytes accessed | tf_op | source)
XLA Modules:
  0.0 53.3 jit_solution(3441480713239370584)
XLA Ops:
  0.6 1.0 %split.1 = (bf16[272,256]{1,0:T(8,128)(2,1)S(1)}, bf16[240,256]{1,0:T(8,128)(2,1)S(1)}) custom-call(bf16[512,256]{1,0:T(8,128)(2,1)} %whole.1), custom_call_target="tpu_custom_call" | custom-call | tf_op jit(solution)/shard_map/split/pallas_call | solution.py:49
  1.6 1.6 %collective-permute-start.1 = (bf16[272,256]{1,0:T(8,128)(2,1)S(1)}, bf16[272,256]{1,0:T(8,128)(2,1)S(1)}, u32[]{:S(2)}, u32[]{:S(2)}) collective-permute-start(bf16[272,256]{1,0:T(8,128)(2,1)S(1)} %get-tuple-element.32.refs_7_), channel_id=1, source_target_pairs={{0,8},{8,0},{16,24},{24,16},{1,9},{9,1},{17,25},{25,17},{2,10},{10... | collective-permute-start | bytes 417800 | tf_op jit(solution)/shard_map/ppermute | solution.py:406
  3.3 2.6 %collective-permute-start = (bf16[272,256]{1,0:T(8,128)(2,1)S(1)}, bf16[272,256]{1,0:T(8,128)(2,1)S(1)}, u32[]{:S(2)}, u32[]{:S(2)}) collective-permute-start(bf16[272,256]{1,0:T(8,128)(2,1)S(1)} %get-tuple-element.32.refs_7_), channel_id=1, source_target_pairs={{0,16},{8,24},{16,0},{24,8},{1,17},{9,25},{17,1},{25,9},{2,18},{10... | collective-permute-start | bytes 417800 | tf_op jit(solution)/shard_map/ppermute | solution.py:406
  5.9 6.7 %encode.1 = (bf16[8,512,1024]{2,1,0:T(8,128)(2,1)S(1)}, bf16[8,512,1024]{2,1,0:T(8,128)(2,1)S(1)}, f32[512,1024]{1,0:T(8,128)S(1)}) custom-call(s32[1,8,8]{2,1,0:T(8,128)} %signs_in.1, bf16[1,8,512,1024]{3,2,1,0:T(8,128)(2,1)} %inc.1, bf16[1,8,512,1024]{3,2,1,0:T(8,128)(2,1)} %adj.3), custom_call_target="tpu_custom_call" | custom-call | flops 2147483648 | bytes 8388608 | tf_op jit(solution)/shard_map/encode/pallas_call | solution.py:113
  12.6 0.0 collective-permute-done.1.refs_8_
  12.6 0.0 collective-permute-done._.refs_9_
  12.6 0.5 collective-permute-start.2
  13.2 0.0 copy-start
  13.2 0.0 copy-start.1
  13.2 0.0 copy-start.2
  13.2 0.0 copy-start.3
  13.2 2.2 %weigh.1 = (bf16[8,512,1024]{2,1,0:T(8,128)(2,1)S(1)}, f32[512,1024]{1,0:T(8,128)S(1)}) custom-call(bf16[1,8,512,1024]{3,2,1,0:T(8,128)(2,1)} %adj.3, bf16[8,512,1024]{2,1,0:T(8,128)(2,1)S(1)} %get-tuple-element.34.enc.refs_5_, bf16[272,256]{1,0:T(8,128)(2,1)S(1)} %collective-permute-done._.refs_9_, ...), custom_call_target="tpu_custom_call", output_to_operand_aliasing={{0}: (3, {}), {1}: (4, {})} | custom-call | flops 1 | bytes 1 | tf_op jit(solution)/shard_map/weigh/pallas_call | solution.py:160
  15.3 1.7 %collective-permute-start.5 = (bf16[240,256]{1,0:T(8,128)(2,1)S(1)}, bf16[240,256]{1,0:T(8,128)(2,1)S(1)}, u32[]{:S(2)}, u32[]{:S(2)}) collective-permute-start(bf16[240,256]{1,0:T(8,128)(2,1)S(1)} %get-tuple-element.44.refs_7_), channel_id=1, source_target_pairs={{0,24},{8,16},{16,8},{24,0},{1,25},{9,17},{17,9},{25,1},{2,26},{10... | collective-permute-start | bytes 368648 | tf_op jit(solution)/shard_map/ppermute | solution.py:406
  17.1 1.4 %collective-permute-start.4 = (bf16[240,256]{1,0:T(8,128)(2,1)S(1)}, bf16[240,256]{1,0:T(8,128)(2,1)S(1)}, u32[]{:S(2)}, u32[]{:S(2)}) collective-permute-start(bf16[240,256]{1,0:T(8,128)(2,1)S(1)} %get-tuple-element.44.refs_7_), channel_id=1, source_target_pairs={{0,16},{8,24},{16,0},{24,8},{1,17},{9,25},{17,1},{25,9},{2,18},{10... | collective-permute-start | bytes 368648 | tf_op jit(solution)/shard_map/ppermute | solution.py:406
  18.5 1.3 %collective-permute-start.3 = (bf16[240,256]{1,0:T(8,128)(2,1)S(1)}, bf16[240,256]{1,0:T(8,128)(2,1)S(1)}, u32[]{:S(2)}, u32[]{:S(2)}) collective-permute-start(bf16[240,256]{1,0:T(8,128)(2,1)S(1)} %get-tuple-element.44.refs_7_), channel_id=1, source_target_pairs={{0,8},{8,0},{16,24},{24,16},{1,9},{9,1},{17,25},{25,17},{2,10},{10... | collective-permute-start | bytes 368648 | tf_op jit(solution)/shard_map/ppermute | solution.py:406
  19.8 0.0 collective-permute-done.2.refs_10_
  19.8 0.0 copy-done
  19.8 0.0 copy-done.1
  19.8 0.0 copy-done.2
  19.8 0.0 copy-done.3
  19.8 4.8 %stage.3 = (f32[2,8,544,128]{3,2,1,0:T(8,128)S(1)}, bf16[8,224,1024]{2,1,0:T(8,128)(2,1)S(1)}, f32[224,256]{1,0:T(8,128)S(1)}, bf16[2,224,256]{2,1,0:T(8,128)(2,...) custom-call(s32[6]{0:T(128)S(1)} %copy-done.3, ...), custom_call_target="tpu_custom_call" | custom-call | tf_op jit(solution)/shard_map/stage/pallas_call | solution.py:338
  24.7 1.9 %collective-permute-start.6 = (bf16[8,16,256]{2,1,0:T(8,128)(2,1)S(1)}, bf16[8,16,256]{2,1,0:T(8,128)(2,1)S(1)}, u32[]{:S(2)}, u32[]{:S(2)}) collective-permute-start(bf16[8,16,256]{2,1,0:T(8,128)(2,1)S(1)} %get-tuple-element.47), channel_id=1, source_target_pairs={{0,1},{1,2},{2,3},{3,4},{4,5},{5,6},{6,7},{8,9},{9,10},{10,11},{11... | collective-permute-start | bytes 196616 | tf_op jit(solution)/shard_map/ppermute | solution.py:509
  26.6 4.5 %collective-permute-start.7 = (bf16[8,16,256]{2,1,0:T(8,128)(2,1)S(1)}, bf16[8,16,256]{2,1,0:T(8,128)(2,1)S(1)}, u32[]{:S(2)}, u32[]{:S(2)}) collective-permute-start(bf16[8,16,256]{2,1,0:T(8,128)(2,1)S(1)} %get-tuple-element.48), channel_id=1, source_target_pairs={{1,0},{2,1},{3,2},{4,3},{5,4},{6,5},{7,6},{9,8},{10,9},{11,10},{12... | collective-permute-start | bytes 196616 | tf_op jit(solution)/shard_map/ppermute | solution.py:508
  31.2 0.0 collective-permute-done.5.refs_10_
  31.2 0.7 %collective-permute-start.10 = (bf16[2,224,256]{2,1,0:T(8,128)(2,1)S(1)}, bf16[2,224,256]{2,1,0:T(8,128)(2,1)S(1)}, u32[]{:S(2)}, u32[]{:S(2)}) collective-permute-start(bf16[2,224,256]{2,1,0:T(8,128)(2,1)S(1)} %get-tuple-element.56), channel_id=1, source_target_pairs={{0,8},{8,0},{16,24},{24,16},{1,9},{9,1},{17,25},{25,17},{2,10},{10... | collective-permute-start | bytes 688136 | tf_op jit(solution)/shard_map/ppermute | solution.py:406
  31.9 0.0 collective-permute-done.4.refs_9_
  31.9 0.0 collective-permute-done.3.refs_8_
  31.9 4.2 %stage.4 = (f32[2,8,544,128]{3,2,1,0:T(8,128)S(1)}, bf16[8,192,1024]{2,1,0:T(8,128)(2,1)S(1)}, f32[192,256]{1,0:T(8,128)S(1)}, bf16[2,192,256]{2,1,0:T(8,128)(2,1)S(1)}, bf16[1,192,256]{2,1,0:T(8,128)(2,1)S(1)}) custom-call(s32[6]{0:T(128)S(1)} %copy-done.3, bf16[6,256,256]{2,1,0:T(8,128)(2,1)S(1)} %copy-done, ...), custom_call_target="tpu_custom_call", output_to_operand_aliasing={{0}: (11, {})} | custom-call | flops 3019898880 | bytes 3145728 | tf_op jit(solution)/shard_map/stage/pallas_call | solution.py:338
  36.1 1.4 %collective-permute-start.9 = (bf16[2,192,256]{2,1,0:T(8,128)(2,1)S(1)}, bf16[2,192,256]{2,1,0:T(8,128)(2,1)S(1)}, u32[]{:S(2)}, u32[]{:S(2)}) collective-permute-start(bf16[2,192,256]{2,1,0:T(8,128)(2,1)S(1)} %get-tuple-element.53), channel_id=1, source_target_pairs={{0,8},{8,0},{16,24},{24,16},{1,9},{9,1},{17,25},{25,17},{2,10},{10... | collective-permute-start | bytes 589832 | tf_op jit(solution)/shard_map/ppermute | solution.py:406
  37.5 0.4 collective-permute-done.10.refs_4_
  38.0 1.2 %collective-permute-start.11 = (bf16[1,224,256]{2,1,0:T(8,128)(2,1)S(1)}, bf16[1,224,256]{2,1,0:T(8,128)(2,1)S(1)}, u32[]{:S(2)}, u32[]{:S(2)}) collective-permute-start(bf16[1,224,256]{2,1,0:T(8,128)(2,1)S(1)} %add_convert_fusion), channel_id=1, source_target_pairs={{0,16},{8,24},{16,0},{24,8},{1,17},{9,25},{17,1},{25,9},{2,18},{10... | collective-permute-start | bytes 344072 | tf_op jit(solution)/shard_map/ppermute | solution.py:406
  39.2 0.0 collective-permute-done.6.refs_5_
  39.2 0.0 collective-permute-done.7.refs_6_
  39.2 2.1 %stage.5 = (f32[2,8,544,128]{3,2,1,0:T(8,128)S(1)}, bf16[8,96,1024]{2,1,0:T(8,128)(2,1)S(1)}, f32[96,256]{1,0:T(8,128)S(1)}, bf16[2,96,256]{2,1,0:T(8,128)(2,1)S(1)}, bf16[1,96,256]{2,1,0:T(8,128)(2,1)S(1)}) custom-call(s32[6]{0:T(128)S(1)} %copy-done.3, bf16[6,256,256]{2,1,0:T(8,128)(2,1)S(1)} %copy-done, ...), custom_call_target="tpu_custom_call", output_to_operand_aliasing={{0}: (7, {})} | custom-call | flops 1006632960 | bytes 1572864 | tf_op jit(solution)/shard_map/stage/pallas_call | solution.py:338
  41.3 1.0 %collective-permute-start.8 = (bf16[2,96,256]{2,1,0:T(8,128)(2,1)S(1)}, bf16[2,96,256]{2,1,0:T(8,128)(2,1)S(1)}, u32[]{:S(2)}, u32[]{:S(2)}) collective-permute-start(bf16[2,96,256]{2,1,0:T(8,128)(2,1)S(1)} %get-tuple-element.51.refs_2_), channel_id=1, source_target_pairs={{0,8},{8,0},{16,24},{24,16},{1,9},{9,1},{17,25},{25,17},{2,10},{10... | collective-permute-start | bytes 294920 | tf_op jit(solution)/shard_map/ppermute | solution.py:406
  42.2 3.4 %collective-permute-done.9.refs_0_.refs_2_ = bf16[2,192,256]{2,1,0:T(8,128)(2,1)S(1)} collective-permute-done((bf16[2,192,256]{2,1,0:T(8,128)(2,1)S(1)}, bf16[2,192,256]{2,1,0:T(8,128)(2,1)S(1)}, u32[]{:S(2)}, u32[]{:S(2)}) %collective-permute-start.9) | collective-permute-done | bytes 196640 | tf_op jit(solution)/shard_map/ppermute | solution.py:406
  45.7 0.1 collective-permute-start.12
  45.8 0.9 %collective-permute-done.8.refs_3_.refs_0_.refs_5_ = bf16[2,96,256]{2,1,0:T(8,128)(2,1)S(1)} collective-permute-done((bf16[2,96,256]{2,1,0:T(8,128)(2,1)S(1)}, bf16[2,96,256]{2,1,0:T(8,128)(2,1)S(1)}, u32[]{:S(2)}, u32[]{:S(2)}) %collective-permute-start.8) | collective-permute-done | bytes 98336 | tf_op jit(solution)/shard_map/ppermute | solution.py:406
  46.7 0.0 collective-permute-done.11.refs_5_
  46.8 2.3 %collective-permute-start.13 = (bf16[1,96,256]{2,1,0:T(8,128)(2,1)S(1)}, bf16[1,96,256]{2,1,0:T(8,128)(2,1)S(1)}, u32[]{:S(2)}, u32[]{:S(2)}) collective-permute-start(bf16[1,96,256]{2,1,0:T(8,128)(2,1)S(1)} %bitcast.3), channel_id=1, source_target_pairs={{0,16},{8,24},{16,0},{24,8},{1,17},{9,25},{17,1},{25,9},{2,18},{10... | collective-permute-start | bytes 147464 | tf_op jit(solution)/shard_map/ppermute | solution.py:406
  49.0 3.4 %flush.1 = bf16[1,8,512,1024]{3,2,1,0:T(8,128)(2,1)} custom-call(bf16[8,224,1024]{2,1,0:T(8,128)(2,1)S(1)} %get-tuple-element.43.refs_0_, bf16[8,192,1024]{2,1,0:T(8,128)(2,1)S(1)} %get-tuple-element.46.refs_1_, bf16[8,96,1024]{2,1,0:T(8,128)(2,1)S(1)} %get-tuple-element.50.refs_2_, bf16[2,96,256]{2,1,0:T(8,128)(2,1)S(1)} %collective-permute-done.8.refs_3_.refs_0_.refs_5_), custom_call_target="tpu_custom_call" | custom-call | flops 1 | bytes 1 | tf_op jit(solution)/shard_map/flush/pallas_call | solution.py:387
  52.4 0.0 collective-permute-done.12.refs_3_
  52.4 0.0 collective-permute-done.13.refs_6_
  52.5 0.9 %add.11 = f32[512,256]{1,0:T(8,128)} custom-call(f32[224,256]{1,0:T(8,128)S(1)} %get-tuple-element.58.refs_0_, f32[192,256]{1,0:T(8,128)S(1)} %get-tuple-element.59.refs_1_, bf16[2,192,256]{2,1,0:T(8,128)(2,1)S(1)} %collective-permute-done.9.refs_0_.refs_2_, bf16[1,192,256]{2,1,0:T(8,128)(2,1)S(1)} %collective-permute-done.12.refs_3_, ...), custom_call_target="tpu_custom_call" | custom-call | tf_op jit(solution)/shard_map/add/pallas_call | solution.py:185
  (3 shorter events, 0.1 us)
Async XLA Ops:
  1.6 11.0 %collective-permute-start.1 = (bf16[272,256]{1,0:T(8,128)(2,1)S(1)}, bf16[272,256]{1,0:T(8,128)(2,1)S(1)}, u32[]{:S(2)}, u32[]{:S(2)}) collective-permute-start(bf16[272,256]{1,0:T(8,128)(2,1)S(1)} %get-tuple-element.32.refs_7_), channel_id=1, source_target_pairs={{0,8},{8,0},{16,24},{24,16},{1,9},{9,1},{17,25},{25,17},{2,10},{10... | collective-permute-start | bytes 417800 | tf_op jit(solution)/shard_map/ppermute | solution.py:406
  3.3 9.4 %collective-permute-start = (bf16[272,256]{1,0:T(8,128)(2,1)S(1)}, bf16[272,256]{1,0:T(8,128)(2,1)S(1)}, u32[]{:S(2)}, u32[]{:S(2)}) collective-permute-start(bf16[272,256]{1,0:T(8,128)(2,1)S(1)} %get-tuple-element.32.refs_7_), channel_id=1, source_target_pairs={{0,16},{8,24},{16,0},{24,8},{1,17},{9,25},{17,1},{25,9},{2,18},{10... | collective-permute-start | bytes 417800 | tf_op jit(solution)/shard_map/ppermute | solution.py:406
  12.6 7.2 %collective-permute-start.2 = (bf16[272,256]{1,0:T(8,128)(2,1)S(1)}, bf16[272,256]{1,0:T(8,128)(2,1)S(1)}, u32[]{:S(2)}, u32[]{:S(2)}) collective-permute-start(bf16[272,256]{1,0:T(8,128)(2,1)S(1)} %collective-permute-done._.refs_9_), channel_id=1, source_target_pairs={{0,8},{8,0},{16,24},{24,16},{1,9},{9,1},{17,25},{25,17},{2,10},{10... | collective-permute-start | bytes 417800 | tf_op jit(solution)/shard_map/ppermute | solution.py:406
  13.2 6.6 %copy-start = (bf16[6,256,256]{2,1,0:T(8,128)(2,1)S(1)}, bf16[6,256,256]{2,1,0:T(8,128)(2,1)}, u32[]{:S(2)}) copy-start(bf16[6,256,256]{2,1,0:T(8,128)(2,1)} %refs_1_.5) | copy-start | bytes 2359300
  13.2 6.6 %copy-start.1 = (bf16[256,1024]{1,0:T(8,128)(2,1)S(1)}, bf16[256,1024]{1,0:T(8,128)(2,1)}, u32[]{:S(2)}) copy-start(bf16[256,1024]{1,0:T(8,128)(2,1)} %refs_2_.5) | copy-start | bytes 1572868
  13.2 6.6 %copy-start.2 = (bf16[1024,256]{1,0:T(8,128)(2,1)S(1)}, bf16[1024,256]{1,0:T(8,128)(2,1)}, u32[]{:S(2)}) copy-start(bf16[1024,256]{1,0:T(8,128)(2,1)} %refs_6_.3) | copy-start | bytes 1572868
  13.2 6.7 %copy-start.3 = (s32[6]{0:T(128)S(1)}, s32[6]{0:T(128)}, u32[]{:S(2)}) copy-start(s32[6]{0:T(128)} %refs_0_.5) | copy-start | bytes 76
  15.3 15.8 %collective-permute-start.5 = (bf16[240,256]{1,0:T(8,128)(2,1)S(1)}, bf16[240,256]{1,0:T(8,128)(2,1)S(1)}, u32[]{:S(2)}, u32[]{:S(2)}) collective-permute-start(bf16[240,256]{1,0:T(8,128)(2,1)S(1)} %get-tuple-element.44.refs_7_), channel_id=1, source_target_pairs={{0,24},{8,16},{16,8},{24,0},{1,25},{9,17},{17,9},{25,1},{2,26},{10... | collective-permute-start | bytes 368648 | tf_op jit(solution)/shard_map/ppermute | solution.py:406
  17.1 14.8 %collective-permute-start.4 = (bf16[240,256]{1,0:T(8,128)(2,1)S(1)}, bf16[240,256]{1,0:T(8,128)(2,1)S(1)}, u32[]{:S(2)}, u32[]{:S(2)}) collective-permute-start(bf16[240,256]{1,0:T(8,128)(2,1)S(1)} %get-tuple-element.44.refs_7_), channel_id=1, source_target_pairs={{0,16},{8,24},{16,0},{24,8},{1,17},{9,25},{17,1},{25,9},{2,18},{10... | collective-permute-start | bytes 368648 | tf_op jit(solution)/shard_map/ppermute | solution.py:406
  18.5 13.5 %collective-permute-start.3 = (bf16[240,256]{1,0:T(8,128)(2,1)S(1)}, bf16[240,256]{1,0:T(8,128)(2,1)S(1)}, u32[]{:S(2)}, u32[]{:S(2)}) collective-permute-start(bf16[240,256]{1,0:T(8,128)(2,1)S(1)} %get-tuple-element.44.refs_7_), channel_id=1, source_target_pairs={{0,8},{8,0},{16,24},{24,16},{1,9},{9,1},{17,25},{25,17},{2,10},{10... | collective-permute-start | bytes 368648 | tf_op jit(solution)/shard_map/ppermute | solution.py:406
  24.7 14.5 %collective-permute-start.6 = (bf16[8,16,256]{2,1,0:T(8,128)(2,1)S(1)}, bf16[8,16,256]{2,1,0:T(8,128)(2,1)S(1)}, u32[]{:S(2)}, u32[]{:S(2)}) collective-permute-start(bf16[8,16,256]{2,1,0:T(8,128)(2,1)S(1)} %get-tuple-element.47), channel_id=1, source_target_pairs={{0,1},{1,2},{2,3},{3,4},{4,5},{5,6},{6,7},{8,9},{9,10},{10,11},{11... | collective-permute-start | bytes 196616 | tf_op jit(solution)/shard_map/ppermute | solution.py:509
  26.6 12.6 %collective-permute-start.7 = (bf16[8,16,256]{2,1,0:T(8,128)(2,1)S(1)}, bf16[8,16,256]{2,1,0:T(8,128)(2,1)S(1)}, u32[]{:S(2)}, u32[]{:S(2)}) collective-permute-start(bf16[8,16,256]{2,1,0:T(8,128)(2,1)S(1)} %get-tuple-element.48), channel_id=1, source_target_pairs={{1,0},{2,1},{3,2},{4,3},{5,4},{6,5},{7,6},{9,8},{10,9},{11,10},{12... | collective-permute-start | bytes 196616 | tf_op jit(solution)/shard_map/ppermute | solution.py:508
  31.2 6.8 %collective-permute-start.10 = (bf16[2,224,256]{2,1,0:T(8,128)(2,1)S(1)}, bf16[2,224,256]{2,1,0:T(8,128)(2,1)S(1)}, u32[]{:S(2)}, u32[]{:S(2)}) collective-permute-start(bf16[2,224,256]{2,1,0:T(8,128)(2,1)S(1)} %get-tuple-element.56), channel_id=1, source_target_pairs={{0,8},{8,0},{16,24},{24,16},{1,9},{9,1},{17,25},{25,17},{2,10},{10... | collective-permute-start | bytes 688136 | tf_op jit(solution)/shard_map/ppermute | solution.py:406
  36.1 9.5 %collective-permute-start.9 = (bf16[2,192,256]{2,1,0:T(8,128)(2,1)S(1)}, bf16[2,192,256]{2,1,0:T(8,128)(2,1)S(1)}, u32[]{:S(2)}, u32[]{:S(2)}) collective-permute-start(bf16[2,192,256]{2,1,0:T(8,128)(2,1)S(1)} %get-tuple-element.53), channel_id=1, source_target_pairs={{0,8},{8,0},{16,24},{24,16},{1,9},{9,1},{17,25},{25,17},{2,10},{10... | collective-permute-start | bytes 589832 | tf_op jit(solution)/shard_map/ppermute | solution.py:406
  38.0 8.7 %collective-permute-start.11 = (bf16[1,224,256]{2,1,0:T(8,128)(2,1)S(1)}, bf16[1,224,256]{2,1,0:T(8,128)(2,1)S(1)}, u32[]{:S(2)}, u32[]{:S(2)}) collective-permute-start(bf16[1,224,256]{2,1,0:T(8,128)(2,1)S(1)} %add_convert_fusion), channel_id=1, source_target_pairs={{0,16},{8,24},{16,0},{24,8},{1,17},{9,25},{17,1},{25,9},{2,18},{10... | collective-permute-start | bytes 344072 | tf_op jit(solution)/shard_map/ppermute | solution.py:406
  41.3 5.4 %collective-permute-start.8 = (bf16[2,96,256]{2,1,0:T(8,128)(2,1)S(1)}, bf16[2,96,256]{2,1,0:T(8,128)(2,1)S(1)}, u32[]{:S(2)}, u32[]{:S(2)}) collective-permute-start(bf16[2,96,256]{2,1,0:T(8,128)(2,1)S(1)} %get-tuple-element.51.refs_2_), channel_id=1, source_target_pairs={{0,8},{8,0},{16,24},{24,16},{1,9},{9,1},{17,25},{25,17},{2,10},{10... | collective-permute-start | bytes 294920 | tf_op jit(solution)/shard_map/ppermute | solution.py:406
  45.7 6.7 %collective-permute-start.12 = (bf16[1,192,256]{2,1,0:T(8,128)(2,1)S(1)}, bf16[1,192,256]{2,1,0:T(8,128)(2,1)S(1)}, u32[]{:S(2)}, u32[]{:S(2)}) collective-permute-start(bf16[1,192,256]{2,1,0:T(8,128)(2,1)S(1)} %bitcast.2), channel_id=1, source_target_pairs={{0,16},{8,24},{16,0},{24,8},{1,17},{9,25},{17,1},{25,9},{2,18},{10... | collective-permute-start | bytes 294920 | tf_op jit(solution)/shard_map/ppermute | solution.py:406
  46.8 5.7 %collective-permute-start.13 = (bf16[1,96,256]{2,1,0:T(8,128)(2,1)S(1)}, bf16[1,96,256]{2,1,0:T(8,128)(2,1)S(1)}, u32[]{:S(2)}, u32[]{:S(2)}) collective-permute-start(bf16[1,96,256]{2,1,0:T(8,128)(2,1)S(1)} %bitcast.3), channel_id=1, source_target_pairs={{0,16},{8,24},{16,0},{24,8},{1,17},{9,25},{17,1},{25,9},{2,18},{10... | collective-permute-start | bytes 147464 | tf_op jit(solution)/shard_map/ppermute | solution.py:406

commit v7 on v6

--- a/solution.py
+++ b/solution.py
@@ -490,7 +490,7 @@
     far_side = groups // 2
     first = exchange(contrast_a, "group", 1, groups)
     top = exchange(contrast_a, "group", far_side, groups)
-    weighed = nbox // 8 * 5
+    weighed = nbox // 8 * 7
     enc, adj, part = encode(signs, incident, adjoint, weighed)
     top, first, enc = lax.optimization_barrier((top, first, enc))
     pieces_a = gather_pieces({0: contrast_a, 1: first, far_side: top}, "group", groups)

time: 53.5 us -> 53 us (level)
    pallas_call x1, Pallas kernels: 2.16 us -> 1.53 us  [weigh(): pl.pallas_call(functools.partial(weigh_kernel, block, weighed // block),...]
where the time goes in v7:
time: 53 us; the launch traced here: 52.7 us
  Pallas kernels  24.8 us (47%)
  starting transfers between devices  22.1 us (42%)
  waiting for transfers between devices  4.9 us (9%)
  between operations  0.78 us (1%)
    ppermute x12, starting transfers between devices, exchange(): return lax.ppermute(x, axis, [(i, i ^ m) for i in range(count)])  15.7 us
    pallas_call x3, Pallas kernels, stage(): pl.pallas_call(functools.partial(stage_kernel, axis, count, mine, placed,...  11.1 us
    pallas_call x1, Pallas kernels, encode(): pl.pallas_call(functools.partial(encode_kernel, block, group, weighed //...  6.89 us
    ppermute x12, waiting for transfers between devices, exchange(): return lax.ppermute(x, axis, [(i, i ^ m) for i in range(count)])  4.89 us
    ppermute x1, starting transfers between devices, on_device(): high = lax.ppermute(edges[0], 'tile', downward)  4.54 us
    pallas_call x1, Pallas kernels, flush(): pl.pallas_call(functools.partial(flush_kernel, segments), in_specs=[VMEM]...  3.37 us
    ppermute x1, starting transfers between devices, on_device(): low = lax.ppermute(edges[1], 'tile', upward)  1.92 us
    pallas_call x1, Pallas kernels, weigh(): pl.pallas_call(functools.partial(weigh_kernel, block, weighed // block),...  1.53 us
  transfers between devices with their start and end apart: 14, of which 3 were waited for; matrix products, arithmetic and copies ran while one was open for 0% of the time, Pallas kernels for 44%

profile of v7, /device:TPU:4, one launch (start us, length us, event | category | flops | bytes accessed | tf_op | source)
XLA Modules:
  0.0 52.7 jit_solution(3787378744144653160)
XLA Ops:
  0.6 1.0 %split.1 = (bf16[272,256]{1,0:T(8,128)(2,1)S(1)}, bf16[240,256]{1,0:T(8,128)(2,1)S(1)}) custom-call(bf16[512,256]{1,0:T(8,128)(2,1)} %whole.1), custom_call_target="tpu_custom_call" | custom-call | tf_op jit(solution)/shard_map/split/pallas_call | solution.py:49
  1.6 1.6 %collective-permute-start.1 = (bf16[272,256]{1,0:T(8,128)(2,1)S(1)}, bf16[272,256]{1,0:T(8,128)(2,1)S(1)}, u32[]{:S(2)}, u32[]{:S(2)}) collective-permute-start(bf16[272,256]{1,0:T(8,128)(2,1)S(1)} %get-tuple-element.32.refs_7_), channel_id=1, source_target_pairs={{0,8},{8,0},{16,24},{24,16},{1,9},{9,1},{17,25},{25,17},{2,10},{10... | collective-permute-start | bytes 417800 | tf_op jit(solution)/shard_map/ppermute | solution.py:406
  3.3 2.6 %collective-permute-start = (bf16[272,256]{1,0:T(8,128)(2,1)S(1)}, bf16[272,256]{1,0:T(8,128)(2,1)S(1)}, u32[]{:S(2)}, u32[]{:S(2)}) collective-permute-start(bf16[272,256]{1,0:T(8,128)(2,1)S(1)} %get-tuple-element.32.refs_7_), channel_id=1, source_target_pairs={{0,16},{8,24},{16,0},{24,8},{1,17},{9,25},{17,1},{25,9},{2,18},{10... | collective-permute-start | bytes 417800 | tf_op jit(solution)/shard_map/ppermute | solution.py:406
  5.9 6.9 %encode.1 = (bf16[8,512,1024]{2,1,0:T(8,128)(2,1)S(1)}, bf16[8,512,1024]{2,1,0:T(8,128)(2,1)S(1)}, f32[512,1024]{1,0:T(8,128)S(1)}) custom-call(s32[1,8,8]{2,1,0:T(8,128)} %signs_in.1, bf16[1,8,512,1024]{3,2,1,0:T(8,128)(2,1)} %inc.1, bf16[1,8,512,1024]{3,2,1,0:T(8,128)(2,1)} %adj.3), custom_call_target="tpu_custom_call" | custom-call | flops 2147483648 | bytes 8388608 | tf_op jit(solution)/shard_map/encode/pallas_call | solution.py:113
  12.8 0.0 collective-permute-done.1.refs_8_
  12.8 0.0 collective-permute-done._.refs_9_
  12.8 0.5 collective-permute-start.2
  13.3 0.0 copy-start
  13.3 0.0 copy-start.1
  13.3 0.0 copy-start.2
  13.3 0.0 copy-start.3
  13.3 1.5 %weigh.1 = (bf16[8,512,1024]{2,1,0:T(8,128)(2,1)S(1)}, f32[512,1024]{1,0:T(8,128)S(1)}) custom-call(bf16[1,8,512,1024]{3,2,1,0:T(8,128)(2,1)} %adj.3, bf16[8,512,1024]{2,1,0:T(8,128)(2,1)S(1)} %get-tuple-element.34.enc.refs_5_, bf16[272,256]{1,0:T(8,128)(2,1)S(1)} %collective-permute-done._.refs_9_, ...), custom_call_target="tpu_custom_call", output_to_operand_aliasing={{0}: (3, {}), {1}: (4, {})} | custom-call | flops 1 | bytes 1 | tf_op jit(solution)/shard_map/weigh/pallas_call | solution.py:160
  14.9 1.6 %collective-permute-start.5 = (bf16[240,256]{1,0:T(8,128)(2,1)S(1)}, bf16[240,256]{1,0:T(8,128)(2,1)S(1)}, u32[]{:S(2)}, u32[]{:S(2)}) collective-permute-start(bf16[240,256]{1,0:T(8,128)(2,1)S(1)} %get-tuple-element.44.refs_7_), channel_id=1, source_target_pairs={{0,24},{8,16},{16,8},{24,0},{1,25},{9,17},{17,9},{25,1},{2,26},{10... | collective-permute-start | bytes 368648 | tf_op jit(solution)/shard_map/ppermute | solution.py:406
  16.5 1.5 %collective-permute-start.4 = (bf16[240,256]{1,0:T(8,128)(2,1)S(1)}, bf16[240,256]{1,0:T(8,128)(2,1)S(1)}, u32[]{:S(2)}, u32[]{:S(2)}) collective-permute-start(bf16[240,256]{1,0:T(8,128)(2,1)S(1)} %get-tuple-element.44.refs_7_), channel_id=1, source_target_pairs={{0,16},{8,24},{16,0},{24,8},{1,17},{9,25},{17,1},{25,9},{2,18},{10... | collective-permute-start | bytes 368648 | tf_op jit(solution)/shard_map/ppermute | solution.py:406
  18.0 1.4 %collective-permute-start.3 = (bf16[240,256]{1,0:T(8,128)(2,1)S(1)}, bf16[240,256]{1,0:T(8,128)(2,1)S(1)}, u32[]{:S(2)}, u32[]{:S(2)}) collective-permute-start(bf16[240,256]{1,0:T(8,128)(2,1)S(1)} %get-tuple-element.44.refs_7_), channel_id=1, source_target_pairs={{0,8},{8,0},{16,24},{24,16},{1,9},{9,1},{17,25},{25,17},{2,10},{10... | collective-permute-start | bytes 368648 | tf_op jit(solution)/shard_map/ppermute | solution.py:406
  19.3 0.0 collective-permute-done.2.refs_10_
  19.3 0.0 copy-done
  19.3 0.0 copy-done.1
  19.3 0.0 copy-done.2
  19.3 0.0 copy-done.3
  19.3 4.8 %stage.3 = (f32[2,8,544,128]{3,2,1,0:T(8,128)S(1)}, bf16[8,224,1024]{2,1,0:T(8,128)(2,1)S(1)}, f32[224,256]{1,0:T(8,128)S(1)}, bf16[2,224,256]{2,1,0:T(8,128)(2,...) custom-call(s32[6]{0:T(128)S(1)} %copy-done.3, ...), custom_call_target="tpu_custom_call" | custom-call | tf_op jit(solution)/shard_map/stage/pallas_call | solution.py:338
  24.2 1.9 %collective-permute-start.6 = (bf16[8,16,256]{2,1,0:T(8,128)(2,1)S(1)}, bf16[8,16,256]{2,1,0:T(8,128)(2,1)S(1)}, u32[]{:S(2)}, u32[]{:S(2)}) collective-permute-start(bf16[8,16,256]{2,1,0:T(8,128)(2,1)S(1)} %get-tuple-element.47), channel_id=1, source_target_pairs={{0,1},{1,2},{2,3},{3,4},{4,5},{5,6},{6,7},{8,9},{9,10},{10,11},{11... | collective-permute-start | bytes 196616 | tf_op jit(solution)/shard_map/ppermute | solution.py:509
  26.1 4.5 %collective-permute-start.7 = (bf16[8,16,256]{2,1,0:T(8,128)(2,1)S(1)}, bf16[8,16,256]{2,1,0:T(8,128)(2,1)S(1)}, u32[]{:S(2)}, u32[]{:S(2)}) collective-permute-start(bf16[8,16,256]{2,1,0:T(8,128)(2,1)S(1)} %get-tuple-element.48), channel_id=1, source_target_pairs={{1,0},{2,1},{3,2},{4,3},{5,4},{6,5},{7,6},{9,8},{10,9},{11,10},{12... | collective-permute-start | bytes 196616 | tf_op jit(solution)/shard_map/ppermute | solution.py:508
  30.7 0.0 collective-permute-done.5.refs_10_
  30.7 0.7 %collective-permute-start.10 = (bf16[2,224,256]{2,1,0:T(8,128)(2,1)S(1)}, bf16[2,224,256]{2,1,0:T(8,128)(2,1)S(1)}, u32[]{:S(2)}, u32[]{:S(2)}) collective-permute-start(bf16[2,224,256]{2,1,0:T(8,128)(2,1)S(1)} %get-tuple-element.56), channel_id=1, source_target_pairs={{0,8},{8,0},{16,24},{24,16},{1,9},{9,1},{17,25},{25,17},{2,10},{10... | collective-permute-start | bytes 688136 | tf_op jit(solution)/shard_map/ppermute | solution.py:406
  31.4 0.0 collective-permute-done.4.refs_9_
  31.4 0.0 collective-permute-done.3.refs_8_
  31.4 4.2 %stage.4 = (f32[2,8,544,128]{3,2,1,0:T(8,128)S(1)}, bf16[8,192,1024]{2,1,0:T(8,128)(2,1)S(1)}, f32[192,256]{1,0:T(8,128)S(1)}, bf16[2,192,256]{2,1,0:T(8,128)(2,1)S(1)}, bf16[1,192,256]{2,1,0:T(8,128)(2,1)S(1)}) custom-call(s32[6]{0:T(128)S(1)} %copy-done.3, bf16[6,256,256]{2,1,0:T(8,128)(2,1)S(1)} %copy-done, ...), custom_call_target="tpu_custom_call", output_to_operand_aliasing={{0}: (11, {})} | custom-call | flops 3019898880 | bytes 3145728 | tf_op jit(solution)/shard_map/stage/pallas_call | solution.py:338
  35.6 1.4 %collective-permute-start.9 = (bf16[2,192,256]{2,1,0:T(8,128)(2,1)S(1)}, bf16[2,192,256]{2,1,0:T(8,128)(2,1)S(1)}, u32[]{:S(2)}, u32[]{:S(2)}) collective-permute-start(bf16[2,192,256]{2,1,0:T(8,128)(2,1)S(1)} %get-tuple-element.53), channel_id=1, source_target_pairs={{0,8},{8,0},{16,24},{24,16},{1,9},{9,1},{17,25},{25,17},{2,10},{10... | collective-permute-start | bytes 589832 | tf_op jit(solution)/shard_map/ppermute | solution.py:406
  37.0 0.4 collective-permute-done.10.refs_4_
  37.5 1.1 %collective-permute-start.11 = (bf16[1,224,256]{2,1,0:T(8,128)(2,1)S(1)}, bf16[1,224,256]{2,1,0:T(8,128)(2,1)S(1)}, u32[]{:S(2)}, u32[]{:S(2)}) collective-permute-start(bf16[1,224,256]{2,1,0:T(8,128)(2,1)S(1)} %add_convert_fusion), channel_id=1, source_target_pairs={{0,16},{8,24},{16,0},{24,8},{1,17},{9,25},{17,1},{25,9},{2,18},{10... | collective-permute-start | bytes 344072 | tf_op jit(solution)/shard_map/ppermute | solution.py:406
  38.5 0.0 collective-permute-done.6.refs_5_
  38.6 0.0 collective-permute-done.7.refs_6_
  38.6 2.1 %stage.5 = (f32[2,8,544,128]{3,2,1,0:T(8,128)S(1)}, bf16[8,96,1024]{2,1,0:T(8,128)(2,1)S(1)}, f32[96,256]{1,0:T(8,128)S(1)}, bf16[2,96,256]{2,1,0:T(8,128)(2,1)S(1)}, bf16[1,96,256]{2,1,0:T(8,128)(2,1)S(1)}) custom-call(s32[6]{0:T(128)S(1)} %copy-done.3, bf16[6,256,256]{2,1,0:T(8,128)(2,1)S(1)} %copy-done, ...), custom_call_target="tpu_custom_call", output_to_operand_aliasing={{0}: (7, {})} | custom-call | flops 1006632960 | bytes 1572864 | tf_op jit(solution)/shard_map/stage/pallas_call | solution.py:338
  40.7 0.9 %collective-permute-start.8 = (bf16[2,96,256]{2,1,0:T(8,128)(2,1)S(1)}, bf16[2,96,256]{2,1,0:T(8,128)(2,1)S(1)}, u32[]{:S(2)}, u32[]{:S(2)}) collective-permute-start(bf16[2,96,256]{2,1,0:T(8,128)(2,1)S(1)} %get-tuple-element.51.refs_2_), channel_id=1, source_target_pairs={{0,8},{8,0},{16,24},{24,16},{1,9},{9,1},{17,25},{25,17},{2,10},{10... | collective-permute-start | bytes 294920 | tf_op jit(solution)/shard_map/ppermute | solution.py:406
  41.6 3.6 %collective-permute-done.9.refs_0_.refs_2_ = bf16[2,192,256]{2,1,0:T(8,128)(2,1)S(1)} collective-permute-done((bf16[2,192,256]{2,1,0:T(8,128)(2,1)S(1)}, bf16[2,192,256]{2,1,0:T(8,128)(2,1)S(1)}, u32[]{:S(2)}, u32[]{:S(2)}) %collective-permute-start.9) | collective-permute-done | bytes 196640 | tf_op jit(solution)/shard_map/ppermute | solution.py:406
  45.2 0.1 collective-permute-start.12
  45.3 0.9 %collective-permute-done.8.refs_3_.refs_0_.refs_5_ = bf16[2,96,256]{2,1,0:T(8,128)(2,1)S(1)} collective-permute-done((bf16[2,96,256]{2,1,0:T(8,128)(2,1)S(1)}, bf16[2,96,256]{2,1,0:T(8,128)(2,1)S(1)}, u32[]{:S(2)}, u32[]{:S(2)}) %collective-permute-start.8) | collective-permute-done | bytes 98336 | tf_op jit(solution)/shard_map/ppermute | solution.py:406
  46.2 0.0 collective-permute-done.11.refs_5_
  46.3 2.2 %collective-permute-start.13 = (bf16[1,96,256]{2,1,0:T(8,128)(2,1)S(1)}, bf16[1,96,256]{2,1,0:T(8,128)(2,1)S(1)}, u32[]{:S(2)}, u32[]{:S(2)}) collective-permute-start(bf16[1,96,256]{2,1,0:T(8,128)(2,1)S(1)} %bitcast.3), channel_id=1, source_target_pairs={{0,16},{8,24},{16,0},{24,8},{1,17},{9,25},{17,1},{25,9},{2,18},{10... | collective-permute-start | bytes 147464 | tf_op jit(solution)/shard_map/ppermute | solution.py:406
  48.4 3.4 %flush.1 = bf16[1,8,512,1024]{3,2,1,0:T(8,128)(2,1)} custom-call(bf16[8,224,1024]{2,1,0:T(8,128)(2,1)S(1)} %get-tuple-element.43.refs_0_, bf16[8,192,1024]{2,1,0:T(8,128)(2,1)S(1)} %get-tuple-element.46.refs_1_, bf16[8,96,1024]{2,1,0:T(8,128)(2,1)S(1)} %get-tuple-element.50.refs_2_, bf16[2,96,256]{2,1,0:T(8,128)(2,1)S(1)} %collective-permute-done.8.refs_3_.refs_0_.refs_5_), custom_call_target="tpu_custom_call" | custom-call | flops 1 | bytes 1 | tf_op jit(solution)/shard_map/flush/pallas_call | solution.py:387
  51.8 0.0 collective-permute-done.12.refs_3_
  51.8 0.0 collective-permute-done.13.refs_6_
  51.8 0.9 %add.11 = f32[512,256]{1,0:T(8,128)} custom-call(f32[224,256]{1,0:T(8,128)S(1)} %get-tuple-element.58.refs_0_, f32[192,256]{1,0:T(8,128)S(1)} %get-tuple-element.59.refs_1_, bf16[2,192,256]{2,1,0:T(8,128)(2,1)S(1)} %collective-permute-done.9.refs_0_.refs_2_, bf16[1,192,256]{2,1,0:T(8,128)(2,1)S(1)} %collective-permute-done.12.refs_3_, ...), custom_call_target="tpu_custom_call" | custom-call | tf_op jit(solution)/shard_map/add/pallas_call | solution.py:185
  (3 shorter events, 0.1 us)
Async XLA Ops:
  1.6 11.1 %collective-permute-start.1 = (bf16[272,256]{1,0:T(8,128)(2,1)S(1)}, bf16[272,256]{1,0:T(8,128)(2,1)S(1)}, u32[]{:S(2)}, u32[]{:S(2)}) collective-permute-start(bf16[272,256]{1,0:T(8,128)(2,1)S(1)} %get-tuple-element.32.refs_7_), channel_id=1, source_target_pairs={{0,8},{8,0},{16,24},{24,16},{1,9},{9,1},{17,25},{25,17},{2,10},{10... | collective-permute-start | bytes 417800 | tf_op jit(solution)/shard_map/ppermute | solution.py:406
  3.3 9.5 %collective-permute-start = (bf16[272,256]{1,0:T(8,128)(2,1)S(1)}, bf16[272,256]{1,0:T(8,128)(2,1)S(1)}, u32[]{:S(2)}, u32[]{:S(2)}) collective-permute-start(bf16[272,256]{1,0:T(8,128)(2,1)S(1)} %get-tuple-element.32.refs_7_), channel_id=1, source_target_pairs={{0,16},{8,24},{16,0},{24,8},{1,17},{9,25},{17,1},{25,9},{2,18},{10... | collective-permute-start | bytes 417800 | tf_op jit(solution)/shard_map/ppermute | solution.py:406
  12.8 6.5 %collective-permute-start.2 = (bf16[272,256]{1,0:T(8,128)(2,1)S(1)}, bf16[272,256]{1,0:T(8,128)(2,1)S(1)}, u32[]{:S(2)}, u32[]{:S(2)}) collective-permute-start(bf16[272,256]{1,0:T(8,128)(2,1)S(1)} %collective-permute-done._.refs_9_), channel_id=1, source_target_pairs={{0,8},{8,0},{16,24},{24,16},{1,9},{9,1},{17,25},{25,17},{2,10},{10... | collective-permute-start | bytes 417800 | tf_op jit(solution)/shard_map/ppermute | solution.py:406
  13.3 6.0 %copy-start = (bf16[6,256,256]{2,1,0:T(8,128)(2,1)S(1)}, bf16[6,256,256]{2,1,0:T(8,128)(2,1)}, u32[]{:S(2)}) copy-start(bf16[6,256,256]{2,1,0:T(8,128)(2,1)} %refs_1_.5) | copy-start | bytes 2359300
  13.3 6.0 %copy-start.1 = (bf16[256,1024]{1,0:T(8,128)(2,1)S(1)}, bf16[256,1024]{1,0:T(8,128)(2,1)}, u32[]{:S(2)}) copy-start(bf16[256,1024]{1,0:T(8,128)(2,1)} %refs_2_.5) | copy-start | bytes 1572868
  13.3 6.0 %copy-start.2 = (bf16[1024,256]{1,0:T(8,128)(2,1)S(1)}, bf16[1024,256]{1,0:T(8,128)(2,1)}, u32[]{:S(2)}) copy-start(bf16[1024,256]{1,0:T(8,128)(2,1)} %refs_6_.3) | copy-start | bytes 1572868
  13.3 6.0 %copy-start.3 = (s32[6]{0:T(128)S(1)}, s32[6]{0:T(128)}, u32[]{:S(2)}) copy-start(s32[6]{0:T(128)} %refs_0_.5) | copy-start | bytes 76
  14.9 15.8 %collective-permute-start.5 = (bf16[240,256]{1,0:T(8,128)(2,1)S(1)}, bf16[240,256]{1,0:T(8,128)(2,1)S(1)}, u32[]{:S(2)}, u32[]{:S(2)}) collective-permute-start(bf16[240,256]{1,0:T(8,128)(2,1)S(1)} %get-tuple-element.44.refs_7_), channel_id=1, source_target_pairs={{0,24},{8,16},{16,8},{24,0},{1,25},{9,17},{17,9},{25,1},{2,26},{10... | collective-permute-start | bytes 368648 | tf_op jit(solution)/shard_map/ppermute | solution.py:406
  16.5 15.0 %collective-permute-start.4 = (bf16[240,256]{1,0:T(8,128)(2,1)S(1)}, bf16[240,256]{1,0:T(8,128)(2,1)S(1)}, u32[]{:S(2)}, u32[]{:S(2)}) collective-permute-start(bf16[240,256]{1,0:T(8,128)(2,1)S(1)} %get-tuple-element.44.refs_7_), channel_id=1, source_target_pairs={{0,16},{8,24},{16,0},{24,8},{1,17},{9,25},{17,1},{25,9},{2,18},{10... | collective-permute-start | bytes 368648 | tf_op jit(solution)/shard_map/ppermute | solution.py:406
  18.0 13.5 %collective-permute-start.3 = (bf16[240,256]{1,0:T(8,128)(2,1)S(1)}, bf16[240,256]{1,0:T(8,128)(2,1)S(1)}, u32[]{:S(2)}, u32[]{:S(2)}) collective-permute-start(bf16[240,256]{1,0:T(8,128)(2,1)S(1)} %get-tuple-element.44.refs_7_), channel_id=1, source_target_pairs={{0,8},{8,0},{16,24},{24,16},{1,9},{9,1},{17,25},{25,17},{2,10},{10... | collective-permute-start | bytes 368648 | tf_op jit(solution)/shard_map/ppermute | solution.py:406
  24.2 14.3 %collective-permute-start.6 = (bf16[8,16,256]{2,1,0:T(8,128)(2,1)S(1)}, bf16[8,16,256]{2,1,0:T(8,128)(2,1)S(1)}, u32[]{:S(2)}, u32[]{:S(2)}) collective-permute-start(bf16[8,16,256]{2,1,0:T(8,128)(2,1)S(1)} %get-tuple-element.47), channel_id=1, source_target_pairs={{0,1},{1,2},{2,3},{3,4},{4,5},{5,6},{6,7},{8,9},{9,10},{10,11},{11... | collective-permute-start | bytes 196616 | tf_op jit(solution)/shard_map/ppermute | solution.py:509
  26.1 12.4 %collective-permute-start.7 = (bf16[8,16,256]{2,1,0:T(8,128)(2,1)S(1)}, bf16[8,16,256]{2,1,0:T(8,128)(2,1)S(1)}, u32[]{:S(2)}, u32[]{:S(2)}) collective-permute-start(bf16[8,16,256]{2,1,0:T(8,128)(2,1)S(1)} %get-tuple-element.48), channel_id=1, source_target_pairs={{1,0},{2,1},{3,2},{4,3},{5,4},{6,5},{7,6},{9,8},{10,9},{11,10},{12... | collective-permute-start | bytes 196616 | tf_op jit(solution)/shard_map/ppermute | solution.py:508
  30.7 6.7 %collective-permute-start.10 = (bf16[2,224,256]{2,1,0:T(8,128)(2,1)S(1)}, bf16[2,224,256]{2,1,0:T(8,128)(2,1)S(1)}, u32[]{:S(2)}, u32[]{:S(2)}) collective-permute-start(bf16[2,224,256]{2,1,0:T(8,128)(2,1)S(1)} %get-tuple-element.56), channel_id=1, source_target_pairs={{0,8},{8,0},{16,24},{24,16},{1,9},{9,1},{17,25},{25,17},{2,10},{10... | collective-permute-start | bytes 688136 | tf_op jit(solution)/shard_map/ppermute | solution.py:406
  35.6 9.5 %collective-permute-start.9 = (bf16[2,192,256]{2,1,0:T(8,128)(2,1)S(1)}, bf16[2,192,256]{2,1,0:T(8,128)(2,1)S(1)}, u32[]{:S(2)}, u32[]{:S(2)}) collective-permute-start(bf16[2,192,256]{2,1,0:T(8,128)(2,1)S(1)} %get-tuple-element.53), channel_id=1, source_target_pairs={{0,8},{8,0},{16,24},{24,16},{1,9},{9,1},{17,25},{25,17},{2,10},{10... | collective-permute-start | bytes 589832 | tf_op jit(solution)/shard_map/ppermute | solution.py:406
  37.5 8.7 %collective-permute-start.11 = (bf16[1,224,256]{2,1,0:T(8,128)(2,1)S(1)}, bf16[1,224,256]{2,1,0:T(8,128)(2,1)S(1)}, u32[]{:S(2)}, u32[]{:S(2)}) collective-permute-start(bf16[1,224,256]{2,1,0:T(8,128)(2,1)S(1)} %add_convert_fusion), channel_id=1, source_target_pairs={{0,16},{8,24},{16,0},{24,8},{1,17},{9,25},{17,1},{25,9},{2,18},{10... | collective-permute-start | bytes 344072 | tf_op jit(solution)/shard_map/ppermute | solution.py:406
  40.7 5.5 %collective-permute-start.8 = (bf16[2,96,256]{2,1,0:T(8,128)(2,1)S(1)}, bf16[2,96,256]{2,1,0:T(8,128)(2,1)S(1)}, u32[]{:S(2)}, u32[]{:S(2)}) collective-permute-start(bf16[2,96,256]{2,1,0:T(8,128)(2,1)S(1)} %get-tuple-element.51.refs_2_), channel_id=1, source_target_pairs={{0,8},{8,0},{16,24},{24,16},{1,9},{9,1},{17,25},{25,17},{2,10},{10... | collective-permute-start | bytes 294920 | tf_op jit(solution)/shard_map/ppermute | solution.py:406
  45.2 6.6 %collective-permute-start.12 = (bf16[1,192,256]{2,1,0:T(8,128)(2,1)S(1)}, bf16[1,192,256]{2,1,0:T(8,128)(2,1)S(1)}, u32[]{:S(2)}, u32[]{:S(2)}) collective-permute-start(bf16[1,192,256]{2,1,0:T(8,128)(2,1)S(1)} %bitcast.2), channel_id=1, source_target_pairs={{0,16},{8,24},{16,0},{24,8},{1,17},{9,25},{17,1},{25,9},{2,18},{10... | collective-permute-start | bytes 294920 | tf_op jit(solution)/shard_map/ppermute | solution.py:406
  46.3 5.6 %collective-permute-start.13 = (bf16[1,96,256]{2,1,0:T(8,128)(2,1)S(1)}, bf16[1,96,256]{2,1,0:T(8,128)(2,1)S(1)}, u32[]{:S(2)}, u32[]{:S(2)}) collective-permute-start(bf16[1,96,256]{2,1,0:T(8,128)(2,1)S(1)} %bitcast.3), channel_id=1, source_target_pairs={{0,16},{8,24},{16,0},{24,8},{1,17},{9,25},{17,1},{25,9},{2,18},{10... | collective-permute-start | bytes 147464 | tf_op jit(solution)/shard_map/ppermute | solution.py:406
